TPU v7x, 128 devices: a whole 4x4x4 slice. The times are simulated.
128 devices in a mesh: comp: 4 (over x_lo, core), tile: 32 (over z, x_hi, y).
Axes of the slice: x: 4 (x_hi: 2, x_lo: 2; x = x_hi * 2 + x_lo), y: 4, z: 4, core: 2. Of those that a mesh axis runs over, the one named last changes fastest.
Arguments:
- fields: float32 [4, 32, 1966080], P('comp', 'tile'), may hold values from -6 to 6
- atm_mixing: float32 [3, 128, 128], replicated, as said below
- ocean_mixing: float32 [4, 80, 80], replicated, as said below
- sea_mask: int32 [4, 32, 48, 128], P('comp', 'tile'), may hold values 0 or 1
- source_slot: int32 [4, 32, 256], P('comp', 'tile'), may hold values from 0 to 239
- target_tile: int32 [4, 32, 256, 1], P('comp', 'tile'), may hold values from 0 to 31; in each aligned block of 256 rows (0 to 255, 256 to 511, ..., all dimensions but the last counted through in order) at most 16 rows name the same one
- target_slot: int32 [4, 32, 256], P('comp', 'tile'), may hold values from 0 to 239
- remap_blocks: bfloat16 [4, 32, 256, 128, 128], P('comp', 'tile'), may hold values from -0.5 to 0.5
Outputs:
- new_fields: float32 [4, 32, 1966080], P('comp', 'tile')
Inputs may be any that keep to these rules, and one draw needn't show every extreme that they name: `target_tile`: among one device's 256 entries no tile is named more than 16 times; in every draw some device names some tile exactly 16 times. `atm_mixing`: each matrix has a diagonal above 0.7 and nonnegative entries whose off-diagonal sum in every row stays below 0.7. `ocean_mixing`: each matrix has a diagonal above 0.7 and nonnegative entries whose off-diagonal sum in every row stays below 0.7.
All inputs are finite; a program needn't handle non-finite values. No bound on the sum of `sea_mask` on one device may be relied on, other than what follows from the above.
Results may differ from a plain program's by a relative error of at most 0.0003.
Values sent between devices are 32-bit elements; how exact they have to be, the bound alone decides.
No kernel may reach another device: no remote copies, remote signals or barrier semaphores. Data moves between devices by JAX's collectives and lax.ppermute only.
A program may use at most 128 MiB of HBM per device.

v0:
```python
import jax
import jax.numpy as jnp
from jax import lax
from jax.sharding import PartitionSpec as P

FA = 3
FO = 4
LA = 128
LO = 80


COUPLE_RATE = 0.1
NU_ATMOS = 0.02
NU_OCEAN = 0.015


def with_halo(block, sides, width):
    for axis, dim in sides:
        count = lax.axis_size(axis)
        forward = [(i, i + 1) for i in range(count - 1)]
        forward.append((count - 1, 0))
        backward = [(target, source) for source, target in forward]
        low = lax.ppermute(
            lax.slice_in_dim(block, block.shape[dim] - width, None, axis=dim), axis, forward
        )
        high = lax.ppermute(lax.slice_in_dim(block, 0, width, axis=dim), axis, backward)
        block = jnp.concatenate([low, block, high], axis=dim)
    return block


def laplace(widened):
    middle = widened[..., 1:-1, :]
    padded = jnp.pad(middle, [(0, 0)] * (middle.ndim - 1) + [(1, 1)])
    return (
        widened[..., 2:, :]
        + widened[..., :-2, :]
        + padded[..., 2:]
        + padded[..., :-2]
        - 4.0 * middle
    )


def mixing(matrix, column_state):
    return jnp.einsum("flm,fmcr->flcr", matrix, column_state, precision=lax.Precision.HIGHEST)


def local(
    fields, atm_mixing, ocean_mixing, sea_mask, source_slot, target_tile, target_slot, remap_blocks
):
    n_comp = lax.axis_size("comp")
    n_tile = lax.axis_size("tile")
    groups = n_comp - 1
    is_sea = lax.axis_index("comp") == groups
    sea_cols = sea_mask.shape[2]
    row_count = sea_mask.shape[3]
    atm_cols = sea_cols * 5 // 6
    sea_flags = sea_mask[0, 0].astype(jnp.float32)
    column_data = fields[0, 0]
    sources = source_slot[0, 0]
    targets = target_tile[0, 0, :, 0]
    target_codes = target_slot[0, 0]
    weights = remap_blocks[0, 0]
    entries = sources.shape[0]

    def atm_pick(values):
        surface = values.reshape(FA, LA, atm_cols, row_count)[:, LA - 1].astype(jnp.bfloat16)
        return jnp.take(surface, sources % atm_cols, axis=1)

    def sea_pick(values):
        surface = values.reshape(FO, LO, sea_cols, row_count)[:FA, 0].astype(jnp.bfloat16)
        return jnp.take(surface, sources % sea_cols, axis=1)

    picked = lax.cond(is_sea, sea_pick, atm_pick, column_data)
    partials = jnp.einsum("pij,fpj->pfi", weights, picked, preferred_element_type=jnp.float32)
    partials = partials.reshape(entries, FA * row_count)
    dest_group = jnp.where(is_sea, target_codes % (groups * atm_cols) // atm_cols, groups)
    dest_block = jnp.where(is_sea, target_codes % atm_cols, target_codes % sea_cols)
    row_ids = (dest_group * n_tile + targets) * sea_cols + dest_block
    chooser = (
        jnp.arange(sea_cols * lax.axis_size(("comp", "tile")), dtype=jnp.int32)[:, None]
        == row_ids[None, :]
    )
    forcing = lax.psum_scatter(
        jnp.dot(chooser.astype(jnp.float32), partials, precision=lax.Precision.HIGHEST),
        ("comp", "tile"),
        scatter_dimension=0,
        tiled=True,
    )
    forcing = jnp.moveaxis(forcing.reshape(sea_cols, FA, row_count), 1, 0)

    def atm_force(values):
        column_state = values.reshape(FA, LA, atm_cols, row_count)
        pushed = COUPLE_RATE * forcing[:, :atm_cols] * sea_flags[:atm_cols]
        return column_state.at[:, LA - 1].add(pushed).reshape(-1)

    def sea_force(values):
        column_state = values.reshape(FO, LO, sea_cols, row_count)
        pushed = COUPLE_RATE * forcing * sea_flags
        return column_state.at[:FA, 0].add(pushed).reshape(-1)

    column_data = lax.cond(is_sea, sea_force, atm_force, column_data)
    rim_rows = FA * LA

    def atm_edges(values):
        column_state = values.reshape(FA * LA, atm_cols, row_count)
        return jnp.concatenate([column_state[:, :2], column_state[:, -2:]], axis=1)

    def sea_edges(values):
        column_state = values.reshape(FO * LO, sea_cols, row_count)
        edge_cols = jnp.concatenate([column_state[:, :2], column_state[:, -2:]], axis=1)
        return jnp.pad(edge_cols, ((0, rim_rows - FO * LO), (0, 0), (0, 0)))

    def atm_step(values, left_rim, right_rim):
        column_state = values.reshape(FA * LA, atm_cols, row_count)
        widened = jnp.concatenate([left_rim, column_state, right_rim], axis=1).reshape(
            FA, LA, atm_cols + 4, row_count
        )
        smoothed = column_state.reshape(FA, LA, atm_cols, row_count) - NU_ATMOS * laplace(
            laplace(widened)
        )
        return mixing(atm_mixing, smoothed).reshape(-1)

    def sea_step(values, left_rim, right_rim):
        column_state = values.reshape(FO * LO, sea_cols, row_count)
        widened = jnp.concatenate([left_rim[: FO * LO], column_state, right_rim[: FO * LO]], axis=1)
        widened = widened.reshape(FO, LO, sea_cols + 4, row_count)
        smoothed = column_state.reshape(FO, LO, sea_cols, row_count) - NU_OCEAN * laplace(
            laplace(widened)
        )
        return (mixing(ocean_mixing, smoothed) * sea_flags).reshape(-1)

    for repeat in range(2):
        edge_cols = lax.cond(is_sea, sea_edges, atm_edges, column_data)
        widened_edges = with_halo(edge_cols, (("tile", 1),), 2)
        left_rim = widened_edges[:, :2]
        right_rim = widened_edges[:, 6:]
        column_data = lax.cond(is_sea, sea_step, atm_step, column_data, left_rim, right_rim)
    return column_data.reshape(1, 1, -1)


def solution(mesh):
    in_specs = (
        P("comp", "tile", None),
        P(),
        P(),
        P("comp", "tile", None, None),
        P("comp", "tile", None),
        P("comp", "tile", None, None),
        P("comp", "tile", None),
        P("comp", "tile", None, None, None),
    )
    out_specs = P("comp", "tile", None)
    return jax.shard_map(local, mesh=mesh, in_specs=in_specs, out_specs=out_specs, check_vma=False)
```

profile of v0, /device:TPU:1, one launch (start us, length us, event | category | flops | bytes accessed | tf_op | source)
XLA Modules:
  0.0 1004.9 jit_solution(5197886718073198112)
XLA Ops:
  6.5 6.5 copy.99
  13.1 86.8 %conditional.6 = (bf16[3,256,128]{2,0,1:T(4,128)(2,1)S(1)}) conditional(s32[]{:T(128)} %convert_element_type.38, (s32[256]{0:T(256)S(1)}, f32[1,1,1966080]{2,1,0:T(1,128)}) %tuple.92, (s32[256]{0:T(256)S(1)}, f32[1,1,1966080]{2,1,0:T(1,128)}) %tuple.93), branch_computations={%region_0.1_spmd, %region_1.2_spmd} | conditional | flops 2068480 | bytes 12739080 | solution.py:73
  13.1 84.5 %convert_reduce_fusion = bf16[1966080]{0:T(1024)(128)(2,1)} fusion(f32[1,1,1966080]{2,1,0:T(1,128)} %get-tuple-element.109), kind=kLoop, calls=%fused_computation.97 | loop fusion | flops 1966080 | bytes 11796480 | tf_op jit(solution)/shard_map/convert.1
  97.6 0.8 slice.263
  98.4 1.0 gather_fusion
  99.4 0.3 select_bitcast_fusion
  99.9 0.0 copy-start.15
  99.9 7.8 fusion.58
  107.7 0.2 copy.50
  108.0 0.0 copy-start.12
  108.0 7.5 fusion.60
  115.5 0.0 reduce-scatter.2.cloned.1.call-update
  115.5 676.7 %reduce-scatter.2.cloned.1.call-done = f32[48,384]{1,0:T(8,128)} async-done(((f32[6144,384]{1,0:T(8,128)}), f32[48,384]{1,0:T(8,128)}) %reduce-scatter.2.cloned.1.call-update) | async-done | bytes 73744 | tf_op jit(solution)/shard_map/reduce_scatter | solution.py:83
  792.2 0.9 reshape.226
  793.1 1.5 conditional.7
  793.2 1.5 fusion.2
  794.6 2.5 conditional.8
  794.6 2.2 fusion.64
  796.8 0.4 pad_maximum_fusion
  797.2 0.3 fusion.69
  797.5 0.1 collective-permute-start.1
  797.6 7.2 collective-permute-start
  804.8 9.3 collective-permute-done.1
  814.1 87.2 %conditional.9 = (f32[1966080]{0:T(1024)}) conditional(s32[]{:T(128)} %convert_element_type.38, (f32[1966080]{0:T(1024)}, f32[384,2,128]{2,1,0:T(2,128)S(1)}, f32[384,2,128]{2,1,0:T(2,128)S(1)}, f32[3,128,128]{2,1,0:T(8,128)}) %tuple.54, (f32[1966080]{0:T(1024)}, f32[384,2,128]{2,1,0:T(2,128)S(1)}, f32[384,2,128]{2,1,0:T(2,128)S(1)}, ...), branch_computations={%region_7.8_spmd, %region_8.9_spmd} | conditional | flops 3052240896 | bytes 195625088 | solution.py:137
  814.5 0.7 copy-done.7
  815.2 8.3 pad_maximum_fusion.1
  823.5 13.7 %fusion.6 = f32[3,128,42,128]{3,2,1,0:T(8,128)S(1)} fusion(f32[3,128,42,128]{3,2,1,0:T(8,128)} %pad_maximum_fusion.1, f32[3,128,2,128]{3,2,1,0:T(2,128)} %bitcast.123, f32[3,128,40,128]{3,2,1,0:T(8,128)S(1)} %bitcast.94, f32[3,128,2,128]{3,2,1,0:T(2,128)S(1)} %bitcast.119), kind=kLoop, calls=%fused_computation.20 | loop fusion | flops 14450688 | bytes 25165824 | tf_op jit(solution)/shard_map/cond/branch_0_fun/sub | solution.py:35
  837.2 3.6 copy-done.4
  840.9 3.9 slice.249
  844.7 20.5 %fusion.11 = f32[3,128,40,128]{3,2,1,0:T(8,128)} fusion(f32[3,128,40,128]{3,2,1,0:T(8,128)} %bitcast.93, f32[3,128,40,128]{3,2,1,0:T(8,128)} %slice.249, f32[3,128,42,128]{3,2,1,0:T(8,128)} %copy-done.4), kind=kLoop, calls=%fused_computation.28 | loop fusion | flops 13762560 | bytes 39321600 | tf_op jit(solution)/shard_map/cond/branch_0_fun/sub | solution.py:118
  865.2 17.0 %fusion.14 = f32[3,128,40,128]{1,3,2,0:T(8,128)} fusion(f32[3,128,40,128]{3,2,1,0:T(8,128)} %fusion.11, f32[3,128,128]{2,1,0:T(8,128)S(1)} %copy-done.8), kind=kOutput, calls=%fused_computation.32 | convolution fusion | flops 3019898880 | bytes 15925248 | tf_op jit(solution)/shard_map/cond/branch_0_fun/flm,fmcr->flcr/dot_general | solution.py:44
  882.3 9.2 copy.41
  901.3 2.6 conditional.10
  901.3 2.2 fusion.66
  903.4 0.4 pad_maximum_fusion.5
  903.8 0.3 fusion.68
  904.1 0.1 collective-permute-start.3
  904.2 7.2 collective-permute-start.2
  911.4 8.4 collective-permute-done.3
  919.8 78.0 %conditional.11 = (f32[1,1,1966080]{2,1,0:T(1,128)}) conditional(s32[]{:T(128)} %convert_element_type.38, (f32[1966080]{0:T(1024)}, f32[384,2,128]{2,1,0:T(2,128)S(1)}, f32[384,2,128]{2,1,0:T(2,128)S(1)}, f32[3,128,128]{2,1,0:T(8,128)}) %tuple.56, (f32[1966080]{0:T(1024)}, f32[384,2,128]{2,1,0:T(2,128)S(1)}, f32[384,2,128]{2,1,0:T(2,128)S(1)}, ...), branch_computations={%region_11.12_spmd, %region_12.13_spmd} | conditional | flops 3052240896 | bytes 195625088 | solution.py:137
  919.8 0.7 copy-done.6
  920.6 8.3 pad_maximum_fusion.6
  928.9 13.7 %fusion.33 = f32[3,128,42,128]{3,2,1,0:T(8,128)S(1)} fusion(f32[3,128,42,128]{3,2,1,0:T(8,128)} %pad_maximum_fusion.6, f32[3,128,2,128]{3,2,1,0:T(2,128)} %bitcast.121, f32[3,128,40,128]{3,2,1,0:T(8,128)S(1)} %bitcast.106, f32[3,128,2,128]{3,2,1,0:T(2,128)S(1)} %bitcast.117), kind=kLoop, calls=%fused_computation.63 | loop fusion | flops 14450688 | bytes 25165824 | tf_op jit(solution)/shard_map/cond/branch_0_fun/sub | solution.py:35
  942.6 3.6 copy-done.5
  946.2 4.0 slice.259
  950.2 20.5 %fusion.38 = f32[3,128,40,128]{3,2,1,0:T(8,128)} fusion(f32[3,128,40,128]{3,2,1,0:T(8,128)} %bitcast.105, f32[3,128,40,128]{3,2,1,0:T(8,128)} %slice.259, f32[3,128,42,128]{3,2,1,0:T(8,128)} %copy-done.5), kind=kLoop, calls=%fused_computation.71 | loop fusion | flops 13762560 | bytes 39321600 | tf_op jit(solution)/shard_map/cond/branch_0_fun/sub | solution.py:118
  970.7 17.0 %fusion.41 = f32[3,128,40,128]{1,3,2,0:T(8,128)} fusion(f32[3,128,40,128]{3,2,1,0:T(8,128)} %fusion.38, f32[3,128,128]{2,1,0:T(8,128)S(1)} %copy-done.9), kind=kOutput, calls=%fused_computation.75 | convolution fusion | flops 3019898880 | bytes 15925248 | tf_op jit(solution)/shard_map/cond/branch_0_fun/flm,fmcr->flcr/dot_general | solution.py:44
  987.7 9.1 copy.45
  (29 shorter events, 0.1 us)
Async XLA Ops:
  6.5 6.5 copy-start.13
  6.5 6.5 copy-start.14
  6.5 785.7 %reduce-scatter.2.cloned.1.call-start = ((), (), s32[]{:S(2)}) async-start(), calls=%async_computation.1 | async-start | bytes 9510912 | tf_op jit(solution)/shard_map/reduce_scatter | solution.py:83
  99.9 8.0 copy-start.15
  108.0 7.5 copy-start.12
  797.5 16.6 %collective-permute-start.1 = (f32[384,2,128]{2,1,0:T(2,128)S(1)}, f32[384,2,128]{2,1,0:T(2,128)S(1)}, u32[]{:S(2)}, u32[]{:S(2)}) collective-permute-start(f32[384,2,128]{2,1,0:T(2,128)S(1)} %get-tuple-element.163), channel_id=1, source_target_pairs={{0,1},{1,2},{2,3},{3,4},{4,5},{5,6},{6,7},{7,8},{8,9},{9,10},{10,1... | collective-permute-start | bytes 1179656 | tf_op jit(solution)/shard_map/ppermute | solution.py:23
  797.6 16.5 %collective-permute-start = (f32[384,2,128]{2,1,0:T(2,128)S(1)}, f32[384,2,128]{2,1,0:T(2,128)S(1)}, u32[]{:S(2)}, u32[]{:S(2)}) collective-permute-start(f32[384,2,128]{2,1,0:T(2,128)S(1)} %get-tuple-element.164), channel_id=1, source_target_pairs={{1,0},{2,1},{3,2},{4,3},{5,4},{6,5},{7,6},{8,7},{9,8},{10,9},{11,1... | collective-permute-start | bytes 1179656 | tf_op jit(solution)/shard_map/ppermute | solution.py:26
  814.5 0.7 copy-start.7
  815.2 8.3 copy-start
  837.2 3.6 copy-start.4
  844.7 20.5 %copy-start.8 = (f32[3,128,128]{2,1,0:T(8,128)S(1)}, f32[3,128,128]{2,1,0:T(8,128)}, u32[]{:S(2)}) copy-start(f32[3,128,128]{2,1,0:T(8,128)} %get-tuple-element.121) | copy-start | bytes 589828 | tf_op jit(solution)/shard_map/cond
  904.1 15.7 %collective-permute-start.3 = (f32[384,2,128]{2,1,0:T(2,128)S(1)}, f32[384,2,128]{2,1,0:T(2,128)S(1)}, u32[]{:S(2)}, u32[]{:S(2)}) collective-permute-start(f32[384,2,128]{2,1,0:T(2,128)S(1)} %get-tuple-element.161), channel_id=1, source_target_pairs={{0,1},{1,2},{2,3},{3,4},{4,5},{5,6},{6,7},{7,8},{8,9},{9,10},{10,1... | collective-permute-start | bytes 1179656 | tf_op jit(solution)/shard_map/ppermute | solution.py:23
  904.2 15.6 %collective-permute-start.2 = (f32[384,2,128]{2,1,0:T(2,128)S(1)}, f32[384,2,128]{2,1,0:T(2,128)S(1)}, u32[]{:S(2)}, u32[]{:S(2)}) collective-permute-start(f32[384,2,128]{2,1,0:T(2,128)S(1)} %get-tuple-element.162), channel_id=1, source_target_pairs={{1,0},{2,1},{3,2},{4,3},{5,4},{6,5},{7,6},{8,7},{9,8},{10,9},{11,1... | collective-permute-start | bytes 1179656 | tf_op jit(solution)/shard_map/ppermute | solution.py:26
  919.8 0.7 copy-start.6
  920.6 8.3 copy-start.1
  942.6 3.6 copy-start.5
  950.2 20.5 %copy-start.9 = (f32[3,128,128]{2,1,0:T(8,128)S(1)}, f32[3,128,128]{2,1,0:T(8,128)}, u32[]{:S(2)}) copy-start(f32[3,128,128]{2,1,0:T(8,128)} %get-tuple-element.130) | copy-start | bytes 589828 | tf_op jit(solution)/shard_map/cond
Sparse Core Ops, SparseCore 0:
  115.6 676.5 reduce-scatter.1
where the time goes:
time: 1010 us; the launch traced here: 1000 us
  waiting for transfers between devices  694 us (69%)
  other arithmetic  172 us (17%)
  matrix products  49.3 us (5%)
  local copies, waits for them, and re-layouts  49.2 us (5%)
  starting transfers between devices  14.5 us (1%)
  between operations  13.8 us (1%)
  loops' own time  11.5 us (1%)
    reduce_scatter x1, waiting for transfers between devices, local(): lax.psum_scatter(jnp.dot(chooser.astype(jnp.float32), partials, precision...  677 us
    another operation x1, other arithmetic  84.5 us
    sub x2, other arithmetic, atm_step(): column_state.reshape(FA, LA, atm_cols, row_count)  41 us
    dot_general x2, matrix products, mixing(): jnp.einsum('flm,fmcr->flcr', matrix, column_state, precision=lax.Precisio...  34.1 us
    sub x2, other arithmetic, laplace(): widened[..., 2:, :] + widened[..., :-2, :] + padded[..., 2:]  27.4 us
  transfers between devices with their start and end apart: 5, of which 3 were waited for; matrix products, arithmetic and copies ran while one was open for 0% of the time, Pallas kernels for 0%

commit v1 on v0

v1 whole, which is shorter than its diff:
```python
import functools

import jax
import jax.numpy as jnp
from jax import lax
from jax.experimental import pallas as pl
from jax.experimental.pallas import tpu as pltpu
from jax.sharding import PartitionSpec as P

FA = 3
FO = 4
LA = 128
LO = 80
R = 128
CAP = 16

COUPLE_RATE = 0.1
NU_ATMOS = 0.02
NU_OCEAN = 0.015

HALO = 4
CHUNK_ROWS = 56
MIB = 1 << 20


def lane_edges(rows):
    lane = lax.broadcasted_iota(jnp.int32, (rows, R), 1)
    return lane == 0, lane == R - 1


def lap(before, middle, after, edges):
    first, last = edges
    down = jnp.where(first, 0.0, pltpu.roll(middle, 1, 1))
    up = jnp.where(last, 0.0, pltpu.roll(middle, R - 1, 1))
    return (before + after) + (down + up) - 4.0 * middle


def filtered_columns(column, count, nu, mask, edges):
    x, l1, y, l3 = {}, {}, {}, {}
    for k in range(-HALO, count + HALO):
        x[k] = column(k)
        j = k - 1
        if j >= -3:
            l1[j] = lap(x[j - 1], x[j], x[j + 1], edges)
        j = k - 2
        if j >= -2:
            y[j] = x[j] - nu * lap(l1[j - 1], l1[j], l1[j + 1], edges)
            if mask is not None:
                y[j] = y[j] * mask(j)
            x.pop(j - 1, None)
            l1.pop(j - 1, None)
        j = k - 3
        if j >= -1:
            l3[j] = lap(y[j - 1], y[j], y[j + 1], edges)
        j = k - 4
        if j >= 0:
            z = y[j] - nu * lap(l3[j - 1], l3[j], l3[j + 1], edges)
            if mask is not None:
                z = z * mask(j)
            y.pop(j - 1, None)
            l3.pop(j - 1, None)
            yield j, z


def split_two(value):
    high = value.astype(jnp.bfloat16)
    return high, (value - high.astype(jnp.float32)).astype(jnp.bfloat16)


def remap_kernel(per_step, base_ref, idx0_ref, idx1_ref, surf_ref, codes_ref, w_ref, out_ref, lhs_ref):
    step = pl.program_id(0)
    groups = per_step // 4

    @pl.when(step == 0)
    def _():
        out_ref[...] = jnp.zeros_like(out_ref)
        for t in range(codes_ref.shape[0]):
            out_ref[pl.ds(t * CHUNK_ROWS + 3 * CAP, 1), :] = codes_ref[pl.ds(t, 1), :]
        table = surf_ref[...]
        spots = lax.broadcasted_iota(jnp.int32, (idx0_ref.shape[0], table.shape[0]), 1)
        for half, ref in enumerate((idx0_ref, idx1_ref)):
            pick = jnp.where(spots == ref[...], 1.0, 0.0).astype(jnp.bfloat16)
            lhs_ref[:, half * R : (half + 1) * R] = jnp.dot(
                pick, table, preferred_element_type=jnp.float32
            ).astype(jnp.bfloat16)

    for g in range(groups):
        left = w_ref[4 * g : 4 * g + 2].reshape(2 * R, R)
        right = w_ref[4 * g + 2 : 4 * g + 4].reshape(2 * R, R)
        block = jnp.concatenate([left, right], axis=1)
        rows = lhs_ref[pl.ds(pl.multiple_of((step * groups + g) * 16, 16), 16), :]
        res = lax.dot_general(
            rows, block, (((1,), (1,)), ((), ())), preferred_element_type=jnp.float32
        )
        for e in range(4):
            base = base_ref[step * per_step + 4 * g + e]
            half = e % 2
            for f in range(FA):
                out_ref[pl.ds(base + f * CAP, 1), :] = res[
                    f * 4 + e : f * 4 + e + 1, half * R : (half + 1) * R
                ]


def remap(base, idx0, idx1, surf, codes, weights):
    entries = weights.shape[0]
    per_step = 32
    whole = lambda shape: pl.BlockSpec(shape, lambda i, b: (0,) * len(shape))
    n_tile = codes.shape[0]
    out_shape = (n_tile * CHUNK_ROWS, R)
    return pl.pallas_call(
        functools.partial(remap_kernel, per_step),
        out_shape=jax.ShapeDtypeStruct(out_shape, jnp.float32),
        grid_spec=pltpu.PrefetchScalarGridSpec(
            num_scalar_prefetch=1,
            grid=(entries // per_step,),
            in_specs=[
                whole(idx0.shape),
                whole(idx1.shape),
                whole(surf.shape),
                whole(codes.shape),
                pl.BlockSpec((per_step, R, R), lambda i, b: (i, 0, 0)),
            ],
            out_specs=whole(out_shape),
            scratch_shapes=[pltpu.VMEM((entries * 4, 2 * R), jnp.bfloat16)],
        ),
        compiler_params=pltpu.CompilerParams(vmem_limit_bytes=32 * MIB),
        cost_estimate=pl.CostEstimate(
            flops=2 * entries * R * R * 16, bytes_accessed=weights.size * 2, transcendentals=0
        ),
        name="remap",
    )(base, idx0, idx1, surf, codes, weights)


def combine_kernel(rows, recv_ref, out_ref):
    n_tile = recv_ref.shape[0]
    spots = lax.broadcasted_iota(jnp.int32, (rows, R), 0).astype(jnp.float32) + 1.0
    total = [jnp.zeros((rows, R), jnp.float32) for _ in range(FA)]
    for g in range(n_tile // 8):
        code = jnp.sum(recv_ref[g * 8 : (g + 1) * 8, 3 * CAP, :], axis=0, keepdims=True)
        pick = jnp.where(spots == code, 1.0, 0.0).astype(jnp.bfloat16)
        for f in range(FA):
            value = recv_ref[g * 8 : (g + 1) * 8, f * CAP : (f + 1) * CAP, :].reshape(8 * CAP, R)
            high = value.astype(jnp.bfloat16)
            rest = value - high.astype(jnp.float32)
            middle = rest.astype(jnp.bfloat16)
            both = jnp.dot(
                pick,
                jnp.concatenate([high, middle], axis=1),
                preferred_element_type=jnp.float32,
            )
            total[f] = total[f] + (both[:, :R] + both[:, R:])
    per_group = rows // 4
    for f in range(FA):
        for c in range(4):
            out_ref[c, f] = total[f][c * per_group : (c + 1) * per_group]


def combine(recv, sea_cols):
    return pl.pallas_call(
        functools.partial(combine_kernel, 4 * sea_cols),
        out_shape=jax.ShapeDtypeStruct((4, FA, sea_cols, R), jnp.float32),
        compiler_params=pltpu.CompilerParams(vmem_limit_bytes=32 * MIB),
        name="combine",
    )(recv)


def dynamics_part(
    fields, levels, cols, nu, x_ref, left_ref, right_ref, matrix_ref, mask_ref, out_ref, x_vmem, y_vmem, sems
):
    rows_per_field = levels * cols
    copies = []
    for f in range(fields):
        span = pl.ds(f * rows_per_field, rows_per_field)
        copies.append(pltpu.make_async_copy(x_ref.at[span], x_vmem.at[span], sems.at[f]))
        copies[-1].start()
    edges = lane_edges(16)
    for f in range(fields):
        matrix = matrix_ref[f]
        squared = jnp.dot(
            matrix, matrix, precision=lax.Precision.HIGHEST, preferred_element_type=jnp.float32
        )
        high, low = split_two(squared)
        stacked = jnp.concatenate(
            [
                jnp.concatenate([high, high], axis=1),
                jnp.concatenate([low, jnp.zeros_like(low)], axis=1),
            ],
            axis=0,
        )
        copies[f].wait()

        def filter_rows(i, carry, f=f):
            first = f * levels + i * 16

            def column(k):
                if k < 0:
                    return left_ref[pl.ds(first * HALO + k + HALO, 16, stride=HALO), :]
                if k >= cols:
                    return right_ref[pl.ds(first * HALO + k - cols, 16, stride=HALO), :]
                return x_vmem[pl.ds(first * cols + k, 16, stride=cols), :]

            mask = None
            if mask_ref is not None:
                mask = lambda k: jnp.broadcast_to(mask_ref[k + 2 : k + 3, :], (16, R))
            for k, z in filtered_columns(column, cols, nu, mask, edges):
                z_high, z_low = split_two(z)
                spot = pl.multiple_of(i * 16, 16)
                y_vmem[pl.ds(spot, 16), k * R : (k + 1) * R] = z_high
                y_vmem[pl.ds(levels + spot, 16), k * R : (k + 1) * R] = z_low
            return carry

        lax.fori_loop(0, levels // 16, filter_rows, 0)

        for j in range(cols // 2):
            both = jnp.dot(
                stacked,
                y_vmem[: 2 * levels, 2 * j * R : 2 * (j + 1) * R],
                preferred_element_type=jnp.float32,
            )
            mixed = both[:levels] + both[levels:]
            for h in range(2):
                out_ref[pl.ds(f * rows_per_field + 2 * j + h, levels, stride=cols), :] = mixed[
                    :, h * R : (h + 1) * R
                ]


def dynamics_kernel(
    sizes, sea_ref, x_ref, left_ref, right_ref, atm_ref, ocean_ref, mask_ref, out_ref, x_vmem, y_vmem, sems
):
    atm_cols, sea_cols = sizes

    @pl.when(sea_ref[0] == 0)
    def _():
        dynamics_part(
            FA, LA, atm_cols, NU_ATMOS, x_ref, left_ref, right_ref, atm_ref, None, out_ref, x_vmem, y_vmem, sems
        )

    @pl.when(sea_ref[0] != 0)
    def _():
        dynamics_part(
            FO, LO, sea_cols, NU_OCEAN, x_ref, left_ref, right_ref, ocean_ref, mask_ref, out_ref, x_vmem, y_vmem, sems
        )


def dynamics(is_sea, x, left, right, atm_mixing, ocean_mixing, mask, sizes):
    vmem = pl.BlockSpec(memory_space=pltpu.VMEM)
    rows = x.shape[0]
    width = max(sizes) * R
    return pl.pallas_call(
        functools.partial(dynamics_kernel, sizes),
        out_shape=pltpu.VMEM((rows, R), jnp.float32),
        in_specs=[pl.BlockSpec(memory_space=pltpu.SMEM), pl.BlockSpec(memory_space=pl.ANY)] + [vmem] * 5,
        out_specs=vmem,
        scratch_shapes=[
            pltpu.VMEM((rows, R), jnp.float32),
            pltpu.VMEM((2 * LA, width), jnp.bfloat16),
            pltpu.SemaphoreType.DMA((FO,)),
        ],
        compiler_params=pltpu.CompilerParams(vmem_limit_bytes=40 * MIB),
        cost_estimate=pl.CostEstimate(
            flops=8 * rows * R * R, bytes_accessed=24 * rows * R, transcendentals=0
        ),
        name="dynamics",
    )(is_sea, x, left, right, atm_mixing, ocean_mixing, mask)


def filter_forcing(cols, nu, forcing_ref, halo_ref, mask_ref, work_ref, g_ref):
    lo, hi = 8, 8 + cols
    first, last = lane_edges(cols + 16)
    lane_edge = (first, last)
    for f in range(FA):
        work_ref[0 : cols + 16, :] = jnp.zeros((cols + 16, R), jnp.float32)
        work_ref[lo - HALO : lo, :] = halo_ref[0, f]
        work_ref[lo:hi, :] = forcing_ref[f, :cols]
        work_ref[hi : hi + HALO, :] = halo_ref[1, f]
        value = work_ref[0 : cols + 16, :]

        def along(v):
            return lap(pltpu.roll(v, 1, 0), v, pltpu.roll(v, cols + 15, 0), lane_edge)

        value = value - nu * along(along(value))
        if mask_ref is not None:
            value = value * mask_ref[0 : cols + 16, :]
        value = value - nu * along(along(value))
        if mask_ref is not None:
            value = value * mask_ref[0 : cols + 16, :]
        g_ref[f, :cols] = value[lo:hi]


def update_part(cols, column_ref, part_ref, out_ref, g_ref, stage_ref, sems, pieces, levels):
    rows = part_ref.shape[0] // pieces
    per_piece = rows // cols
    for p in range(pieces):
        for q in range(per_piece):
            number = p * per_piece + q
            f = number // levels
            span = pl.ds(number * cols, cols)
            if f < FA:
                stage_ref[span, :] = part_ref[span, :] + column_ref[number] * g_ref[f, :cols]
            else:
                stage_ref[span, :] = part_ref[span, :]
        span = pl.ds(p * rows, rows)
        pltpu.make_async_copy(stage_ref.at[span], out_ref.at[span], sems.at[p]).start()
    for p in range(pieces):
        span = pl.ds(p * rows, rows)
        pltpu.make_async_copy(stage_ref.at[span], out_ref.at[span], sems.at[p]).wait()


def update_kernel(
    sizes, pieces, sea_ref, column_ref, part_ref, forcing_ref, halo_ref, mask_ref, out_ref, work_ref, g_ref, stage_ref, sems
):
    atm_cols, sea_cols = sizes

    @pl.when(sea_ref[0] == 0)
    def _():
        filter_forcing(atm_cols, NU_ATMOS, forcing_ref, halo_ref, None, work_ref, g_ref)
        update_part(atm_cols, column_ref, part_ref, out_ref, g_ref, stage_ref, sems, pieces, LA)

    @pl.when(sea_ref[0] != 0)
    def _():
        filter_forcing(sea_cols, NU_OCEAN, forcing_ref, halo_ref, mask_ref, work_ref, g_ref)
        update_part(sea_cols, column_ref, part_ref, out_ref, g_ref, stage_ref, sems, pieces, LO)


def update(is_sea, column, part, forcing, halo, mask, sizes):
    vmem = pl.BlockSpec(memory_space=pltpu.VMEM)
    smem = pl.BlockSpec(memory_space=pltpu.SMEM)
    rows = part.shape[0]
    pieces = 8
    return pl.pallas_call(
        functools.partial(update_kernel, sizes, pieces),
        out_shape=jax.ShapeDtypeStruct((rows, R), jnp.float32),
        in_specs=[smem, smem, vmem, vmem, vmem, vmem],
        out_specs=pl.BlockSpec(memory_space=pl.ANY),
        scratch_shapes=[
            pltpu.VMEM((max(sizes) + 16, R), jnp.float32),
            pltpu.VMEM((FA, max(sizes), R), jnp.float32),
            pltpu.VMEM((rows, R), jnp.float32),
            pltpu.SemaphoreType.DMA((pieces,)),
        ],
        compiler_params=pltpu.CompilerParams(vmem_limit_bytes=40 * MIB),
        cost_estimate=pl.CostEstimate(
            flops=2 * rows * R, bytes_accessed=8 * rows * R, transcendentals=0
        ),
        name="update",
    )(is_sea, column, part, forcing, halo, mask)


def local(
    fields, atm_mixing, ocean_mixing, sea_mask, source_slot, target_tile, target_slot, remap_blocks
):
    n_comp = lax.axis_size("comp")
    n_tile = lax.axis_size("tile")
    groups = n_comp - 1
    is_sea = lax.axis_index("comp") == groups
    sea_cols = sea_mask.shape[2]
    atm_cols = sea_cols * 5 // 6
    sizes = (atm_cols, sea_cols)
    sea_flag = is_sea.astype(jnp.int32).reshape(1)
    mask = sea_mask[0, 0].astype(jnp.float32)
    state = fields[0, 0]
    sources = source_slot[0, 0]
    tiles = target_tile[0, 0, :, 0]
    codes = target_slot[0, 0]
    weights = remap_blocks[0, 0]
    entries = sources.shape[0]
    forward = [(i, (i + 1) % n_tile) for i in range(n_tile)]
    backward = [(b, a) for a, b in forward]

    def atm_edges(values):
        split = values.reshape(FA * LA, atm_cols // HALO, HALO, R)
        return split[:, 0], split[:, -1]

    def sea_edges(values):
        split = values.reshape(FO * LO, sea_cols // HALO, HALO, R)
        spare = FA * LA - FO * LO
        cut = mask.reshape(sea_cols // HALO, HALO, R)
        fill = lambda edge, own: jnp.concatenate(
            [edge, own[None], jnp.zeros((spare - 1, HALO, R), jnp.float32)], axis=0
        )
        return fill(split[:, 0], cut[0]), fill(split[:, -1], cut[-1])

    low_edge, high_edge = lax.cond(is_sea, sea_edges, atm_edges, state)
    left = lax.ppermute(high_edge, "tile", forward)
    right = lax.ppermute(low_edge, "tile", backward)

    def atm_surface(values):
        top = values.reshape(FA, LA, atm_cols, R)[:, LA - 1]
        return jnp.pad(top, ((0, 0), (0, sea_cols - atm_cols), (0, 0))).astype(jnp.bfloat16)

    def sea_surface(values):
        return values.reshape(FO, LO, sea_cols, R)[:FA, 0].astype(jnp.bfloat16)

    surface = lax.cond(is_sea, sea_surface, atm_surface, state).reshape(FA * sea_cols, R)
    source = jnp.where(is_sea, sources % sea_cols, sources % atm_cols)
    order = jnp.arange(entries)
    same = (tiles[:, None] == tiles[None, :]) & (order[None, :] < order[:, None])
    rank = jnp.sum(same.astype(jnp.int32), axis=1)
    base = tiles * CHUNK_ROWS + rank
    row = jnp.arange(16)
    pick_row = source.reshape(entries // 4, 1, 4) + (jnp.arange(4) * sea_cols)[None, :, None]
    pick_row = pick_row.reshape(entries // 4, 16)
    in_use = row < 4 * FA
    idx0 = jnp.where(in_use & (row % 4 < 2), pick_row, -1).reshape(entries * 4, 1)
    idx1 = jnp.where(in_use & (row % 4 >= 2), pick_row, -1).reshape(entries * 4, 1)
    dest_group = jnp.where(is_sea, codes % (groups * atm_cols) // atm_cols, groups)
    dest_block = jnp.where(is_sea, codes % atm_cols, codes % sea_cols)
    dest_row = (dest_group * sea_cols + dest_block + 1).astype(jnp.float32)
    slots = jnp.arange(n_tile * CAP)
    slot_code = jnp.sum(
        jnp.where(slots[:, None] == (tiles * CAP + rank)[None, :], dest_row[None, :], 0.0), axis=1
    ).reshape(n_tile, 1, CAP)
    per_row = R // CAP
    own_part = (jnp.arange(per_row) == lax.axis_index("tile") % per_row).astype(jnp.float32)
    code_rows = (slot_code * own_part[None, :, None]).reshape(n_tile, R)
    sent = remap(base, idx0, idx1, surface, code_rows, weights)
    received = lax.all_to_all(
        sent.reshape(n_tile, CHUNK_ROWS, R), "tile", split_axis=0, concat_axis=0, tiled=True
    )

    flat_left = left.reshape(FA * LA * HALO, R)
    flat_right = right.reshape(FA * LA * HALO, R)
    mask_left, mask_right = left[FO * LO], right[FO * LO]
    wide_mask = jnp.concatenate([mask_left[2:], mask, mask_right[:2]], axis=0)
    part = dynamics(
        sea_flag,
        state.reshape(-1, R),
        flat_left,
        flat_right,
        atm_mixing,
        ocean_mixing,
        wide_mask,
        sizes,
    )

    shares = lax.all_to_all(combine(received, sea_cols), "comp", split_axis=0, concat_axis=0, tiled=True)
    pushed = COUPLE_RATE * jnp.sum(shares, axis=0) * mask
    low_part = pushed[:, :HALO]
    high_part = jnp.where(is_sea, pushed[:, sea_cols - HALO :], pushed[:, atm_cols - HALO : atm_cols])
    halo = jnp.stack(
        [lax.ppermute(high_part, "tile", forward), lax.ppermute(low_part, "tile", backward)]
    )
    atm_column = jnp.einsum(
        "flm,fm->fl", atm_mixing, atm_mixing[:, :, LA - 1], precision=lax.Precision.HIGHEST
    ).reshape(-1)
    ocean_column = jnp.einsum(
        "flm,fm->fl", ocean_mixing, ocean_mixing[:, :, 0], precision=lax.Precision.HIGHEST
    ).reshape(-1)
    ocean_column = jnp.pad(ocean_column, (0, FA * LA - FO * LO))
    column = jnp.where(is_sea, ocean_column, atm_column)
    work_mask = jnp.concatenate(
        [jnp.zeros((4, R), jnp.float32), mask_left, mask, mask_right, jnp.zeros((4, R), jnp.float32)], axis=0
    )
    done = update(sea_flag, column, part, pushed, halo, work_mask, sizes)
    return done.reshape(1, 1, -1)


def solution(mesh):
    in_specs = (
        P("comp", "tile", None),
        P(),
        P(),
        P("comp", "tile", None, None),
        P("comp", "tile", None),
        P("comp", "tile", None, None),
        P("comp", "tile", None),
        P("comp", "tile", None, None, None),
    )
    out_specs = P("comp", "tile", None)
    return jax.shard_map(local, mesh=mesh, in_specs=in_specs, out_specs=out_specs, check_vma=False)
```

time: 1010 us -> 225 us (0.22)
  waiting for transfers between devices: 694 us -> 27.9 us
  other arithmetic: 172 us -> 88 us
  Pallas kernels: 0 us -> 60.8 us
  matrix products: 49.3 us -> 0.74 us
  local copies, waits for them, and re-layouts: 49.2 us -> 15.8 us
  starting transfers between devices: 14.5 us -> 31.2 us
  between operations: 13.8 us -> 0.49 us
  loops' own time: 11.5 us -> 0.03 us
    reduce_scatter x1 -> x0, waiting for transfers between devices: 677 us -> none  [local(): lax.psum_scatter(jnp.dot(chooser.astype(jnp.float32), partials, precision...]
    sub x4 -> x0, other arithmetic: 68.4 us -> none  [the longest x2 41 us: atm_step(): column_state.reshape(FA, LA, atm_cols, row_count)]
    pallas_call x0 -> x4, Pallas kernels: none -> 60.8 us  [the longest x1 50.2 us: dynamics(): pl.pallas_call(functools.partial(dynamics_kernel, sizes), out_shape=pltpu...]
    dot_general x4 -> x2, matrix products: 49.3 us -> 0.74 us  [the longest x1 0.38 us: local(): jnp.einsum('flm,fm->fl', atm_mixing, atm_mixing[:, :, LA - 1], precision=...]
    dot_general x3 -> x0, local copies, waits for them, and re-layouts: 18.4 us -> none  [the longest x2 18.2 us: mixing(): jnp.einsum('flm,fmcr->flcr', matrix, column_state, precision=lax.Precisio...]
    concatenate x4 -> x1, other arithmetic: 17.3 us -> 0.01 us  [local(): wide_mask = jnp.concatenate([mask_left[2:], mask, mask_right[:2]], axis=0)]
    all_to_all x0 -> x2, starting transfers between devices: none -> 16.8 us  [the longest x1 11.5 us: local(): lax.all_to_all(sent.reshape(n_tile, CHUNK_ROWS, R), 'tile', split_axis=0,...]
    slice x7 -> x4, local copies, waits for them, and re-layouts: 13.6 us -> 0.37 us  [the longest x1 0.23 us: local(): atm_mixing[:, :, LA - 1]]
  transfers between devices with their start and end apart: 5 -> 6, of which waited for: 3 -> 2; matrix products, arithmetic and copies ran while one was open for 0% -> 2% of each run, Pallas kernels for 0% -> 22%
where the time goes in v1:
time: 225 us
  other arithmetic  88 us (39%)
  Pallas kernels  60.8 us (27%)
  starting transfers between devices  31.2 us (14%)
  waiting for transfers between devices  27.9 us (12%)
  local copies, waits for them, and re-layouts  15.8 us (7%)
    another operation x1, other arithmetic  84.6 us
    pallas_call x1, Pallas kernels, dynamics(): pl.pallas_call(functools.partial(dynamics_kernel, sizes), out_shape=pltpu...  50.2 us
    ppermute x1, waiting for transfers between devices, local(): left = lax.ppermute(high_edge, 'tile', forward)  22.4 us
    all_to_all x1, starting transfers between devices, local(): lax.all_to_all(sent.reshape(n_tile, CHUNK_ROWS, R), 'tile', split_axis=0,...  11.5 us
    unnamed x12, local copies, waits for them, and re-layouts  9.84 us
    ppermute x1, starting transfers between devices, local(): lax.ppermute(low_part, 'tile', backward)  7.18 us
    ppermute x1, starting transfers between devices, local(): right = lax.ppermute(low_edge, 'tile', backward)  5.96 us
    all_to_all x1, waiting for transfers between devices, local(): lax.all_to_all(combine(received, sea_cols), 'comp', split_axis=0, concat_...  5.52 us
  transfers between devices with their start and end apart: 6, of which 2 were waited for; matrix products, arithmetic and copies ran while one was open for 2% of the time, Pallas kernels for 22%

profile of v1, /device:TPU:1, one launch (start us, length us, event | category | flops | bytes accessed | tf_op | source)
XLA Modules:
  0.0 224.9 jit_solution(1830865864232651131)
XLA Ops:
  0.1 0.9 convert_reduce_fusion.2
  1.0 0.1 add.129
  1.1 0.1 add.130
  1.1 0.7 remainder_reduce_fusion
  1.9 0.7 broadcast_remainder_fusion
  2.5 0.1 mul.79
  2.6 0.1 mul.80
  2.7 0.7 multiply_add_fusion
  3.4 0.1 select_reduce_fusion
  3.6 0.1 mul.76
  3.6 0.1 copy.25
  3.7 0.1 rem.118
  3.8 0.1 rem.114
  3.9 0.1 copy.26
  4.0 0.3 broadcast_in_dim.48
  4.4 0.3 broadcast_in_dim.49
  4.8 0.2 add.141
  5.0 0.3 add.142
  5.3 85.3 %conditional.3 = (bf16[144,128]{1,0:T(8,128)(2,1)S(1)}) conditional(s32[]{:T(128)} %convert_element_type.42, f32[1,1,1966080]{2,1,0:T(1,128)} %param.12, f32[1,1,1966080]{2,1,0:T(1,128)} %param.12), branch_computations={%region_3.4_spmd, %region_4.5_spmd} | conditional | flops 1966080 | bytes 11925514 | solution.py:394
  5.3 84.6 %convert_reduce_fusion = bf16[1966080]{0:T(1024)(128)(2,1)} fusion(f32[1,1,1966080]{2,1,0:T(1,128)} %param.2), kind=kLoop, calls=%fused_computation.8 | loop fusion | flops 1966080 | bytes 11796480 | tf_op jit(solution)/shard_map/convert.4
  89.9 0.8 slice_bitcast_fusion.6
  90.6 0.0 copy-start.5
  90.7 0.1 broadcast_select_fusion
  90.8 0.0 copy-start.2
  90.8 3.4 %copy-done.2 = bf16[1,1,256,128,128]{4,3,2,1,0:T(8,128)(2,1)S(1)} copy-done((bf16[1,1,256,128,128]{4,3,2,1,0:T(8,128)(2,1)S(1)}, bf16[1,1,256,128,128]{4,3,2,1,0:T(8,128)(2,1)}, u32[]{:S(2)}) %copy-start.2) | copy-done | bytes 8388632
  94.2 5.2 %remap.1 = f32[1792,128]{1,0:T(8,128)} custom-call(s32[256]{0:T(256)S(1)} %get-tuple-element.37.base_ref, s32[1024,1]{1,0:T(8,128)S(1)} %get-tuple-element.33.idx0_ref, s32[1024,1]{1,0:T(8,128)S(1)} %get-tuple-element.32.idx1_ref, bf16[144,128]{1,0:T(8,128)(2,1)S(1)} %get-tuple-element.46.surf_ref, f32[32,128]{1,0:T(8,128)S(1)} %broadcast_multiply_fusion.2.codes_ref, ...), custom_call_target="tpu_custom_call" | custom-call | flops 134217728 | bytes 8388608 | tf_op jit(solution)/shard_map/remap/pallas_call | solution.py:110
  99.4 11.5 %all-to-all-start = ((f32[32,56,128]{2,1,0:T(8,128)}), f32[32,56,128]{2,1,0:T(8,128)S(1)}, u32[]{:S(2)}, u32[]{:S(2)}) async-start(f32[32,56,128]{2,1,0:T(8,128)} %bitcast.29), calls=%async_computation | async-start | bytes 1835008 | tf_op jit(solution)/shard_map/all_to_all | solution.py:417
  110.9 2.8 %conditional.2 = (f32[384,4,128]{2,1,0:T(4,128)}, f32[384,4,128]{2,1,0:T(4,128)}) conditional(s32[]{:T(128)} %convert_element_type.42, f32[1,1,1966080]{2,1,0:T(1,128)} %param.12, (f32[1,1,1966080]{2,1,0:T(1,128)}, f32[48,128]{1,0:T(8,128)S(1)}) %tuple.21), branch_computations={%region_0.0_spmd, %region_1.0_spmd} | conditional | flops 786432 | bytes 5520912 | solution.py:383
  110.9 2.7 %slice_bitcast_fusion = (f32[384,4,128]{2,1,0:T(4,128)}, f32[384,4,128]{2,1,0:T(4,128)}) fusion(f32[384,10,4,128]{3,2,1,0:T(4,128)} %bitcast.67), kind=kLoop, calls=%fused_computation | loop fusion | bytes 3145728 | tf_op jit(solution)/shard_map/cond/branch_0_fun/squeeze | solution.py:372
  113.7 1.2 collective-permute-start
  114.9 6.0 %collective-permute-start.1 = (f32[384,4,128]{2,1,0:T(4,128)}, f32[384,4,128]{2,1,0:T(4,128)S(1)}, u32[]{:S(2)}, u32[]{:S(2)}) collective-permute-start(f32[384,4,128]{2,1,0:T(4,128)} %get-tuple-element.21), channel_id=1, source_target_pairs={{1,0},{2,1},{3,2},{4,3},{5,4},{6,5},{7,6},{8,7},{9,8},{10,9},{11,1... | collective-permute-start | bytes 2359304 | tf_op jit(solution)/shard_map/ppermute | solution.py:385
  120.8 0.1 slice_reduce_fusion.1
  121.0 0.4 fusion.4
  121.4 0.0 copy-done.3
  121.4 0.2 slice_reduce_fusion
  121.6 0.1 reshape.193
  121.7 0.4 fusion.5
  122.1 22.4 %collective-permute-done = f32[384,4,128]{2,1,0:T(4,128)S(1)} collective-permute-done((f32[384,4,128]{2,1,0:T(4,128)}, f32[384,4,128]{2,1,0:T(4,128)S(1)}, u32[]{:S(2)}, u32[]{:S(2)}) %collective-permute-start) | collective-permute-done | bytes 786464 | tf_op jit(solution)/shard_map/ppermute | solution.py:384
  144.5 1.2 combine.1
  145.7 5.3 %all-to-all-start.1 = ((f32[4,3,48,128]{3,2,1,0:T(8,128)}), f32[4,3,48,128]{3,2,1,0:T(8,128)S(1)}, u32[]{:S(2)}, u32[]{:S(2)}) async-start(f32[4,3,48,128]{3,2,1,0:T(8,128)} %combine.1), calls=%async_computation.1 | async-start | bytes 589824 | tf_op jit(solution)/shard_map/all_to_all | solution.py:436
  151.0 5.5 %all-to-all-done.1 = f32[4,3,48,128]{3,2,1,0:T(8,128)S(1)} async-done(((f32[4,3,48,128]{3,2,1,0:T(8,128)}), f32[4,3,48,128]{3,2,1,0:T(8,128)S(1)}, u32[]{:S(2)}, u32[]{:S(2)}) %all-to-all-start.1) | async-done | bytes 294944 | tf_op jit(solution)/shard_map/all_to_all | solution.py:436
  156.6 0.1 collective-permute-start.2
  156.6 7.2 %collective-permute-start.3 = (f32[3,4,128]{2,1,0:T(4,128)S(1)}, f32[3,4,128]{2,1,0:T(4,128)S(1)}, u32[]{:S(2)}, u32[]{:S(2)}) collective-permute-start(f32[3,4,128]{2,1,0:T(4,128)S(1)} %get-tuple-element.35), channel_id=1, source_target_pairs={{1,0},{2,1},{3,2},{4,3},{5,4},{6,5},{7,6},{8,7},{9,8},{10,9},{11,1... | collective-permute-start | bytes 18440 | tf_op jit(solution)/shard_map/ppermute | solution.py:441
  163.8 50.2 %dynamics.1.part_ref = f32[15360,128]{1,0:T(8,128)S(1)} custom-call(s32[1]{0:T(128)} %bitcast.11.sea_ref, f32[15360,128]{1,0:T(8,128)} %bitcast.66, f32[1536,128]{1,0:T(8,128)S(1)} %bitcast.64, f32[1536,128]{1,0:T(8,128)S(1)} %bitcast.65, f32[3,128,128]{2,1,0:T(8,128)S(1)} %copy-done.3, f32[4,80,80]{2,1,0:T(8,128)S(1)} %copy-done.4, ...), custom_call_target="tpu_custom_call" | custom-call | flops 2013265920 | bytes 47185920 | tf_op jit(solution)/shard_map/dynamics/pallas_call | solution.py:249
  214.1 0.0 copy-start
  214.1 3.2 %copy-done = f32[15360,128]{1,0:T(8,128)} copy-done((f32[15360,128]{1,0:T(8,128)}, f32[15360,128]{1,0:T(8,128)S(1)}, u32[]{:S(2)}) %copy-start) | copy-done | bytes 7864344
  217.4 3.2 %copy-done.1 = f32[15360,128]{1,0:T(8,128)S(1)} copy-done((f32[15360,128]{1,0:T(8,128)S(1)}, f32[15360,128]{1,0:T(8,128)}, u32[]{:S(2)}) %copy-start.1) | copy-done | bytes 7864344
  220.6 4.2 %update.1 = f32[15360,128]{1,0:T(8,128)} custom-call(s32[1]{0:T(128)} %bitcast.11.sea_ref, f32[384]{0:T(512)S(1)} %bitcast_select_fusion.column_ref, f32[15360,128]{1,0:T(8,128)S(1)} %copy-done.1, f32[3,48,128]{2,1,0:T(8,128)S(1)} %broadcast_multiply_fusion.forcing_ref, f32[2,3,4,128]{3,2,1,0:T(4,128)S(1)} %pad_maximum_fusion.1.halo_ref, ...), custom_call_target="tpu_custom_call" | custom-call | flops 3932160 | bytes 15728640 | tf_op jit(solution)/shard_map/update/pallas_call | solution.py:330
  (36 shorter events, 0.3 us)
Async XLA Ops:
  90.6 20.2 %copy-start.5 = (s32[1,1,48,128]{3,2,1,0:T(8,128)S(1)}, s32[1,1,48,128]{3,2,1,0:T(8,128)}, u32[]{:S(2)}) copy-start(s32[1,1,48,128]{3,2,1,0:T(8,128)} %param.15) | copy-start | bytes 73732
  90.8 3.4 %copy-start.2 = (bf16[1,1,256,128,128]{4,3,2,1,0:T(8,128)(2,1)S(1)}, bf16[1,1,256,128,128]{4,3,2,1,0:T(8,128)(2,1)}, u32[]{:S(2)}) copy-start(bf16[1,1,256,128,128]{4,3,2,1,0:T(8,128)(2,1)} %param.19) | copy-start | bytes 25165828
  99.4 21.5 %copy-start.4 = (f32[4,80,80]{2,1,0:T(8,128)S(1)}, f32[4,80,80]{2,1,0:T(8,128)}, u32[]{:S(2)}) copy-start(f32[4,80,80]{2,1,0:T(8,128)} %ocean_ref.1) | copy-start | bytes 307204
  99.4 22.0 %copy-start.3 = (f32[3,128,128]{2,1,0:T(8,128)S(1)}, f32[3,128,128]{2,1,0:T(8,128)}, u32[]{:S(2)}) copy-start(f32[3,128,128]{2,1,0:T(8,128)} %atm_ref.1) | copy-start | bytes 589828
  99.4 45.1 %all-to-all-start = ((f32[32,56,128]{2,1,0:T(8,128)}), f32[32,56,128]{2,1,0:T(8,128)S(1)}, u32[]{:S(2)}, u32[]{:S(2)}) async-start(f32[32,56,128]{2,1,0:T(8,128)} %bitcast.29), calls=%async_computation | async-start | bytes 1835008 | tf_op jit(solution)/shard_map/all_to_all | solution.py:417
  113.7 30.8 %collective-permute-start = (f32[384,4,128]{2,1,0:T(4,128)}, f32[384,4,128]{2,1,0:T(4,128)S(1)}, u32[]{:S(2)}, u32[]{:S(2)}) collective-permute-start(f32[384,4,128]{2,1,0:T(4,128)} %get-tuple-element.20), channel_id=1, source_target_pairs={{0,1},{1,2},{2,3},{3,4},{4,5},{5,6},{6,7},{7,8},{8,9},{9,10},{10,1... | collective-permute-start | bytes 2359304 | tf_op jit(solution)/shard_map/ppermute | solution.py:384
  114.9 29.6 %collective-permute-start.1 = (f32[384,4,128]{2,1,0:T(4,128)}, f32[384,4,128]{2,1,0:T(4,128)S(1)}, u32[]{:S(2)}, u32[]{:S(2)}) collective-permute-start(f32[384,4,128]{2,1,0:T(4,128)} %get-tuple-element.21), channel_id=1, source_target_pairs={{1,0},{2,1},{3,2},{4,3},{5,4},{6,5},{7,6},{8,7},{9,8},{10,9},{11,1... | collective-permute-start | bytes 2359304 | tf_op jit(solution)/shard_map/ppermute | solution.py:385
  145.7 10.8 %all-to-all-start.1 = ((f32[4,3,48,128]{3,2,1,0:T(8,128)}), f32[4,3,48,128]{3,2,1,0:T(8,128)S(1)}, u32[]{:S(2)}, u32[]{:S(2)}) async-start(f32[4,3,48,128]{3,2,1,0:T(8,128)} %combine.1), calls=%async_computation.1 | async-start | bytes 589824 | tf_op jit(solution)/shard_map/all_to_all | solution.py:436
  156.6 60.8 %collective-permute-start.2 = (f32[3,4,128]{2,1,0:T(4,128)S(1)}, f32[3,4,128]{2,1,0:T(4,128)S(1)}, u32[]{:S(2)}, u32[]{:S(2)}) collective-permute-start(f32[3,4,128]{2,1,0:T(4,128)S(1)} %get-tuple-element.34), channel_id=1, source_target_pairs={{0,1},{1,2},{2,3},{3,4},{4,5},{5,6},{6,7},{7,8},{8,9},{9,10},{10,1... | collective-permute-start | bytes 18440 | tf_op jit(solution)/shard_map/ppermute | solution.py:441
  156.6 60.7 %collective-permute-start.3 = (f32[3,4,128]{2,1,0:T(4,128)S(1)}, f32[3,4,128]{2,1,0:T(4,128)S(1)}, u32[]{:S(2)}, u32[]{:S(2)}) collective-permute-start(f32[3,4,128]{2,1,0:T(4,128)S(1)} %get-tuple-element.35), channel_id=1, source_target_pairs={{1,0},{2,1},{3,2},{4,3},{5,4},{6,5},{7,6},{8,7},{9,8},{10,9},{11,1... | collective-permute-start | bytes 18440 | tf_op jit(solution)/shard_map/ppermute | solution.py:441
  214.1 3.2 %copy-start = (f32[15360,128]{1,0:T(8,128)}, f32[15360,128]{1,0:T(8,128)S(1)}, u32[]{:S(2)}) copy-start(f32[15360,128]{1,0:T(8,128)S(1)} %dynamics.1.part_ref) | copy-start | bytes 23592964
  217.4 3.2 %copy-start.1 = (f32[15360,128]{1,0:T(8,128)S(1)}, f32[15360,128]{1,0:T(8,128)}, u32[]{:S(2)}) copy-start(f32[15360,128]{1,0:T(8,128)} %copy-done) | copy-start | bytes 23592964

commit v2 on v1

v2 whole, which is shorter than its diff:
```python
import functools

import jax
import jax.numpy as jnp
import numpy as np
from jax import lax
from jax.experimental import pallas as pl
from jax.experimental.pallas import tpu as pltpu
from jax.sharding import PartitionSpec as P

FA = 3
FO = 4
LA = 128
LO = 80
R = 128
CAP = 16

COUPLE_RATE = 0.1
NU_ATMOS = 0.02
NU_OCEAN = 0.015

HALO = 4
CHUNK_ROWS = 56
MIB = 1 << 20


def split_two(value):
    high = value.astype(jnp.bfloat16)
    return high, (value - high.astype(jnp.float32)).astype(jnp.bfloat16)


def row_operator():
    u = np.eye(R, k=1) + np.eye(R, k=-1) - 4.0 * np.eye(R)
    both = np.concatenate([2.0 * u, u @ u + 2.0 * np.eye(R)], axis=1)
    return jnp.asarray(np.concatenate([both, both], axis=0), jnp.bfloat16)


def apply_filter(value, column_sums, row_parts, nu):
    return value - nu * (column_sums + row_parts)


def filter_planes(column, spans, nu, mask, operator, lhs_ref, emit):
    rows = 16
    places = {}
    for first, last in spans:
        for k in range(first - 1, last + 1):
            spot = places[first, k] = len(places) * rows
            high, low = split_two(column(k))
            lhs_ref[spot : spot + rows, :R] = high
            lhs_ref[spot : spot + rows, R:] = low
    both = jnp.dot(lhs_ref[: len(places) * rows], operator, preferred_element_type=jnp.float32)

    def part(place, half):
        spot = places[place]
        return both[spot : spot + rows, half * R : (half + 1) * R]

    for first, last in spans:
        for k in range(first, last):
            column_sums = column(k - 2) + column(k + 2)
            row_parts = (part((first, k - 1), 0) + part((first, k + 1), 0)) + part((first, k), 1)
            plane = apply_filter(column(k), column_sums, row_parts, nu)
            if mask is not None:
                plane = plane * mask(k)
            emit(k, plane)


def stacked_square(matrix):
    squared = jnp.dot(
        matrix, matrix, precision=lax.Precision.HIGHEST, preferred_element_type=jnp.float32
    )
    high, low = split_two(squared)
    return jnp.concatenate(
        [
            jnp.concatenate([high, high], axis=1),
            jnp.concatenate([low, jnp.zeros_like(low)], axis=1),
        ],
        axis=0,
    )


def surface_copies(sizes, sea, x_ref, surf_ref, sems):
    atm_cols, sea_cols = sizes
    if sea:
        cols, starts = sea_cols, [f * LO * sea_cols for f in range(FA)]
    else:
        cols, starts = atm_cols, [(f * LA + LA - 1) * atm_cols for f in range(FA)]
    return [
        pltpu.make_async_copy(
            x_ref.at[pl.ds(start, cols)], surf_ref.at[pl.ds(f * sea_cols, cols)], sems.at[f]
        )
        for f, start in enumerate(starts)
    ]


def small_mod(value, modulus, limit):
    for step in range(modulus, limit, modulus):
        value = jnp.where(value >= modulus, value - modulus, value)
    return value


def as_column(row):
    n = row.shape[1]
    diagonal = lax.broadcasted_iota(jnp.int32, (n, n), 0) == lax.broadcasted_iota(jnp.int32, (n, n), 1)
    return jnp.sum(jnp.where(diagonal, row, 0.0), axis=1, keepdims=True)


def ones_where(condition):
    return jnp.where(condition, 1.0, 0.0).astype(jnp.bfloat16)


def remap_kernel(
    sizes, n_tile, chunks, place_ref, source_ref, tile_ref, slot_ref, x_ref, w_ref, out_ref, w_vmem, surf_ref, pick_ref, part_ref, w_sems, x_sems
):
    atm_cols, sea_cols = sizes
    entries = source_ref.shape[1]
    quarter = entries // 4
    per_chunk = quarter // chunks
    code_limit = 5 * sea_cols
    copies = [
        pltpu.make_async_copy(
            w_ref.at[:, pl.ds(n * per_chunk, per_chunk)], w_vmem.at[:, pl.ds(n * per_chunk, per_chunk)], w_sems.at[n]
        )
        for n in range(chunks)
    ]
    is_sea = place_ref[0] != 0
    for sea in (False, True):

        @pl.when(is_sea == sea)
        def _(sea=sea):
            for copy in surface_copies(sizes, sea, x_ref, surf_ref, x_sems):
                copy.start()

    for copy in copies:
        copy.start()

    tile = tile_ref[...].astype(jnp.float32)
    tile_column = as_column(tile)
    earlier = lax.broadcasted_iota(jnp.int32, (entries, entries), 0) < lax.broadcasted_iota(
        jnp.int32, (entries, entries), 1
    )
    rank = jnp.sum(jnp.where((tile_column == tile) & earlier, 1.0, 0.0), axis=0, keepdims=True)
    code = slot_ref[...]
    for_atm = small_mod(code, 3 * atm_cols, code_limit)
    for_atm_block = small_mod(for_atm, atm_cols, 3 * atm_cols)
    for_atm_group = jnp.where(for_atm >= atm_cols, 1, 0) + jnp.where(for_atm >= 2 * atm_cols, 1, 0)
    for_sea = 3 * sea_cols + small_mod(code, sea_cols, code_limit)
    dest = jnp.where(is_sea, for_atm_group * sea_cols + for_atm_block, for_sea)
    dest = (dest + 1).astype(jnp.float32)
    lane = rank + (CAP * lax.rem(place_ref[1], R // CAP)).astype(jnp.float32)
    spots = lax.broadcasted_iota(jnp.int32, (R, entries), 0).astype(jnp.float32)
    marks = jnp.where(spots == lane, dest, 0.0).astype(jnp.bfloat16)
    tiles = lax.broadcasted_iota(jnp.int32, (n_tile, entries), 0).astype(jnp.float32)
    codes = lax.dot_general(
        ones_where(tiles == tile), marks, (((1,), (1,)), ((), ())), preferred_element_type=jnp.float32
    )
    tail = CHUNK_ROWS - FA * CAP
    for t in range(n_tile):
        out_ref[t, FA * CAP :, :] = jnp.concatenate(
            [codes[t : t + 1], jnp.zeros((tail - 1, R), jnp.float32)], axis=0
        )

    source = source_ref[...]
    source = jnp.where(
        is_sea, small_mod(source, sea_cols, code_limit), small_mod(source, atm_cols, code_limit)
    )
    source_column = as_column(source.astype(jnp.float32))
    columns = lax.broadcasted_iota(jnp.int32, (entries, sea_cols), 1).astype(jnp.float32)
    chooser = ones_where(columns == source_column)
    for sea in (False, True):

        @pl.when(is_sea == sea)
        def _(sea=sea):
            for copy in surface_copies(sizes, sea, x_ref, surf_ref, x_sems):
                copy.wait()
            if not sea:
                for f in range(FA):
                    surf_ref[f * sea_cols + atm_cols : (f + 1) * sea_cols, :] = jnp.zeros(
                        (sea_cols - atm_cols, R), jnp.float32
                    )

    for f in range(FA):
        surface = surf_ref[f * sea_cols : (f + 1) * sea_cols, :].astype(jnp.bfloat16)
        pick_ref[f * entries : (f + 1) * entries, :] = jnp.dot(
            chooser, surface, preferred_element_type=jnp.float32
        )
    pick_ref[FA * entries :, :] = jnp.zeros((entries, R), jnp.float32)

    member = lax.rem(lax.broadcasted_iota(jnp.int32, (16, R), 0), 4)
    for n in range(chunks):
        copies[n].wait()
        for g in range(n * per_chunk, (n + 1) * per_chunk):
            picked = pick_ref[pl.ds(g, 16, stride=quarter), :]
            rows = jnp.concatenate(
                [jnp.where(member < 2, picked, 0.0), jnp.where(member >= 2, picked, 0.0)], axis=1
            ).astype(jnp.bfloat16)
            block = jnp.concatenate(
                [
                    jnp.concatenate([w_vmem[0, g], w_vmem[2, g]], axis=1),
                    jnp.concatenate([w_vmem[1, g], w_vmem[3, g]], axis=1),
                ],
                axis=0,
            )
            res = lax.dot_general(
                rows, block, (((1,), (1,)), ((), ())), preferred_element_type=jnp.float32
            )
            part_ref[pl.ds(g, 16, stride=quarter), :] = jnp.where(member % 2 == 0, res[:, :R], res[:, R:])

    slot = tile * CAP + rank
    slots = lax.broadcasted_iota(jnp.int32, (n_tile * CAP, entries), 0).astype(jnp.float32)
    placer = ones_where(slots == slot)
    for f in range(FA):
        high, low = split_two(part_ref[f * entries : (f + 1) * entries, :])
        both = jnp.dot(placer, jnp.concatenate([high, low], axis=1), preferred_element_type=jnp.float32)
        placed = both[:, :R] + both[:, R:]
        for t in range(n_tile):
            out_ref[t, f * CAP : (f + 1) * CAP, :] = placed[t * CAP : (t + 1) * CAP]


def remap(place, source, tile, slot, x, weights, n_tile, sizes):
    entries = weights.shape[0]
    chunks = 8
    vmem = pl.BlockSpec(memory_space=pltpu.VMEM)
    anywhere = pl.BlockSpec(memory_space=pl.ANY)
    return pl.pallas_call(
        functools.partial(remap_kernel, sizes, n_tile, chunks),
        out_shape=jax.ShapeDtypeStruct((n_tile, CHUNK_ROWS, R), jnp.float32),
        in_specs=[pl.BlockSpec(memory_space=pltpu.SMEM), vmem, vmem, vmem, anywhere, anywhere],
        out_specs=vmem,
        scratch_shapes=[
            pltpu.VMEM((4, entries // 4, R, R), jnp.bfloat16),
            pltpu.VMEM((FA * sizes[1], R), jnp.float32),
            pltpu.VMEM((4 * entries, R), jnp.float32),
            pltpu.VMEM((4 * entries, R), jnp.float32),
            pltpu.SemaphoreType.DMA((chunks,)),
            pltpu.SemaphoreType.DMA((FA,)),
        ],
        compiler_params=pltpu.CompilerParams(vmem_limit_bytes=56 * MIB),
        cost_estimate=pl.CostEstimate(
            flops=2 * entries * R * R * 16, bytes_accessed=weights.size * 2, transcendentals=0
        ),
        name="remap",
    )(place, source, tile, slot, x, weights.reshape(4, entries // 4, R, R))


def combine_kernel(rows, recv_ref, out_ref):
    n_tile = recv_ref.shape[0]
    spots = lax.broadcasted_iota(jnp.int32, (rows, R), 0).astype(jnp.float32) + 1.0
    total = [jnp.zeros((rows, R), jnp.float32) for _ in range(FA)]
    for g in range(n_tile // 8):
        code = jnp.sum(recv_ref[g * 8 : (g + 1) * 8, 3 * CAP, :], axis=0, keepdims=True)
        pick = jnp.where(spots == code, 1.0, 0.0).astype(jnp.bfloat16)
        for f in range(FA):
            value = recv_ref[g * 8 : (g + 1) * 8, f * CAP : (f + 1) * CAP, :].reshape(8 * CAP, R)
            high = value.astype(jnp.bfloat16)
            rest = value - high.astype(jnp.float32)
            middle = rest.astype(jnp.bfloat16)
            both = jnp.dot(
                pick,
                jnp.concatenate([high, middle], axis=1),
                preferred_element_type=jnp.float32,
            )
            total[f] = total[f] + (both[:, :R] + both[:, R:])
    per_group = rows // 4
    for f in range(FA):
        for c in range(4):
            out_ref[c, f] = total[f][c * per_group : (c + 1) * per_group]


def combine(recv, sea_cols):
    return pl.pallas_call(
        functools.partial(combine_kernel, 4 * sea_cols),
        out_shape=jax.ShapeDtypeStruct((4, FA, sea_cols, R), jnp.float32),
        compiler_params=pltpu.CompilerParams(vmem_limit_bytes=32 * MIB),
        name="combine",
    )(recv)


def filtered_twice(levels, cols, inner, outer, nu, column, mask, operator, lhs_ref, mid_ref, store):
    order = {k: n for n, k in enumerate(k for first, last in inner for k in range(first, last))}

    def middle(k):
        return mid_ref[order[k] * 16 : (order[k] + 1) * 16, :]

    def keep(k, plane):
        mid_ref[order[k] * 16 : (order[k] + 1) * 16, :] = plane

    filter_planes(column, inner, nu, mask, operator, lhs_ref.at[0], keep)
    filter_planes(middle, outer, nu, mask, operator, lhs_ref.at[1], store)


def mixed_planes(stacked, y_vmem, levels, pair):
    both = jnp.dot(
        stacked,
        y_vmem[: 2 * levels, 2 * pair * R : 2 * (pair + 1) * R],
        preferred_element_type=jnp.float32,
    )
    return both[:levels] + both[levels:]


def plane_store(y_vmem, levels, i, first_plane):
    spot = pl.multiple_of(i * 16, 16)

    def store(k, plane):
        high, low = split_two(plane)
        lanes = slice((k - first_plane) * R, (k - first_plane + 1) * R)
        y_vmem[pl.ds(spot, 16), lanes] = high
        y_vmem[pl.ds(levels + spot, 16), lanes] = low

    return store


def inner_part(
    fields, levels, cols, nu, x_ref, matrix_ref, mask_ref, op_ref, out_ref, x_vmem, y_vmem, lhs_ref, mid_ref, out_vmem, in_sems, out_sems
):
    rows_per_field = levels * cols
    spans = [pl.ds(f * rows_per_field, rows_per_field) for f in range(fields)]
    reads = [pltpu.make_async_copy(x_ref.at[s], x_vmem.at[s], in_sems.at[f]) for f, s in enumerate(spans)]
    writes = [pltpu.make_async_copy(out_vmem.at[s], out_ref.at[s], out_sems.at[f]) for f, s in enumerate(spans)]
    for read in reads:
        read.start()
    mask = None
    if mask_ref is not None:
        mask = lambda k: jnp.broadcast_to(mask_ref[k : k + 1, :], (16, R))
    for f in range(fields):
        stacked = stacked_square(matrix_ref[f])
        reads[f].wait()

        def filter_rows(i, carry, f=f):
            first = f * levels + i * 16
            column = lambda k: x_vmem[pl.ds(first * cols + k, 16, stride=cols), :]
            filtered_twice(
                levels, cols, [(2, cols - 2)], [(HALO, cols - HALO)], nu, column, mask, op_ref[...], lhs_ref, mid_ref,
                plane_store(y_vmem, levels, i, HALO),
            )
            return carry

        lax.fori_loop(0, levels // 16, filter_rows, 0)

        for pair in range((cols - 2 * HALO) // 2):
            mixed = mixed_planes(stacked, y_vmem, levels, pair)
            for h in range(2):
                k = HALO + 2 * pair + h
                out_vmem[pl.ds(f * rows_per_field + k, levels, stride=cols), :] = mixed[:, h * R : (h + 1) * R]
        writes[f].start()
    for write in writes:
        write.wait()


def inner_kernel(sizes, sea_ref, x_ref, atm_ref, ocean_ref, mask_ref, op_ref, out_ref, *scratch):
    atm_cols, sea_cols = sizes

    @pl.when(sea_ref[0] == 0)
    def _():
        inner_part(FA, LA, atm_cols, NU_ATMOS, x_ref, atm_ref, None, op_ref, out_ref, *scratch)

    @pl.when(sea_ref[0] != 0)
    def _():
        inner_part(FO, LO, sea_cols, NU_OCEAN, x_ref, ocean_ref, mask_ref, op_ref, out_ref, *scratch)


def inner_dynamics(is_sea, x, atm_mixing, ocean_mixing, mask, sizes):
    vmem = pl.BlockSpec(memory_space=pltpu.VMEM)
    anywhere = pl.BlockSpec(memory_space=pl.ANY)
    rows = x.shape[0]
    widest = max(sizes)
    return pl.pallas_call(
        functools.partial(inner_kernel, sizes),
        out_shape=jax.ShapeDtypeStruct((rows, R), jnp.float32),
        in_specs=[pl.BlockSpec(memory_space=pltpu.SMEM), anywhere] + [vmem] * 4,
        out_specs=anywhere,
        scratch_shapes=[
            pltpu.VMEM((rows, R), jnp.float32),
            pltpu.VMEM((2 * LA, (widest - 2 * HALO) * R), jnp.bfloat16),
            pltpu.VMEM((2, widest * 16, 2 * R), jnp.bfloat16),
            pltpu.VMEM((widest * 16, R), jnp.float32),
            pltpu.VMEM((rows, R), jnp.float32),
            pltpu.SemaphoreType.DMA((FO,)),
            pltpu.SemaphoreType.DMA((FO,)),
        ],
        compiler_params=pltpu.CompilerParams(vmem_limit_bytes=56 * MIB),
        cost_estimate=pl.CostEstimate(
            flops=2 * rows * R * R, bytes_accessed=2 * rows * R, transcendentals=0
        ),
        name="inner_dynamics",
    )(is_sea, x, atm_mixing, ocean_mixing, mask, row_operator())


def rim_part(
    fields, levels, cols, nu, x_ref, left_ref, right_ref, matrix_ref, mask_ref, op_ref, out_ref, low_vmem, high_vmem, y_vmem, lhs_ref, mid_ref, sems
):
    count, count_all = fields * levels, low_vmem.shape[0]
    copies = [
        pltpu.make_async_copy(x_ref.at[:, pl.ds(start, 8), :], vmem.at[pl.ds(0, count)], sems.at[n])
        for n, (start, vmem) in enumerate(((0, low_vmem), (cols - 8, high_vmem)))
    ]
    for copy in copies:
        copy.start()
    mask = None
    if mask_ref is not None:
        mask = lambda k: jnp.broadcast_to(mask_ref[k + HALO : k + HALO + 1, :], (16, R))
    for copy in copies:
        copy.wait()
    low_vmem, high_vmem = (v.reshape(count_all * 8, R) for v in (low_vmem, high_vmem))
    for f in range(fields):
        stacked = stacked_square(matrix_ref[f])

        def filter_rows(i, carry, f=f):
            first = pl.multiple_of(f * levels + i * 16, 16)

            def column(k):
                if k < 0:
                    return left_ref[pl.ds(first * HALO + k + HALO, 16, stride=HALO), :]
                if k < 8:
                    return low_vmem[pl.ds(first * 8 + k, 16, stride=8), :]
                if k < cols:
                    return high_vmem[pl.ds(first * 8 + k - (cols - 8), 16, stride=8), :]
                return right_ref[pl.ds(first * HALO + k - cols, 16, stride=HALO), :]

            store = plane_store(y_vmem, levels, i, 0)
            filtered_twice(
                levels, cols, [(-2, 6), (cols - 6, cols + 2)], [(0, HALO), (cols - HALO, cols)], nu, column, mask,
                op_ref[...], lhs_ref, mid_ref, lambda k, plane: store(k if k < HALO else k - cols + 2 * HALO, plane),
            )
            return carry

        lax.fori_loop(0, levels // 16, filter_rows, 0)
        for pair in range(HALO):
            mixed = mixed_planes(stacked, y_vmem, levels, pair)
            for h in range(2):
                out_ref[pl.ds(f * levels * 8 + 2 * pair + h, levels, stride=8), :] = mixed[:, h * R : (h + 1) * R]


def rim_kernel(
    sizes, sea_ref, x_atm_ref, x_sea_ref, left_ref, right_ref, atm_ref, ocean_ref, mask_ref, op_ref, out_ref, *scratch
):
    atm_cols, sea_cols = sizes

    @pl.when(sea_ref[0] == 0)
    def _():
        rim_part(
            FA, LA, atm_cols, NU_ATMOS, x_atm_ref, left_ref, right_ref, atm_ref, None, op_ref, out_ref, *scratch
        )

    @pl.when(sea_ref[0] != 0)
    def _():
        rim_part(
            FO, LO, sea_cols, NU_OCEAN, x_sea_ref, left_ref, right_ref, ocean_ref, mask_ref, op_ref, out_ref, *scratch
        )


def rim_dynamics(is_sea, x_atm, x_sea, left, right, atm_mixing, ocean_mixing, mask, sizes):
    vmem = pl.BlockSpec(memory_space=pltpu.VMEM)
    anywhere = pl.BlockSpec(memory_space=pl.ANY)
    count = x_atm.shape[0]
    return pl.pallas_call(
        functools.partial(rim_kernel, sizes),
        out_shape=jax.ShapeDtypeStruct((count * 8, R), jnp.float32),
        in_specs=[pl.BlockSpec(memory_space=pltpu.SMEM), anywhere, anywhere] + [vmem] * 6,
        out_specs=vmem,
        scratch_shapes=[
            pltpu.VMEM((count, 8, R), jnp.float32),
            pltpu.VMEM((count, 8, R), jnp.float32),
            pltpu.VMEM((2 * LA, 8 * R), jnp.bfloat16),
            pltpu.VMEM((2, 20 * 16, 2 * R), jnp.bfloat16),
            pltpu.VMEM((16 * 16, R), jnp.float32),
            pltpu.SemaphoreType.DMA((2,)),
        ],
        compiler_params=pltpu.CompilerParams(vmem_limit_bytes=16 * MIB),
        cost_estimate=pl.CostEstimate(
            flops=20 * count * 40 * R * R, bytes_accessed=count * 24 * R * 4, transcendentals=0
        ),
        name="rim_dynamics",
    )(is_sea, x_atm, x_sea, left, right, atm_mixing, ocean_mixing, mask, row_operator())


def lane_edges(rows):
    lane = lax.broadcasted_iota(jnp.int32, (rows, R), 1)
    return lane == 0, lane == R - 1


def lap(before, middle, after, edges):
    first, last = edges
    down = jnp.where(first, 0.0, pltpu.roll(middle, 1, 1))
    up = jnp.where(last, 0.0, pltpu.roll(middle, R - 1, 1))
    return (before + after) + (down + up) - 4.0 * middle


def filter_forcing(cols, nu, forcing_ref, halo_ref, mask_ref, work_ref, g_ref):
    lo, hi = 8, 8 + cols
    first, last = lane_edges(cols + 16)
    lane_edge = (first, last)
    for f in range(FA):
        work_ref[0 : cols + 16, :] = jnp.zeros((cols + 16, R), jnp.float32)
        work_ref[lo - HALO : lo, :] = halo_ref[0, f]
        work_ref[lo:hi, :] = forcing_ref[f, :cols]
        work_ref[hi : hi + HALO, :] = halo_ref[1, f]
        value = work_ref[0 : cols + 16, :]

        def along(v):
            return lap(pltpu.roll(v, 1, 0), v, pltpu.roll(v, cols + 15, 0), lane_edge)

        value = value - nu * along(along(value))
        if mask_ref is not None:
            value = value * mask_ref[0 : cols + 16, :]
        value = value - nu * along(along(value))
        if mask_ref is not None:
            value = value * mask_ref[0 : cols + 16, :]
        g_ref[f, :cols] = value[lo:hi]


def update_part(cols, levels, pieces, nu, column_ref, part_ref, rim_ref, forcing_ref, halo_ref, mask_ref, out_ref, work_ref, g_ref, stage_ref, in_sems, out_sems):
    rows = part_ref.shape[0] // pieces
    spans = [pl.ds(p * rows, rows) for p in range(pieces)]
    reads = [pltpu.make_async_copy(part_ref.at[s], stage_ref.at[s], in_sems.at[p]) for p, s in enumerate(spans)]
    writes = [pltpu.make_async_copy(stage_ref.at[s], out_ref.at[s], out_sems.at[p]) for p, s in enumerate(spans)]
    for read in reads:
        read.start()
    filter_forcing(cols, nu, forcing_ref, halo_ref, mask_ref, work_ref, g_ref)
    upper = lax.broadcasted_iota(jnp.int32, (8, R), 0) < HALO
    for p in range(pieces):
        reads[p].wait()
        for number in range(p * rows // cols, (p + 1) * rows // cols):
            f = number // levels
            rim = rim_ref[number * 8 : (number + 1) * 8, :]
            for v in range(cols // 8):
                span = slice(number * cols + v * 8, number * cols + v * 8 + 8)
                if f >= FA and 0 < v < cols // 8 - 1:
                    continue
                value = stage_ref[span, :]
                if v == 0:
                    value = jnp.where(upper, rim, value)
                if v == cols // 8 - 1:
                    value = jnp.where(upper, value, rim)
                if f < FA:
                    value = value + column_ref[number] * g_ref[f, v * 8 : v * 8 + 8, :]
                stage_ref[span, :] = value
        writes[p].start()
    for write in writes:
        write.wait()


def update_kernel(
    sizes, pieces, sea_ref, column_ref, part_ref, rim_ref, forcing_ref, halo_ref, mask_ref, *rest
):
    atm_cols, sea_cols = sizes

    @pl.when(sea_ref[0] == 0)
    def _():
        update_part(
            atm_cols, LA, pieces, NU_ATMOS, column_ref, part_ref, rim_ref, forcing_ref, halo_ref, None, *rest
        )

    @pl.when(sea_ref[0] != 0)
    def _():
        update_part(
            sea_cols, LO, pieces, NU_OCEAN, column_ref, part_ref, rim_ref, forcing_ref, halo_ref, mask_ref, *rest
        )


def update(is_sea, column, part, rim, forcing, halo, mask, sizes):
    vmem = pl.BlockSpec(memory_space=pltpu.VMEM)
    smem = pl.BlockSpec(memory_space=pltpu.SMEM)
    anywhere = pl.BlockSpec(memory_space=pl.ANY)
    rows = part.shape[0]
    pieces = 8
    return pl.pallas_call(
        functools.partial(update_kernel, sizes, pieces),
        out_shape=jax.ShapeDtypeStruct((rows, R), jnp.float32),
        in_specs=[smem, smem, anywhere, vmem, vmem, vmem, vmem],
        out_specs=anywhere,
        scratch_shapes=[
            pltpu.VMEM((max(sizes) + 16, R), jnp.float32),
            pltpu.VMEM((FA, max(sizes), R), jnp.float32),
            pltpu.VMEM((rows, R), jnp.float32),
            pltpu.SemaphoreType.DMA((pieces,)),
            pltpu.SemaphoreType.DMA((pieces,)),
        ],
        compiler_params=pltpu.CompilerParams(vmem_limit_bytes=56 * MIB),
        cost_estimate=pl.CostEstimate(
            flops=2 * rows * R, bytes_accessed=8 * rows * R, transcendentals=0
        ),
        name="update",
    )(is_sea, column, part, rim, forcing, halo, mask)


def local(
    fields, atm_mixing, ocean_mixing, sea_mask, source_slot, target_tile, target_slot, remap_blocks
):
    n_comp = lax.axis_size("comp")
    n_tile = lax.axis_size("tile")
    is_sea = lax.axis_index("comp") == n_comp - 1
    sea_cols = sea_mask.shape[2]
    atm_cols = sea_cols * 5 // 6
    sizes = (atm_cols, sea_cols)
    sea_flag = is_sea.astype(jnp.int32).reshape(1)
    mask = sea_mask[0, 0].astype(jnp.float32)
    state = fields[0, 0]
    tiles = target_tile[0, 0, :, 0]
    weights = remap_blocks[0, 0]
    forward = [(i, (i + 1) % n_tile) for i in range(n_tile)]
    backward = [(b, a) for a, b in forward]

    def atm_edges(values):
        split = values.reshape(FA * LA, atm_cols // HALO, HALO, R)
        return split[:, 0], split[:, -1]

    def sea_edges(values):
        split = values.reshape(FO * LO, sea_cols // HALO, HALO, R)
        spare = FA * LA - FO * LO
        cut = mask.reshape(sea_cols // HALO, HALO, R)
        fill = lambda edge, own: jnp.concatenate(
            [edge, own[None], jnp.zeros((spare - 1, HALO, R), jnp.float32)], axis=0
        )
        return fill(split[:, 0], cut[0]), fill(split[:, -1], cut[-1])

    low_edge, high_edge = lax.cond(is_sea, sea_edges, atm_edges, state)
    low_edge, high_edge, tiles = lax.optimization_barrier((low_edge, high_edge, tiles))
    left = lax.ppermute(high_edge, "tile", forward)
    right = lax.ppermute(low_edge, "tile", backward)

    place = jnp.stack([is_sea.astype(jnp.int32), lax.axis_index("tile")])
    sent = remap(
        place,
        source_slot.reshape(1, -1),
        tiles.reshape(1, -1),
        target_slot.reshape(1, -1),
        state.reshape(-1, R),
        weights,
        n_tile,
        sizes,
    )
    received = lax.all_to_all(
        sent, "tile", split_axis=0, concat_axis=0, tiled=True
    )

    part = inner_dynamics(sea_flag, state.reshape(-1, R), atm_mixing, ocean_mixing, mask, sizes)
    mask_left, mask_right = left[FO * LO], right[FO * LO]
    work_mask = jnp.concatenate(
        [jnp.zeros((4, R), jnp.float32), mask_left, mask, mask_right, jnp.zeros((4, R), jnp.float32)], axis=0
    )
    rim = rim_dynamics(
        sea_flag,
        state.reshape(FA * LA, atm_cols, R),
        state.reshape(FO * LO, sea_cols, R),
        left.reshape(FA * LA * HALO, R),
        right.reshape(FA * LA * HALO, R),
        atm_mixing,
        ocean_mixing,
        work_mask[HALO:-HALO],
        sizes,
    )

    received, part = lax.optimization_barrier((received, part))
    shares = lax.all_to_all(combine(received, sea_cols), "comp", split_axis=0, concat_axis=0, tiled=True)
    pushed = COUPLE_RATE * jnp.sum(shares, axis=0) * mask
    low_part = pushed[:, :HALO]
    high_part = jnp.where(is_sea, pushed[:, sea_cols - HALO :], pushed[:, atm_cols - HALO : atm_cols])
    halo = jnp.stack(
        [lax.ppermute(high_part, "tile", forward), lax.ppermute(low_part, "tile", backward)]
    )
    atm_column = jnp.einsum(
        "flm,fm->fl", atm_mixing, atm_mixing[:, :, LA - 1], precision=lax.Precision.HIGHEST
    ).reshape(-1)
    ocean_column = jnp.einsum(
        "flm,fm->fl", ocean_mixing, ocean_mixing[:, :, 0], precision=lax.Precision.HIGHEST
    ).reshape(-1)
    ocean_column = jnp.pad(ocean_column, (0, FA * LA - FO * LO))
    column = jnp.where(is_sea, ocean_column, atm_column)
    done = update(sea_flag, column, part, rim, pushed, halo, work_mask, sizes)
    return done.reshape(1, 1, -1)


def solution(mesh):
    in_specs = (
        P("comp", "tile", None),
        P(),
        P(),
        P("comp", "tile", None, None),
        P("comp", "tile", None),
        P("comp", "tile", None, None),
        P("comp", "tile", None),
        P("comp", "tile", None, None, None),
    )
    out_specs = P("comp", "tile", None)
    return jax.shard_map(local, mesh=mesh, in_specs=in_specs, out_specs=out_specs, check_vma=False)
```

time: 225 us -> 88.7 us (0.39)
  other arithmetic: 88 us -> 2.58 us
  waiting for transfers between devices: 27.9 us -> 5.52 us
  Pallas kernels: 60.8 us -> 46.6 us
  local copies, waits for them, and re-layouts: 15.8 us -> 6.34 us
  starting transfers between devices: 31.2 us -> 26.2 us
    another operation x1, other arithmetic: 84.6 us -> 0.61 us  [local(): place = jnp.stack([is_sea.astype(jnp.int32), lax.axis_index('tile')])]
    ppermute x1, waiting for transfers between devices: 22.4 us -> 0.01 us  [local(): left = lax.ppermute(high_edge, 'tile', forward)]
    pallas_call x2 -> x3, Pallas kernels: 55.4 us -> 37.4 us  [the longest x1 17.5 us: inner_dynamics(): pl.pallas_call(functools.partial(inner_kernel, sizes), out_shape=jax.Shap...]
    unnamed x12 -> x16, local copies, waits for them, and re-layouts: 9.84 us -> 1.3 us
    all_to_all x1, starting transfers between devices: 11.5 us -> 4.3 us  [local(): lax.all_to_all(sent, 'tile', split_axis=0, concat_axis=0, tiled=True)]
    pallas_call x1, Pallas kernels: 4.17 us -> 7.98 us  [update(): pl.pallas_call(functools.partial(update_kernel, sizes, pieces), out_shape...]
  transfers between devices with their start and end apart: 6 -> 6, of which waited for: 2 -> 1; matrix products, arithmetic and copies ran while one was open for 2% -> 5% of each run, Pallas kernels for 22% -> 44%
where the time goes in v2:
time: 88.7 us; the launch traced here: 88.3 us
  Pallas kernels  46.6 us (53%)
  starting transfers between devices  26.2 us (30%)
  local copies, waits for them, and re-layouts  6.34 us (7%)
  waiting for transfers between devices  5.52 us (6%)
  other arithmetic  2.58 us (3%)
    pallas_call x1, Pallas kernels, inner_dynamics(): pl.pallas_call(functools.partial(inner_kernel, sizes), out_shape=jax.Shap...  17.5 us
    pallas_call x1, Pallas kernels, rim_dynamics(): pl.pallas_call(functools.partial(rim_kernel, sizes), out_shape=jax.ShapeD...  11.9 us
    pallas_call x1, Pallas kernels, remap(): pl.pallas_call(functools.partial(remap_kernel, sizes, n_tile, chunks), ou...  8.02 us
    pallas_call x1, Pallas kernels, update(): pl.pallas_call(functools.partial(update_kernel, sizes, pieces), out_shape...  7.98 us
    ppermute x1, starting transfers between devices, local(): right = lax.ppermute(low_edge, 'tile', backward)  7.37 us
    ppermute x1, starting transfers between devices, local(): lax.ppermute(low_part, 'tile', backward)  5.9 us
    all_to_all x1, waiting for transfers between devices, local(): lax.all_to_all(combine(received, sea_cols), 'comp', split_axis=0, concat_...  5.5 us
    all_to_all x1, starting transfers between devices, local(): lax.all_to_all(combine(received, sea_cols), 'comp', split_axis=0, concat_...  4.93 us
  transfers between devices with their start and end apart: 6, of which 1 were waited for; matrix products, arithmetic and copies ran while one was open for 5% of the time, Pallas kernels for 44%

profile of v2, /device:TPU:1, one launch (start us, length us, event | category | flops | bytes accessed | tf_op | source)
XLA Modules:
  0.0 88.3 jit_solution(14476276168864053281)
XLA Ops:
  0.0 0.7 convert_bitcast_fusion.mask_ref
  0.7 2.7 %conditional.1 = (f32[384,4,128]{2,1,0:T(4,128)}, f32[384,4,128]{2,1,0:T(4,128)}) conditional(s32[]{:T(128)} %convert_element_type.12, f32[1,1,1966080]{2,1,0:T(1,128)} %param.12, (f32[1,1,1966080]{2,1,0:T(1,128)}, f32[48,128]{1,0:T(8,128)S(1)}) %tuple.15), branch_computations={%region_0.0_spmd, %region_1.0_spmd} | conditional | flops 786432 | bytes 5520912 | solution.py:616
  0.7 2.7 %slice_bitcast_fusion = (f32[384,4,128]{2,1,0:T(4,128)}, f32[384,4,128]{2,1,0:T(4,128)}) fusion(f32[384,10,4,128]{3,2,1,0:T(4,128)} %bitcast.56), kind=kLoop, calls=%fused_computation | loop fusion | bytes 3145728 | tf_op jit(solution)/shard_map/cond/branch_0_fun/squeeze | solution.py:605
  3.5 2.1 %collective-permute-start = (f32[384,4,128]{2,1,0:T(4,128)}, f32[384,4,128]{2,1,0:T(4,128)S(1)}, u32[]{:S(2)}, u32[]{:S(2)}) collective-permute-start(f32[384,4,128]{2,1,0:T(4,128)} %get-tuple-element.23), channel_id=1, source_target_pairs={{0,1},{1,2},{2,3},{3,4},{4,5},{5,6},{6,7},{7,8},{8,9},{9,10},{10,1... | collective-permute-start | bytes 2359304 | tf_op jit(solution)/shard_map/ppermute | solution.py:618
  5.6 7.4 %collective-permute-start.1 = (f32[384,4,128]{2,1,0:T(4,128)}, f32[384,4,128]{2,1,0:T(4,128)S(1)}, u32[]{:S(2)}, u32[]{:S(2)}) collective-permute-start(f32[384,4,128]{2,1,0:T(4,128)} %get-tuple-element.24), channel_id=1, source_target_pairs={{1,0},{2,1},{3,2},{4,3},{5,4},{6,5},{7,6},{8,7},{9,8},{10,9},{11,1... | collective-permute-start | bytes 2359304 | tf_op jit(solution)/shard_map/ppermute | solution.py:619
  13.0 0.6 pad_add_fusion.place_ref
  13.6 0.0 copy-start.1
  13.6 0.0 copy-start.3
  13.6 8.0 %remap.1 = f32[32,56,128]{2,1,0:T(8,128)} custom-call(s32[2]{0:T(128)} %pad_add_fusion.place_ref, s32[1,256]{1,0:T(1,128)} %bitcast.63, s32[1,256]{1,0:T(1,128)} %bitcast.64, s32[1,256]{1,0:T(1,128)} %bitcast.65, f32[15360,128]{1,0:T(8,128)} %bitcast.52, bf16[4,64,128,128]{3,2,1,0:T(8,128)(2,1)} %bitcast.58), custom_call_target="tpu_custom_call" | custom-call | flops 134217728 | bytes 8388608 | tf_op jit(solution)/shard_map/remap/pallas_call | solution.py:224
  21.6 4.3 %all-to-all-start = ((f32[32,56,128]{2,1,0:T(8,128)}), f32[32,56,128]{2,1,0:T(8,128)S(1)}, u32[]{:S(2)}, u32[]{:S(2)}) async-start(f32[32,56,128]{2,1,0:T(8,128)} %remap.1), calls=%async_computation | async-start | bytes 1835008 | tf_op jit(solution)/shard_map/all_to_all | solution.py:632
  25.9 0.0 copy-done.1
  25.9 0.2 slice_reduce_fusion
  26.2 0.4 fusion.1
  26.6 0.0 copy-done.3
  26.6 0.2 slice_reduce_fusion.1
  26.8 0.4 fusion
  27.1 0.1 reshape.37
  27.2 0.0 copy-start.7
  27.2 0.0 copy-start.2
  27.2 0.0 copy-start.4
  27.2 0.0 copy-start.5
  27.3 17.5 %inner_dynamics.1.part_ref = f32[15360,128]{1,0:T(8,128)} custom-call(s32[1]{0:T(128)} %bitcast.8.sea_ref, f32[15360,128]{1,0:T(8,128)} %bitcast.53, f32[3,128,128]{2,1,0:T(8,128)} %atm_ref.3, f32[4,80,80]{2,1,0:T(8,128)} %ocean_ref.3, f32[48,128]{1,0:T(8,128)S(1)} %convert_bitcast_fusion.mask_ref, bf16[256,256]{1,0:T(8,128)(2,1)} %constant.22.clone.op_ref), custom_call_target="tpu_custom_call" | custom-call | flops 503316480 | bytes 3932160 | tf_op jit(solution)/shard_map/inner_dynamics/pallas_call | solution.py:366
  44.8 0.6 bitcast_select_fusion.column_ref
  45.3 0.0 copy-done.7
  45.3 0.0 collective-permute-done
  45.4 0.0 all-to-all-done.recv_ref
  45.4 1.2 %combine.1 = f32[4,3,48,128]{3,2,1,0:T(8,128)} custom-call(f32[32,56,128]{2,1,0:T(8,128)S(1)} %all-to-all-done.recv_ref), custom_call_target="tpu_custom_call" | custom-call | tf_op jit(solution)/shard_map/combine/pallas_call | solution.py:270
  46.6 4.9 %all-to-all-start.1 = ((f32[4,3,48,128]{3,2,1,0:T(8,128)}), f32[4,3,48,128]{3,2,1,0:T(8,128)S(1)}, u32[]{:S(2)}, u32[]{:S(2)}) async-start(f32[4,3,48,128]{3,2,1,0:T(8,128)} %combine.1), calls=%async_computation.1 | async-start | bytes 589824 | tf_op jit(solution)/shard_map/all_to_all | solution.py:654
  51.5 0.0 collective-permute-done.1
  51.5 5.5 %all-to-all-done.1 = f32[4,3,48,128]{3,2,1,0:T(8,128)S(1)} async-done(((f32[4,3,48,128]{3,2,1,0:T(8,128)}), f32[4,3,48,128]{3,2,1,0:T(8,128)S(1)}, u32[]{:S(2)}, u32[]{:S(2)}) %all-to-all-start.1) | async-done | bytes 294944 | tf_op jit(solution)/shard_map/all_to_all | solution.py:654
  57.1 0.0 copy-start.6
  57.1 1.6 %collective-permute-start.2 = (f32[3,4,128]{2,1,0:T(4,128)S(1)}, f32[3,4,128]{2,1,0:T(4,128)S(1)}, u32[]{:S(2)}, u32[]{:S(2)}) collective-permute-start(f32[3,4,128]{2,1,0:T(4,128)S(1)} %get-tuple-element.34), channel_id=1, source_target_pairs={{0,1},{1,2},{2,3},{3,4},{4,5},{5,6},{6,7},{7,8},{8,9},{9,10},{10,1... | collective-permute-start | bytes 18440 | tf_op jit(solution)/shard_map/ppermute | solution.py:659
  58.7 5.9 %collective-permute-start.3 = (f32[3,4,128]{2,1,0:T(4,128)S(1)}, f32[3,4,128]{2,1,0:T(4,128)S(1)}, u32[]{:S(2)}, u32[]{:S(2)}) collective-permute-start(f32[3,4,128]{2,1,0:T(4,128)S(1)} %get-tuple-element.35), channel_id=1, source_target_pairs={{1,0},{2,1},{3,2},{4,3},{5,4},{6,5},{7,6},{8,7},{9,8},{10,9},{11,1... | collective-permute-start | bytes 18440 | tf_op jit(solution)/shard_map/ppermute | solution.py:659
  64.6 0.0 copy-done.2
  64.6 0.0 copy-done.4
  64.6 0.0 copy-done.5
  64.6 11.9 %rim_dynamics.1.rim_ref = f32[3072,128]{1,0:T(8,128)S(1)} custom-call(s32[1]{0:T(128)} %bitcast.8.sea_ref, f32[384,40,128]{2,1,0:T(8,128)} %bitcast.54, f32[320,48,128]{2,1,0:T(8,128)} %bitcast.55, f32[1536,128]{1,0:T(8,128)S(1)} %bitcast.50, f32[1536,128]{1,0:T(8,128)S(1)} %bitcast.51, f32[3,128,128]{2,1,0:T(8,128)S(1)} %copy-done.2, ...), custom_call_target="tpu_custom_call" | custom-call | flops 5033164800 | bytes 4718592 | tf_op jit(solution)/shard_map/rim_dynamics/pallas_call | solution.py:455
  76.4 0.0 copy-done.6
  76.4 0.0 copy-start
  76.4 1.2 %copy-done = f32[3072,128]{1,0:T(8,128)} copy-done((f32[3072,128]{1,0:T(8,128)}, f32[3072,128]{1,0:T(8,128)S(1)}, u32[]{:S(2)}) %copy-start) | copy-done | bytes 1572888
  77.7 1.8 %concatenate.13.mask_ref = f32[64,128]{1,0:T(8,128)} concatenate(f32[4,128]{1,0:T(4,128)S(1)} %broadcast.10, f32[4,128]{1,0:T(4,128)S(1)} %slice_bitcast_fusion.7, f32[48,128]{1,0:T(8,128)S(1)} %convert_bitcast_fusion.mask_ref, f32[4,128]{1,0:T(4,128)S(1)} %slice_bitcast_fusion.6, f32[4,128]{1,0:T(4,128)S(1)} %broadcast.10), dimensions={0} | concatenate | bytes 65536 | tf_op jit(solution)/shard_map/concatenate | solution.py:638
  79.5 0.0 collective-permute-done.2
  79.5 0.0 collective-permute-done.3
  79.5 0.6 pad_maximum_fusion.1.halo_ref
  80.1 8.0 %update.1 = f32[15360,128]{1,0:T(8,128)} custom-call(s32[1]{0:T(128)} %bitcast.8.sea_ref, f32[384]{0:T(512)} %bitcast_select_fusion.column_ref, f32[15360,128]{1,0:T(8,128)} %inner_dynamics.1.part_ref, f32[3072,128]{1,0:T(8,128)} %copy-done, f32[3,48,128]{2,1,0:T(8,128)} %copy-done.6, f32[2,3,4,128]{3,2,1,0:T(4,128)} %pad_maximum_fusion.1.halo_ref, ...), custom_call_target="tpu_custom_call" | custom-call | flops 3932160 | bytes 15728640 | tf_op jit(solution)/shard_map/update/pallas_call | solution.py:566
  (9 shorter events, 0.1 us)
Async XLA Ops:
  3.5 41.9 %collective-permute-start = (f32[384,4,128]{2,1,0:T(4,128)}, f32[384,4,128]{2,1,0:T(4,128)S(1)}, u32[]{:S(2)}, u32[]{:S(2)}) collective-permute-start(f32[384,4,128]{2,1,0:T(4,128)} %get-tuple-element.23), channel_id=1, source_target_pairs={{0,1},{1,2},{2,3},{3,4},{4,5},{5,6},{6,7},{7,8},{8,9},{9,10},{10,1... | collective-permute-start | bytes 2359304 | tf_op jit(solution)/shard_map/ppermute | solution.py:618
  5.6 45.9 %collective-permute-start.1 = (f32[384,4,128]{2,1,0:T(4,128)}, f32[384,4,128]{2,1,0:T(4,128)S(1)}, u32[]{:S(2)}, u32[]{:S(2)}) collective-permute-start(f32[384,4,128]{2,1,0:T(4,128)} %get-tuple-element.24), channel_id=1, source_target_pairs={{1,0},{2,1},{3,2},{4,3},{5,4},{6,5},{7,6},{8,7},{9,8},{10,9},{11,1... | collective-permute-start | bytes 2359304 | tf_op jit(solution)/shard_map/ppermute | solution.py:619
  13.6 12.3 %copy-start.1 = (f32[3,128,128]{2,1,0:T(8,128)S(1)}, f32[3,128,128]{2,1,0:T(8,128)}, u32[]{:S(2)}) copy-start(f32[3,128,128]{2,1,0:T(8,128)} %atm_ref.3) | copy-start | bytes 589828
  13.6 13.0 %copy-start.3 = (f32[4,80,80]{2,1,0:T(8,128)S(1)}, f32[4,80,80]{2,1,0:T(8,128)}, u32[]{:S(2)}) copy-start(f32[4,80,80]{2,1,0:T(8,128)} %ocean_ref.3) | copy-start | bytes 307204
  21.6 23.7 %all-to-all-start = ((f32[32,56,128]{2,1,0:T(8,128)}), f32[32,56,128]{2,1,0:T(8,128)S(1)}, u32[]{:S(2)}, u32[]{:S(2)}) async-start(f32[32,56,128]{2,1,0:T(8,128)} %remap.1), calls=%async_computation | async-start | bytes 1835008 | tf_op jit(solution)/shard_map/all_to_all | solution.py:632
  27.2 18.1 %copy-start.7 = (s32[1,1,48,128]{3,2,1,0:T(8,128)S(1)}, s32[1,1,48,128]{3,2,1,0:T(8,128)}, u32[]{:S(2)}) copy-start(s32[1,1,48,128]{3,2,1,0:T(8,128)} %param.15) | copy-start | bytes 73732
  27.2 37.3 %copy-start.2 = (f32[3,128,128]{2,1,0:T(8,128)S(1)}, f32[3,128,128]{2,1,0:T(8,128)}, u32[]{:S(2)}) copy-start(f32[3,128,128]{2,1,0:T(8,128)} %atm_ref.3) | copy-start | bytes 589828
  27.2 37.3 %copy-start.4 = (f32[4,80,80]{2,1,0:T(8,128)S(1)}, f32[4,80,80]{2,1,0:T(8,128)}, u32[]{:S(2)}) copy-start(f32[4,80,80]{2,1,0:T(8,128)} %ocean_ref.3) | copy-start | bytes 307204
  27.2 37.3 %copy-start.5 = (bf16[256,256]{1,0:T(8,128)(2,1)S(1)}, bf16[256,256]{1,0:T(8,128)(2,1)}, u32[]{:S(2)}) copy-start(bf16[256,256]{1,0:T(8,128)(2,1)} %constant.22.clone.op_ref) | copy-start | bytes 393220
  46.6 10.5 %all-to-all-start.1 = ((f32[4,3,48,128]{3,2,1,0:T(8,128)}), f32[4,3,48,128]{3,2,1,0:T(8,128)S(1)}, u32[]{:S(2)}, u32[]{:S(2)}) async-start(f32[4,3,48,128]{3,2,1,0:T(8,128)} %combine.1), calls=%async_computation.1 | async-start | bytes 589824 | tf_op jit(solution)/shard_map/all_to_all | solution.py:654
  57.1 19.4 %copy-start.6 = (f32[3,48,128]{2,1,0:T(8,128)}, f32[3,48,128]{2,1,0:T(8,128)S(1)}, u32[]{:S(2)}) copy-start(f32[3,48,128]{2,1,0:T(8,128)S(1)} %broadcast_multiply_fusion.forcing_ref) | copy-start | bytes 221188
  57.1 22.4 %collective-permute-start.2 = (f32[3,4,128]{2,1,0:T(4,128)S(1)}, f32[3,4,128]{2,1,0:T(4,128)S(1)}, u32[]{:S(2)}, u32[]{:S(2)}) collective-permute-start(f32[3,4,128]{2,1,0:T(4,128)S(1)} %get-tuple-element.34), channel_id=1, source_target_pairs={{0,1},{1,2},{2,3},{3,4},{4,5},{5,6},{6,7},{7,8},{8,9},{9,10},{10,1... | collective-permute-start | bytes 18440 | tf_op jit(solution)/shard_map/ppermute | solution.py:659
  58.7 20.8 %collective-permute-start.3 = (f32[3,4,128]{2,1,0:T(4,128)S(1)}, f32[3,4,128]{2,1,0:T(4,128)S(1)}, u32[]{:S(2)}, u32[]{:S(2)}) collective-permute-start(f32[3,4,128]{2,1,0:T(4,128)S(1)} %get-tuple-element.35), channel_id=1, source_target_pairs={{1,0},{2,1},{3,2},{4,3},{5,4},{6,5},{7,6},{8,7},{9,8},{10,9},{11,1... | collective-permute-start | bytes 18440 | tf_op jit(solution)/shard_map/ppermute | solution.py:659
  76.4 1.2 %copy-start = (f32[3072,128]{1,0:T(8,128)}, f32[3072,128]{1,0:T(8,128)S(1)}, u32[]{:S(2)}) copy-start(f32[3072,128]{1,0:T(8,128)S(1)} %rim_dynamics.1.rim_ref) | copy-start | bytes 4718596

commit v3 on v2

v3 whole, which is shorter than its diff:
```python
import functools

import jax
import jax.numpy as jnp
import numpy as np
from jax import lax
from jax.experimental import pallas as pl
from jax.experimental.pallas import tpu as pltpu
from jax.sharding import PartitionSpec as P

FA = 3
FO = 4
LA = 128
LO = 80
R = 128
CAP = 16

COUPLE_RATE = 0.1
NU_ATMOS = 0.02
NU_OCEAN = 0.015

HALO = 4
EDGE_ROWS = 3 * 2 * HALO
FIELD_ROWS = CAP + EDGE_ROWS
CHUNK_ROWS = FA * FIELD_ROWS + 8
MIB = 1 << 20
SIDE = (4, 5)


def split_two(value):
    high = value.astype(jnp.bfloat16)
    return high, (value - high.astype(jnp.float32)).astype(jnp.bfloat16)


def row_operator():
    u = np.eye(R, k=1) + np.eye(R, k=-1) - 4.0 * np.eye(R)
    both = np.concatenate([2.0 * u, u @ u + 2.0 * np.eye(R)], axis=1)
    return jnp.asarray(np.concatenate([both, both], axis=0), jnp.bfloat16)


def apply_filter(value, column_sums, row_parts, nu):
    return value - nu * (column_sums + row_parts)


def filter_planes(column, first, last, nu, mask, operator, lhs_ref, emit):
    rows = 16
    for k in range(first - 1, last + 1):
        spot = (k - first + 1) * rows
        high, low = split_two(column(k))
        lhs_ref[spot : spot + rows, :R] = high
        lhs_ref[spot : spot + rows, R:] = low
    both = jnp.dot(
        lhs_ref[: (last - first + 2) * rows], operator, preferred_element_type=jnp.float32
    )

    def part(k, half):
        spot = (k - first + 1) * rows
        return both[spot : spot + rows, half * R : (half + 1) * R]

    for k in range(first, last):
        column_sums = column(k - 2) + column(k + 2)
        row_parts = (part(k - 1, 0) + part(k + 1, 0)) + part(k, 1)
        plane = apply_filter(column(k), column_sums, row_parts, nu)
        if mask is not None:
            plane = plane * mask(k)
        emit(k, plane)


def surface_copies(sizes, sea, x_ref, surf_ref, sems):
    atm_cols, sea_cols = sizes
    if sea:
        cols, starts = sea_cols, [f * LO * sea_cols for f in range(FA)]
    else:
        cols, starts = atm_cols, [(f * LA + LA - 1) * atm_cols for f in range(FA)]
    return [
        pltpu.make_async_copy(
            x_ref.at[pl.ds(start, cols)], surf_ref.at[pl.ds(f * sea_cols, cols)], sems.at[f]
        )
        for f, start in enumerate(starts)
    ]


def small_mod(value, modulus, limit):
    for step in range(modulus, limit, modulus):
        value = jnp.where(value >= modulus, value - modulus, value)
    return value


def as_column(row):
    n = row.shape[1]
    diagonal = lax.broadcasted_iota(jnp.int32, (n, n), 0) == lax.broadcasted_iota(jnp.int32, (n, n), 1)
    return jnp.sum(jnp.where(diagonal, row, 0.0), axis=1, keepdims=True)


def ones_where(condition):
    return jnp.where(condition, 1.0, 0.0).astype(jnp.bfloat16)


def remap_kernel(
    sizes, n_tile, chunks, sea_ref, place_ref, source_ref, tile_ref, slot_ref, x_ref, w_ref, out_ref, w_vmem, surf_ref, pick_ref, part_ref, w_sems, x_sems
):
    atm_cols, sea_cols = sizes
    entries = source_ref.shape[1]
    quarter = entries // 4
    per_chunk = quarter // chunks
    code_limit = 5 * sea_cols
    copies = [
        pltpu.make_async_copy(
            w_ref.at[:, pl.ds(n * per_chunk, per_chunk)], w_vmem.at[:, pl.ds(n * per_chunk, per_chunk)], w_sems.at[n]
        )
        for n in range(chunks)
    ]
    is_sea = sea_ref[0] != 0
    for sea in (False, True):

        @pl.when(is_sea == sea)
        def _(sea=sea):
            for copy in surface_copies(sizes, sea, x_ref, surf_ref, x_sems):
                copy.start()

    for copy in copies:
        copy.start()

    tile = tile_ref[...].astype(jnp.float32)
    tile_column = as_column(tile)
    earlier = lax.broadcasted_iota(jnp.int32, (entries, entries), 0) < lax.broadcasted_iota(
        jnp.int32, (entries, entries), 1
    )
    rank = jnp.sum(jnp.where((tile_column == tile) & earlier, 1.0, 0.0), axis=0, keepdims=True)
    code = slot_ref[...]
    for_atm = small_mod(code, 3 * atm_cols, code_limit)
    for_atm_block = small_mod(for_atm, atm_cols, 3 * atm_cols)
    for_atm_group = jnp.where(for_atm >= atm_cols, 1, 0) + jnp.where(for_atm >= 2 * atm_cols, 1, 0)
    for_sea_block = small_mod(code, sea_cols, code_limit)
    window = sea_cols + 2 * HALO
    group = jnp.where(is_sea, for_atm_group, 3)
    block = jnp.where(is_sea, for_atm_block, for_sea_block)
    dest = (group * window + block + HALO + 1).astype(jnp.float32)
    lane = rank + (CAP * lax.rem(place_ref[0], R // CAP)).astype(jnp.float32)
    spots = lax.broadcasted_iota(jnp.int32, (R, entries), 0).astype(jnp.float32)
    marks = jnp.where(spots == lane, dest, 0.0).astype(jnp.bfloat16)
    tiles = lax.broadcasted_iota(jnp.int32, (n_tile, entries), 0).astype(jnp.float32)
    codes = lax.dot_general(
        ones_where(tiles == tile), marks, (((1,), (1,)), ((), ())), preferred_element_type=jnp.float32
    )
    tile_number = tile_ref[...]
    high_start = jnp.where(is_sea, atm_cols, sea_cols) - HALO
    edge_tile = jnp.where(block < HALO, tile_number + n_tile - 1, tile_number + 1)
    edge_tile = jnp.where(edge_tile >= n_tile, edge_tile - n_tile, edge_tile)
    edge_row = jnp.where(block < HALO, block + HALO, block - high_start)
    edge_row = edge_tile * EDGE_ROWS + jnp.where(is_sea, group, 0) * (2 * HALO) + edge_row
    on_edge = (block < HALO) | (block >= high_start)
    edge_slot = jnp.where(on_edge, edge_row, -1).astype(jnp.float32)
    tail = CHUNK_ROWS - FA * FIELD_ROWS
    for t in range(n_tile):
        out_ref[t, FA * FIELD_ROWS :, :] = jnp.concatenate(
            [codes[t : t + 1], jnp.zeros((tail - 1, R), jnp.float32)], axis=0
        )

    source = source_ref[...]
    source = jnp.where(
        is_sea, small_mod(source, sea_cols, code_limit), small_mod(source, atm_cols, code_limit)
    )
    source_column = as_column(source.astype(jnp.float32))
    columns = lax.broadcasted_iota(jnp.int32, (entries, sea_cols), 1).astype(jnp.float32)
    chooser = ones_where(columns == source_column)
    for sea in (False, True):

        @pl.when(is_sea == sea)
        def _(sea=sea):
            for copy in surface_copies(sizes, sea, x_ref, surf_ref, x_sems):
                copy.wait()
            if not sea:
                for f in range(FA):
                    surf_ref[f * sea_cols + atm_cols : (f + 1) * sea_cols, :] = jnp.zeros(
                        (sea_cols - atm_cols, R), jnp.float32
                    )

    for f in range(FA):
        surface = surf_ref[f * sea_cols : (f + 1) * sea_cols, :].astype(jnp.bfloat16)
        pick_ref[f * entries : (f + 1) * entries, :] = jnp.dot(
            chooser, surface, preferred_element_type=jnp.float32
        )
    pick_ref[FA * entries :, :] = jnp.zeros((entries, R), jnp.float32)

    member = lax.rem(lax.broadcasted_iota(jnp.int32, (16, R), 0), 4)
    def chunk(n, carry):
        span = pl.ds(n * per_chunk, per_chunk)
        pltpu.make_async_copy(w_ref.at[:, span], w_vmem.at[:, span], w_sems.at[n]).wait()
        for step in range(per_chunk):
            g = n * per_chunk + step
            picked = pick_ref[pl.ds(g, 16, stride=quarter), :]
            rows = jnp.concatenate(
                [jnp.where(member < 2, picked, 0.0), jnp.where(member >= 2, picked, 0.0)], axis=1
            ).astype(jnp.bfloat16)
            block = jnp.concatenate(
                [
                    jnp.concatenate([w_vmem[0, g], w_vmem[2, g]], axis=1),
                    jnp.concatenate([w_vmem[1, g], w_vmem[3, g]], axis=1),
                ],
                axis=0,
            )
            res = lax.dot_general(
                rows, block, (((1,), (1,)), ((), ())), preferred_element_type=jnp.float32
            )
            part_ref[pl.ds(g, 16, stride=quarter), :] = jnp.where(member % 2 == 0, res[:, :R], res[:, R:])
        return carry

    lax.fori_loop(0, chunks, chunk, 0)

    slot = tile * CAP + rank
    slots = lax.broadcasted_iota(jnp.int32, (n_tile * CAP, entries), 0).astype(jnp.float32)
    placer = ones_where(slots == slot)
    edge_slots = lax.broadcasted_iota(jnp.int32, (n_tile * EDGE_ROWS, entries), 0).astype(jnp.float32)
    edge_placer = ones_where(edge_slots == edge_slot)
    for f in range(FA):
        high, low = split_two(part_ref[f * entries : (f + 1) * entries, :])
        values = jnp.concatenate([high, low], axis=1)
        start = f * FIELD_ROWS
        for place_matrix, size in ((placer, CAP), (edge_placer, EDGE_ROWS)):
            both = jnp.dot(place_matrix, values, preferred_element_type=jnp.float32)
            placed = both[:, :R] + both[:, R:]
            for t in range(n_tile):
                out_ref[t, start : start + size, :] = placed[t * size : (t + 1) * size]
            start += size


def remap(is_sea, place, source, tile, slot, x, weights, n_tile, sizes):
    entries = weights.shape[0]
    chunks = 8
    vmem = pl.BlockSpec(memory_space=pltpu.VMEM)
    anywhere = pl.BlockSpec(memory_space=pl.ANY)
    return pl.pallas_call(
        functools.partial(remap_kernel, sizes, n_tile, chunks),
        out_shape=jax.ShapeDtypeStruct((n_tile, CHUNK_ROWS, R), jnp.float32),
        in_specs=[pl.BlockSpec(memory_space=pltpu.SMEM)] * 2 + [vmem, vmem, vmem, anywhere, anywhere],
        out_specs=vmem,
        scratch_shapes=[
            pltpu.VMEM((4, entries // 4, R, R), jnp.bfloat16),
            pltpu.VMEM((FA * sizes[1], R), jnp.float32),
            pltpu.VMEM((4 * entries, R), jnp.float32),
            pltpu.VMEM((4 * entries, R), jnp.float32),
            pltpu.SemaphoreType.DMA((chunks,)),
            pltpu.SemaphoreType.DMA((FA,)),
        ],
        compiler_params=pltpu.CompilerParams(vmem_limit_bytes=56 * MIB),
        cost_estimate=pl.CostEstimate(
            flops=2000 * entries * R * R, bytes_accessed=weights.size * 2, transcendentals=0
        ),
        name="remap",
    )(is_sea, place, source, tile, slot, x, weights.reshape(4, entries // 4, R, R))


def combine_kernel(sizes, sea_ref, recv_ref, out_ref):
    atm_cols, sea_cols = sizes
    n_tile, per_group = recv_ref.shape[0], out_ref.shape[2]
    rows = 4 * per_group
    spots = lax.broadcasted_iota(jnp.int32, (rows, R), 0).astype(jnp.float32) + 1.0
    total = [jnp.zeros((rows, R), jnp.float32) for _ in range(FA)]
    for g in range(n_tile // 8):
        some = slice(g * 8, (g + 1) * 8)
        code = jnp.sum(recv_ref[some, FA * FIELD_ROWS, :], axis=0, keepdims=True)
        pick = ones_where(spots == code)
        for f in range(FA):
            start = f * FIELD_ROWS
            high, low = split_two(recv_ref[some, start : start + CAP, :].reshape(8 * CAP, R))
            both = jnp.dot(
                pick, jnp.concatenate([high, low], axis=1), preferred_element_type=jnp.float32
            )
            total[f] = total[f] + (both[:, :R] + both[:, R:])
    for f in range(FA):
        for c in range(4):
            out_ref[c, f] = total[f][c * per_group : (c + 1) * per_group]
    for f in range(FA):
        start = f * FIELD_ROWS + CAP
        edge = jnp.sum(recv_ref[:, start : start + EDGE_ROWS, :], axis=0)

        @pl.when(sea_ref[0] == 0)
        def _(f=f, edge=edge):
            out_ref[3, f, 0:HALO, :] = edge[0:HALO]
            out_ref[3, f, HALO + sea_cols : 2 * HALO + sea_cols, :] = edge[HALO : 2 * HALO]

        @pl.when(sea_ref[0] != 0)
        def _(f=f, edge=edge):
            for c in range(3):
                first = c * 2 * HALO
                out_ref[c, f, 0:HALO, :] = edge[first : first + HALO]
                out_ref[c, f, HALO + atm_cols : 2 * HALO + atm_cols, :] = edge[first + HALO : first + 2 * HALO]


def combine(is_sea, recv, sizes):
    vmem = pl.BlockSpec(memory_space=pltpu.VMEM)
    return pl.pallas_call(
        functools.partial(combine_kernel, sizes),
        out_shape=jax.ShapeDtypeStruct((4, FA, sizes[1] + 2 * HALO, R), jnp.float32),
        in_specs=[pl.BlockSpec(memory_space=pltpu.SMEM), vmem],
        out_specs=vmem,
        compiler_params=pltpu.CompilerParams(vmem_limit_bytes=16 * MIB),
        name="combine",
    )(is_sea, recv)


def edges_kernel(sea_ref, x_atm_ref, x_sea_ref, mask_ref, low_ref, high_ref, sems):
    for sea, x_ref in ((False, x_atm_ref), (True, x_sea_ref)):
        count, blocks = x_ref.shape[0], x_ref.shape[1]

        @pl.when((sea_ref[0] != 0) == sea)
        def _(sea=sea, x_ref=x_ref, count=count, blocks=blocks):
            copies = [
                pltpu.make_async_copy(x_ref.at[:, 0], low_ref.at[pl.ds(0, count)], sems.at[0]),
                pltpu.make_async_copy(x_ref.at[:, blocks - 1], high_ref.at[pl.ds(0, count)], sems.at[1]),
            ]
            for copy in copies:
                copy.start()
            for ref, block in ((low_ref, 0), (high_ref, blocks - 1)):
                if count < FA * LA:
                    ref[count : FA * LA] = jnp.zeros((FA * LA - count, HALO, R), jnp.float32)
                ref[FA * LA : FA * LA + 1] = mask_ref[block : block + 1].astype(jnp.float32)
                ref[FA * LA + 1 :] = jnp.zeros((ref.shape[0] - FA * LA - 1, HALO, R), jnp.float32)
            for copy in copies:
                copy.wait()


def edge_columns(is_sea, state, mask, sizes):
    atm_cols, sea_cols = sizes
    anywhere = pl.BlockSpec(memory_space=pl.ANY)
    vmem = pl.BlockSpec(memory_space=pltpu.VMEM)
    shape = jax.ShapeDtypeStruct((FA * LA + 2, HALO, R), jnp.float32)
    return pl.pallas_call(
        edges_kernel,
        out_shape=[shape, shape],
        in_specs=[pl.BlockSpec(memory_space=pltpu.SMEM), anywhere, anywhere, vmem],
        out_specs=[vmem, vmem],
        scratch_shapes=[pltpu.SemaphoreType.DMA((2,))],
        compiler_params=pltpu.CompilerParams(vmem_limit_bytes=56 * MIB),
        name="edges",
    )(
        is_sea,
        state.reshape(FA * LA, atm_cols // HALO, HALO, R),
        state.reshape(FO * LO, sea_cols // HALO, HALO, R),
        mask.reshape(sea_cols // HALO, HALO, R),
    )


def filtered_twice(cols, nu, column, mask, operator, lhs_ref, mid_ref, store):
    def middle(k):
        return mid_ref[(k + 2) * 16 : (k + 3) * 16, :]

    def keep(k, plane):
        mid_ref[(k + 2) * 16 : (k + 3) * 16, :] = plane

    filter_planes(column, -2, cols + 2, nu, mask, operator, lhs_ref.at[0], keep)
    filter_planes(middle, 0, cols, nu, mask, operator, lhs_ref.at[1], store)


def dynamics_part(
    fields, levels, cols, surface, side, nu, x_ref, left_ref, right_ref, matrix_ref, mask_ref, op_ref, out_ref, column_ref,
    x_vmem, out_vmem, y_vmem, lhs_ref, mid_ref, mask_vmem, in_sems, out_sems
):
    rows = levels * cols

    def read(f):
        span = pl.ds(pl.multiple_of(f * rows, 8), rows)
        return pltpu.make_async_copy(x_ref.at[span], x_vmem.at[span], in_sems.at[f])

    def write(f):
        span = pl.ds(pl.multiple_of(f * rows, 8), rows)
        return pltpu.make_async_copy(out_vmem.at[span], out_ref.at[span], out_sems.at[f])

    read(0).start()
    mask = None
    if mask_ref is not None:
        spare = FA * LA * HALO
        mask_vmem[0:HALO, :] = left_ref[spare : spare + HALO, :]
        mask_vmem[HALO : HALO + cols, :] = mask_ref[...].astype(jnp.float32)
        mask_vmem[HALO + cols : 2 * HALO + cols, :] = right_ref[spare : spare + HALO, :]
        mask = lambda k: jnp.broadcast_to(mask_vmem[k + HALO : k + HALO + 1, :], (16, R))

    def field(f, carry):
        squared = jnp.dot(
            matrix_ref[f], matrix_ref[f], precision=lax.Precision.HIGHEST, preferred_element_type=jnp.float32
        )
        column_ref[pl.ds(pl.multiple_of(f * levels, 8), levels), :] = jnp.broadcast_to(
            squared[:, surface : surface + 1], (levels, R)
        )
        high, low = split_two(squared)
        stacked = jnp.concatenate(
            [jnp.concatenate([high, high], axis=1), jnp.concatenate([low, jnp.zeros_like(low)], axis=1)], axis=0
        )
        read(f).wait()

        @pl.when(f + 1 < fields)
        def _():
            read(f + 1).start()

        def filter_rows(i, slot):
            first = f * levels + i * 16
            spot = pl.multiple_of(i * 16, 16)

            def column(k):
                if k < 0:
                    return left_ref[pl.ds(first * HALO + k + HALO, 16, stride=HALO), :]
                if k >= cols:
                    return right_ref[pl.ds(first * HALO + k - cols, 16, stride=HALO), :]
                return x_vmem[pl.ds(first * cols + k, 16, stride=cols), :]

            def store(k, plane):
                high, low = split_two(plane)
                y_vmem[pl.ds(spot, 16), k * R : (k + 1) * R] = high
                y_vmem[pl.ds(levels + spot, 16), k * R : (k + 1) * R] = low

            filtered_twice(cols, nu, column, mask, op_ref[...], lhs_ref.at[slot], mid_ref.at[slot], store)

        def filter_some(n, carry):
            for slot in range(side):
                filter_rows(n * side + slot, slot)
            return carry

        lax.fori_loop(0, levels // 16 // side, filter_some, 0)

        for pair in range(cols // 2):
            both = jnp.dot(
                stacked,
                y_vmem[: 2 * levels, 2 * pair * R : 2 * (pair + 1) * R],
                preferred_element_type=jnp.float32,
            )
            mixed = both[:levels] + both[levels:]
            for h in range(2):
                out_vmem[pl.ds(f * rows + 2 * pair + h, levels, stride=cols), :] = mixed[:, h * R : (h + 1) * R]
        write(f).start()
        return carry

    lax.fori_loop(0, fields, field, 0)
    for f in range(fields):
        write(f).wait()


def dynamics_kernel(
    sizes, sea_ref, x_ref, left_ref, right_ref, atm_ref, ocean_ref, mask_ref, op_ref, *rest
):
    atm_cols, sea_cols = sizes

    @pl.when(sea_ref[0] == 0)
    def _():
        dynamics_part(
            FA, LA, atm_cols, LA - 1, SIDE[0], NU_ATMOS, x_ref, left_ref, right_ref, atm_ref, None, op_ref, *rest
        )

    @pl.when(sea_ref[0] != 0)
    def _():
        dynamics_part(
            FO, LO, sea_cols, 0, SIDE[1], NU_OCEAN, x_ref, left_ref, right_ref, ocean_ref, mask_ref, op_ref, *rest
        )


def dynamics(is_sea, x, left, right, atm_mixing, ocean_mixing, mask, sizes):
    vmem = pl.BlockSpec(memory_space=pltpu.VMEM)
    anywhere = pl.BlockSpec(memory_space=pl.ANY)
    rows = x.shape[0]
    widest = max(sizes)
    return pl.pallas_call(
        functools.partial(dynamics_kernel, sizes),
        out_shape=[
            jax.ShapeDtypeStruct((rows, R), jnp.float32),
            jax.ShapeDtypeStruct((FA * LA, R), jnp.float32),
        ],
        in_specs=[pl.BlockSpec(memory_space=pltpu.SMEM), anywhere] + [vmem] * 6,
        out_specs=[anywhere, vmem],
        scratch_shapes=[
            pltpu.VMEM((rows, R), jnp.float32),
            pltpu.VMEM((rows, R), jnp.float32),
            pltpu.VMEM((2 * LA, widest * R), jnp.bfloat16),
            pltpu.VMEM((max(SIDE), 2, (widest + 6) * 16, 2 * R), jnp.bfloat16),
            pltpu.VMEM((max(SIDE), (widest + 4) * 16, R), jnp.float32),
            pltpu.VMEM((widest + 2 * HALO, R), jnp.float32),
            pltpu.SemaphoreType.DMA((FO,)),
            pltpu.SemaphoreType.DMA((FO,)),
        ],
        compiler_params=pltpu.CompilerParams(vmem_limit_bytes=56 * MIB),
        cost_estimate=pl.CostEstimate(
            flops=100 * rows * R * R, bytes_accessed=16 * rows * R, transcendentals=0
        ),
        name="dynamics",
    )(is_sea, x, left, right, atm_mixing, ocean_mixing, mask, row_operator())


def lane_edges(rows):
    lane = lax.broadcasted_iota(jnp.int32, (rows, R), 1)
    return lane == 0, lane == R - 1


def lap(before, middle, after, edges):
    first, last = edges
    down = jnp.where(first, 0.0, pltpu.roll(middle, 1, 1))
    up = jnp.where(last, 0.0, pltpu.roll(middle, R - 1, 1))
    return (before + after) + (down + up) - 4.0 * middle


def filter_forcing(cols, nu, shares_ref, masked, mask_ref, work_ref, g_ref):
    lo, hi, rows = 8, 8 + cols, cols + 16
    edges = lane_edges(rows)
    mask = mask_ref[0:rows, :]

    def along(v):
        return lap(pltpu.roll(v, 1, 0), v, pltpu.roll(v, rows - 1, 0), edges)

    for f in range(FA):
        forcing = (shares_ref[0, f] + shares_ref[1, f]) + (shares_ref[2, f] + shares_ref[3, f])
        work_ref[0:rows, :] = jnp.zeros((rows, R), jnp.float32)
        work_ref[lo - HALO : hi + HALO, :] = COUPLE_RATE * forcing[: cols + 2 * HALO]
        value = work_ref[0:rows, :] * mask
        for _ in range(2):
            value = value - nu * along(along(value))
            if masked:
                value = value * mask
        g_ref[f, :cols] = value[lo:hi]


def update_part(
    cols, levels, fields, pieces, masked, nu, column_ref, part_ref, shares_ref, mask_ref, left_ref, right_ref, out_ref,
    work_ref, g_ref, mask_vmem, stage_ref, in_sems, out_sems, mask_sems
):
    per_piece = fields * levels // pieces
    rows = per_piece * cols

    def read(p):
        span = pl.ds(pl.multiple_of(p * rows, 8), rows)
        return pltpu.make_async_copy(part_ref.at[span], stage_ref.at[span], in_sems.at[p])

    def write(p):
        span = pl.ds(pl.multiple_of(p * rows, 8), rows)
        return pltpu.make_async_copy(stage_ref.at[span], out_ref.at[span], out_sems.at[p])

    span = pl.ds(FA * LA * HALO, 8)
    ends = [
        pltpu.make_async_copy(left_ref.at[span], mask_vmem.at[pl.ds(64, 8)], mask_sems.at[0]),
        pltpu.make_async_copy(right_ref.at[span], mask_vmem.at[pl.ds(72, 8)], mask_sems.at[1]),
    ]
    for copy in ends:
        copy.start()
    for p in range(pieces):
        read(p).start()
    mask_vmem[0:8, :] = jnp.zeros((8, R), jnp.float32)
    mask_vmem[8 : 8 + cols, :] = mask_ref[:cols].astype(jnp.float32)
    mask_vmem[8 + cols : 16 + cols, :] = jnp.zeros((8, R), jnp.float32)
    for copy in ends:
        copy.wait()
    mask_vmem[8 - HALO : 8, :] = mask_vmem[64 : 64 + HALO, :]
    mask_vmem[8 + cols : 8 + HALO + cols, :] = mask_vmem[72 : 72 + HALO, :]
    filter_forcing(cols, nu, shares_ref, masked, mask_vmem, work_ref, g_ref)

    def piece(p, carry):
        read(p).wait()
        field = p * per_piece // levels

        @pl.when(field < FA)
        def _():
            pushed = [g_ref[field, v * 8 : v * 8 + 8, :] for v in range(cols // 8)]

            def group(q, carry):
                number = p * per_piece + q
                factor = jnp.broadcast_to(column_ref[pl.ds(number, 1), :], (8, R))
                for v in range(cols // 8):
                    span = pl.ds(pl.multiple_of(number * cols + v * 8, 8), 8)
                    stage_ref[span, :] = stage_ref[span, :] + factor * pushed[v]
                return carry

            lax.fori_loop(0, per_piece, group, 0, unroll=8)

        write(p).start()
        return carry

    lax.fori_loop(0, pieces, piece, 0)
    for p in range(pieces):
        write(p).wait()


def update_kernel(sizes, sea_ref, *rest):
    atm_cols, sea_cols = sizes

    @pl.when(sea_ref[0] == 0)
    def _():
        update_part(atm_cols, LA, FA, 4 * FA, False, NU_ATMOS, *rest)

    @pl.when(sea_ref[0] != 0)
    def _():
        update_part(sea_cols, LO, FO, 2 * FO, True, NU_OCEAN, *rest)


def update(is_sea, column, part, shares, mask, left, right, sizes):
    vmem = pl.BlockSpec(memory_space=pltpu.VMEM)
    smem = pl.BlockSpec(memory_space=pltpu.SMEM)
    anywhere = pl.BlockSpec(memory_space=pl.ANY)
    rows = part.shape[0]
    return pl.pallas_call(
        functools.partial(update_kernel, sizes),
        out_shape=jax.ShapeDtypeStruct((rows, R), jnp.float32),
        in_specs=[smem, vmem, anywhere, vmem, vmem, anywhere, anywhere],
        out_specs=anywhere,
        scratch_shapes=[
            pltpu.VMEM((max(sizes) + 16, R), jnp.float32),
            pltpu.VMEM((FA, max(sizes), R), jnp.float32),
            pltpu.VMEM((80, R), jnp.float32),
            pltpu.VMEM((rows, R), jnp.float32),
            pltpu.SemaphoreType.DMA((4 * FA,)),
            pltpu.SemaphoreType.DMA((4 * FA,)),
            pltpu.SemaphoreType.DMA((2,)),
        ],
        compiler_params=pltpu.CompilerParams(vmem_limit_bytes=56 * MIB),
        cost_estimate=pl.CostEstimate(
            flops=2 * rows * R, bytes_accessed=8 * rows * R, transcendentals=0
        ),
        name="update",
    )(is_sea, column, part, shares, mask, left, right)


def local(
    fields, atm_mixing, ocean_mixing, sea_mask, source_slot, target_tile, target_slot, remap_blocks
):
    n_comp = lax.axis_size("comp")
    n_tile = lax.axis_size("tile")
    is_sea = lax.axis_index("comp") == n_comp - 1
    sea_cols = sea_mask.shape[2]
    atm_cols = sea_cols * 5 // 6
    sizes = (atm_cols, sea_cols)
    sea_flag = is_sea.astype(jnp.int32).reshape(1)
    mask = sea_mask[0, 0]
    state = fields[0, 0]
    tiles = target_tile[0, 0, :, 0]
    weights = remap_blocks[0, 0]
    forward = [(i, (i + 1) % n_tile) for i in range(n_tile)]
    backward = [(b, a) for a, b in forward]

    low_edge, high_edge = edge_columns(sea_flag, state, mask, sizes)
    low_edge, high_edge, tiles = lax.optimization_barrier((low_edge, high_edge, tiles))
    left = lax.ppermute(high_edge, "tile", forward)
    right = lax.ppermute(low_edge, "tile", backward)

    sent = remap(
        sea_flag,
        lax.axis_index("tile").reshape(1),
        source_slot.reshape(1, -1),
        tiles.reshape(1, -1),
        target_slot.reshape(1, -1),
        state.reshape(-1, R),
        weights,
        n_tile,
        sizes,
    )
    received = lax.all_to_all(
        sent, "tile", split_axis=0, concat_axis=0, tiled=True
    )

    x = state.reshape(-1, R)
    flat_left = left.reshape(-1, R)
    flat_right = right.reshape(-1, R)
    part, column = dynamics(sea_flag, x, flat_left, flat_right, atm_mixing, ocean_mixing, mask, sizes)

    received, part = lax.optimization_barrier((received, part))
    shares = lax.all_to_all(combine(sea_flag, received, sizes), "comp", split_axis=0, concat_axis=0, tiled=True)
    done = update(sea_flag, column, part, shares, mask, flat_left, flat_right, sizes)
    return done.reshape(1, 1, -1)


def solution(mesh):
    in_specs = (
        P("comp", "tile", None),
        P(),
        P(),
        P("comp", "tile", None, None),
        P("comp", "tile", None),
        P("comp", "tile", None, None),
        P("comp", "tile", None),
        P("comp", "tile", None, None, None),
    )
    out_specs = P("comp", "tile", None)
    return jax.shard_map(local, mesh=mesh, in_specs=in_specs, out_specs=out_specs, check_vma=False)
```

time: 88.7 us -> 74.1 us (0.84)
  starting transfers between devices: 26.2 us -> 13.9 us
  blocking collectives: 0 us -> 11.6 us
  Pallas kernels: 46.6 us -> 38.1 us
  local copies, waits for them, and re-layouts: 6.34 us -> 0.96 us
  waiting for transfers between devices: 5.52 us -> 9.08 us
  other arithmetic: 2.58 us -> 0 us
    all_to_all x0 -> x1, blocking collectives: none -> 11.6 us  [local(): lax.all_to_all(combine(sea_flag, received, sizes), 'comp', split_axis=0,...]
    pallas_call x4, Pallas kernels: 38.5 us -> 28.9 us  [the longest x1 17.5 us: dynamics(): pl.pallas_call(functools.partial(dynamics_kernel, sizes), out_shape=[jax....]
    ppermute x2 -> x0, starting transfers between devices: 7.47 us -> none  [the longest x1 5.9 us: local(): lax.ppermute(low_part, 'tile', backward)]
    all_to_all x1 -> x0, waiting for transfers between devices: 5.5 us -> none  [local(): lax.all_to_all(combine(received, sea_cols), 'comp', split_axis=0, concat_...]
    all_to_all x1, waiting for transfers between devices: 0.01 us -> 5.03 us  [local(): lax.all_to_all(sent, 'tile', split_axis=0, concat_axis=0, tiled=True)]
    all_to_all x1 -> x0, starting transfers between devices: 4.93 us -> none  [local(): lax.all_to_all(combine(received, sea_cols), 'comp', split_axis=0, concat_...]
    ppermute x1, waiting for transfers between devices: 0.01 us -> 4.05 us  [local(): left = lax.ppermute(high_edge, 'tile', forward)]
    squeeze x4 -> x0, local copies, waits for them, and re-layouts: 2.75 us -> none  [the longest x1 2.74 us: atm_edges(): return (split[:, 0], split[:, -1])]
  transfers between devices with their start and end apart: 6 -> 3, of which waited for: 1 -> 2; matrix products, arithmetic and copies ran while one was open for 5% -> 0% of each run, Pallas kernels for 44% -> 36%
where the time goes in v3:
time: 74.1 us; the launch traced here: 73.6 us
  Pallas kernels  38.1 us (51%)
  starting transfers between devices  13.9 us (19%)
  blocking collectives  11.6 us (16%)
  waiting for transfers between devices  9.08 us (12%)
  local copies, waits for them, and re-layouts  0.96 us (1%)
    pallas_call x1, Pallas kernels, dynamics(): pl.pallas_call(functools.partial(dynamics_kernel, sizes), out_shape=[jax....  17.5 us
    all_to_all x1, blocking collectives, local(): lax.all_to_all(combine(sea_flag, received, sizes), 'comp', split_axis=0,...  11.6 us
    pallas_call x1, Pallas kernels, remap(): pl.pallas_call(functools.partial(remap_kernel, sizes, n_tile, chunks), ou...  9.2 us
    pallas_call x1, Pallas kernels, update(): pl.pallas_call(functools.partial(update_kernel, sizes), out_shape=jax.Sha...  7.48 us
    ppermute x1, starting transfers between devices, local(): right = lax.ppermute(low_edge, 'tile', backward)  7.45 us
    all_to_all x1, waiting for transfers between devices, local(): lax.all_to_all(sent, 'tile', split_axis=0, concat_axis=0, tiled=True)  5.03 us
    all_to_all x1, starting transfers between devices, local(): lax.all_to_all(sent, 'tile', split_axis=0, concat_axis=0, tiled=True)  4.22 us
    ppermute x1, waiting for transfers between devices, local(): left = lax.ppermute(high_edge, 'tile', forward)  4.05 us
  transfers between devices with their start and end apart: 3, of which 2 were waited for; matrix products, arithmetic and copies ran while one was open for 0% of the time, Pallas kernels for 36%

profile of v3, /device:TPU:1, one launch (start us, length us, event | category | flops | bytes accessed | tf_op | source)
XLA Modules:
  0.0 73.6 jit_solution(16640588847009170049)
XLA Ops:
  0.0 3.3 %edges.1 = (f32[386,4,128]{2,1,0:T(4,128)}, f32[386,4,128]{2,1,0:T(4,128)}) custom-call(s32[1]{0:T(128)} %bitcast.sea_ref, f32[384,10,4,128]{3,2,1,0:T(4,128)} %bitcast.15, f32[320,12,4,128]{3,2,1,0:T(4,128)} %bitcast.16, s32[12,4,128]{2,1,0:T(4,128)} %bitcast.21), custom_call_target="tpu_custom_call" | custom-call | tf_op jit(solution)/shard_map/edges/pallas_call | solution.py:329
  3.3 2.2 %collective-permute-start = (f32[386,4,128]{2,1,0:T(4,128)}, f32[386,4,128]{2,1,0:T(4,128)S(1)}, u32[]{:S(2)}, u32[]{:S(2)}) collective-permute-start(f32[386,4,128]{2,1,0:T(4,128)} %get-tuple-element.16), channel_id=1, source_target_pairs={{0,1},{1,2},{2,3},{3,4},{4,5},{5,6},{6,7},{7,8},{8,9},{9,10},{10,1... | collective-permute-start | bytes 2371592 | tf_op jit(solution)/shard_map/ppermute | solution.py:636
  5.5 7.5 %collective-permute-start.1 = (f32[386,4,128]{2,1,0:T(4,128)}, f32[386,4,128]{2,1,0:T(4,128)}, u32[]{:S(2)}, u32[]{:S(2)}) collective-permute-start(f32[386,4,128]{2,1,0:T(4,128)} %get-tuple-element.17), channel_id=1, source_target_pairs={{1,0},{2,1},{3,2},{4,3},{5,4},{6,5},{7,6},{8,7},{9,8},{10,9},{11,1... | collective-permute-start | bytes 2371592 | tf_op jit(solution)/shard_map/ppermute | solution.py:637
  13.0 9.2 %remap.1 = f32[32,128,128]{2,1,0:T(8,128)} custom-call(s32[1]{0:T(128)} %bitcast.sea_ref, s32[1]{0:T(128)} %bitcast.9.place_ref, s32[1,256]{1,0:T(1,128)} %bitcast.25, s32[1,256]{1,0:T(1,128)} %bitcast.26, s32[1,256]{1,0:T(1,128)} %bitcast.27, f32[15360,128]{1,0:T(8,128)} %bitcast.17, bf16[4,64,128,128]{3,2,1,0:T(8,128)(2,1)} %bitcast.24), custom_call_target="tpu_custom_call" | custom-call | flops 8388608000 | bytes 8388608 | tf_op jit(solution)/shard_map/remap/pallas_call | solution.py:233
  22.2 4.2 %all-to-all-start = ((f32[32,128,128]{2,1,0:T(8,128)}), f32[32,128,128]{2,1,0:T(8,128)S(1)}, u32[]{:S(2)}, u32[]{:S(2)}) async-start(f32[32,128,128]{2,1,0:T(8,128)} %remap.1), calls=%async_computation | async-start | bytes 4194304 | tf_op jit(solution)/shard_map/all_to_all | solution.py:650
  26.4 4.0 %collective-permute-done = f32[386,4,128]{2,1,0:T(4,128)S(1)} collective-permute-done((f32[386,4,128]{2,1,0:T(4,128)}, f32[386,4,128]{2,1,0:T(4,128)S(1)}, u32[]{:S(2)}, u32[]{:S(2)}) %collective-permute-start) | collective-permute-done | bytes 790560 | tf_op jit(solution)/shard_map/ppermute | solution.py:636
  30.4 0.0 copy-start
  30.4 0.0 collective-permute-done.1
  30.4 1.0 %copy-done = f32[386,4,128]{2,1,0:T(4,128)} copy-done((f32[386,4,128]{2,1,0:T(4,128)}, f32[386,4,128]{2,1,0:T(4,128)S(1)}, u32[]{:S(2)}) %copy-start) | copy-done | bytes 790552
  31.4 17.5 %dynamics.1 = (f32[15360,128]{1,0:T(8,128)}, f32[384,128]{1,0:T(8,128)}) custom-call(s32[1]{0:T(128)} %bitcast.sea_ref, f32[15360,128]{1,0:T(8,128)} %bitcast.18, f32[1544,128]{1,0:T(8,128)} %bitcast.19, f32[1544,128]{1,0:T(8,128)} %bitcast.7.right_ref.rest_5_, f32[3,128,128]{2,1,0:T(8,128)} %atm_ref.1, f32[4,80,80]{2,1,0:T(8,128)} %ocean_ref.1, ...), custom_call_target="tpu_custom_call" | custom-call | flops 25165824000 | bytes 31457280 | tf_op jit(solution)/shard_map/dynamics/pallas_call | solution.py:461
  48.9 5.0 %all-to-all-done.recv_ref = f32[32,128,128]{2,1,0:T(8,128)S(1)} async-done(((f32[32,128,128]{2,1,0:T(8,128)}), f32[32,128,128]{2,1,0:T(8,128)S(1)}, u32[]{:S(2)}, u32[]{:S(2)}) %all-to-all-start) | async-done | bytes 2097184 | tf_op jit(solution)/shard_map/all_to_all | solution.py:650
  54.0 0.6 combine.1
  54.6 11.6 %all_to_all.10.rest_2_ = f32[4,3,56,128]{3,2,1,0:T(8,128)} all-to-all(f32[4,3,56,128]{3,2,1,0:T(8,128)S(1)} %combine.1), channel_id=1, replica_groups=mesh['comp'=4,'tile'=32] {'comp'}, dimensions={0} | all-to-all | bytes 688128 | tf_op jit(solution)/shard_map/all_to_all | solution.py:660
  66.2 7.5 %update.1 = f32[15360,128]{1,0:T(8,128)} custom-call(s32[1]{0:T(128)} %bitcast.sea_ref, f32[384,128]{1,0:T(8,128)} %get-tuple-element.18.rest_0_, f32[15360,128]{1,0:T(8,128)} %get-tuple-element.21.rest_1_, f32[4,3,56,128]{3,2,1,0:T(8,128)} %all_to_all.10.rest_2_, s32[48,128]{1,0:T(8,128)} %bitcast.23, f32[1544,128]{1,0:T(8,128)} %bitcast.20, ...), custom_call_target="tpu_custom_call" | custom-call | flops 3932160 | bytes 15728640 | tf_op jit(solution)/shard_map/update/pallas_call | solution.py:595
Async XLA Ops:
  3.3 27.1 %collective-permute-start = (f32[386,4,128]{2,1,0:T(4,128)}, f32[386,4,128]{2,1,0:T(4,128)S(1)}, u32[]{:S(2)}, u32[]{:S(2)}) collective-permute-start(f32[386,4,128]{2,1,0:T(4,128)} %get-tuple-element.16), channel_id=1, source_target_pairs={{0,1},{1,2},{2,3},{3,4},{4,5},{5,6},{6,7},{7,8},{8,9},{9,10},{10,1... | collective-permute-start | bytes 2371592 | tf_op jit(solution)/shard_map/ppermute | solution.py:636
  5.5 24.9 %collective-permute-start.1 = (f32[386,4,128]{2,1,0:T(4,128)}, f32[386,4,128]{2,1,0:T(4,128)}, u32[]{:S(2)}, u32[]{:S(2)}) collective-permute-start(f32[386,4,128]{2,1,0:T(4,128)} %get-tuple-element.17), channel_id=1, source_target_pairs={{1,0},{2,1},{3,2},{4,3},{5,4},{6,5},{7,6},{8,7},{9,8},{10,9},{11,1... | collective-permute-start | bytes 2371592 | tf_op jit(solution)/shard_map/ppermute | solution.py:637
  22.2 31.8 %all-to-all-start = ((f32[32,128,128]{2,1,0:T(8,128)}), f32[32,128,128]{2,1,0:T(8,128)S(1)}, u32[]{:S(2)}, u32[]{:S(2)}) async-start(f32[32,128,128]{2,1,0:T(8,128)} %remap.1), calls=%async_computation | async-start | bytes 4194304 | tf_op jit(solution)/shard_map/all_to_all | solution.py:650
  30.4 1.0 %copy-start = (f32[386,4,128]{2,1,0:T(4,128)}, f32[386,4,128]{2,1,0:T(4,128)S(1)}, u32[]{:S(2)}) copy-start(f32[386,4,128]{2,1,0:T(4,128)S(1)} %collective-permute-done) | copy-start | bytes 2371588

commit v4 on v3

--- a/solution.py
+++ b/solution.py
@@ -2,7 +2,6 @@
 
 import jax
 import jax.numpy as jnp
-import numpy as np
 from jax import lax
 from jax.experimental import pallas as pl
 from jax.experimental.pallas import tpu as pltpu
@@ -20,11 +19,13 @@
 NU_OCEAN = 0.015
 
 HALO = 4
-EDGE_ROWS = 3 * 2 * HALO
+EDGE_ROWS = 2 * HALO
 FIELD_ROWS = CAP + EDGE_ROWS
-CHUNK_ROWS = FA * FIELD_ROWS + 8
+MAIN_ROWS = FA * FIELD_ROWS + 8
+CHUNK_ROWS = MAIN_ROWS + FA * EDGE_ROWS
 MIB = 1 << 20
-SIDE = (4, 5)
+LIMIT = 52
+SIDE = (8, 5)
 
 
 def split_two(value):
@@ -33,9 +34,15 @@
 
 
 def row_operator():
-    u = np.eye(R, k=1) + np.eye(R, k=-1) - 4.0 * np.eye(R)
-    both = np.concatenate([2.0 * u, u @ u + 2.0 * np.eye(R)], axis=1)
-    return jnp.asarray(np.concatenate([both, both], axis=0), jnp.bfloat16)
+    row = lax.broadcasted_iota(jnp.int32, (R, R), 0)
+    lane = lax.broadcasted_iota(jnp.int32, (R, R), 1)
+    apart = jnp.abs(row - lane)
+    u = jnp.where(apart == 0, -4.0, jnp.where(apart == 1, 1.0, 0.0))
+    ends = jnp.where((row == 0) | (row == R - 1), 1.0, 0.0)
+    squared = jnp.where(apart == 1, -8.0, jnp.where(apart == 2, 1.0, 0.0))
+    squared = jnp.where(apart == 0, 20.0 - ends, squared)
+    both = jnp.concatenate([2.0 * u, squared], axis=1).astype(jnp.bfloat16)
+    return jnp.concatenate([both, both], axis=0)
 
 
 def apply_filter(value, column_sums, row_parts, nu):
@@ -97,7 +104,7 @@
 
 
 def remap_kernel(
-    sizes, n_tile, chunks, sea_ref, place_ref, source_ref, tile_ref, slot_ref, x_ref, w_ref, out_ref, w_vmem, surf_ref, pick_ref, part_ref, w_sems, x_sems
+    sizes, n_tile, chunks, sea_ref, place_ref, source_ref, tile_ref, slot_ref, x_ref, w_ref, out_ref, third_ref, w_vmem, surf_ref, pick_ref, part_ref, w_sems, x_sems
 ):
     atm_cols, sea_cols = sizes
     entries = source_ref.shape[1]
@@ -148,12 +155,12 @@
     edge_tile = jnp.where(block < HALO, tile_number + n_tile - 1, tile_number + 1)
     edge_tile = jnp.where(edge_tile >= n_tile, edge_tile - n_tile, edge_tile)
     edge_row = jnp.where(block < HALO, block + HALO, block - high_start)
-    edge_row = edge_tile * EDGE_ROWS + jnp.where(is_sea, group, 0) * (2 * HALO) + edge_row
+    edge_row = (jnp.where(is_sea, group, 0) * n_tile + edge_tile) * EDGE_ROWS + edge_row
     on_edge = (block < HALO) | (block >= high_start)
     edge_slot = jnp.where(on_edge, edge_row, -1).astype(jnp.float32)
-    tail = CHUNK_ROWS - FA * FIELD_ROWS
+    tail = MAIN_ROWS - FA * FIELD_ROWS
     for t in range(n_tile):
-        out_ref[t, FA * FIELD_ROWS :, :] = jnp.concatenate(
+        out_ref[t, FA * FIELD_ROWS : MAIN_ROWS, :] = jnp.concatenate(
             [codes[t : t + 1], jnp.zeros((tail - 1, R), jnp.float32)], axis=0
         )
 
@@ -211,30 +218,38 @@
     slot = tile * CAP + rank
     slots = lax.broadcasted_iota(jnp.int32, (n_tile * CAP, entries), 0).astype(jnp.float32)
     placer = ones_where(slots == slot)
-    edge_slots = lax.broadcasted_iota(jnp.int32, (n_tile * EDGE_ROWS, entries), 0).astype(jnp.float32)
+    edge_slots = lax.broadcasted_iota(jnp.int32, (3 * n_tile * EDGE_ROWS, entries), 0).astype(jnp.float32)
     edge_placer = ones_where(edge_slots == edge_slot)
     for f in range(FA):
         high, low = split_two(part_ref[f * entries : (f + 1) * entries, :])
         values = jnp.concatenate([high, low], axis=1)
         start = f * FIELD_ROWS
-        for place_matrix, size in ((placer, CAP), (edge_placer, EDGE_ROWS)):
-            both = jnp.dot(place_matrix, values, preferred_element_type=jnp.float32)
-            placed = both[:, :R] + both[:, R:]
-            for t in range(n_tile):
-                out_ref[t, start : start + size, :] = placed[t * size : (t + 1) * size]
-            start += size
+        own, edge = (
+            both[:, :R] + both[:, R:]
+            for both in (
+                jnp.dot(matrix, values, preferred_element_type=jnp.float32) for matrix in (placer, edge_placer)
+            )
+        )
+        for t in range(n_tile):
+            out_ref[t, start : start + CAP, :] = own[t * CAP : (t + 1) * CAP]
+            for n, (ref, at) in enumerate(((out_ref, start + CAP), (out_ref, MAIN_ROWS + f * EDGE_ROWS), (third_ref, f * EDGE_ROWS))):
+                row = (n * n_tile + t) * EDGE_ROWS
+                ref[t, at : at + EDGE_ROWS, :] = edge[row : row + EDGE_ROWS]
 
 
 def remap(is_sea, place, source, tile, slot, x, weights, n_tile, sizes):
     entries = weights.shape[0]
-    chunks = 8
+    chunks = 4
     vmem = pl.BlockSpec(memory_space=pltpu.VMEM)
-    anywhere = pl.BlockSpec(memory_space=pl.ANY)
+    hbm = pl.BlockSpec(memory_space=pltpu.HBM)
     return pl.pallas_call(
         functools.partial(remap_kernel, sizes, n_tile, chunks),
-        out_shape=jax.ShapeDtypeStruct((n_tile, CHUNK_ROWS, R), jnp.float32),
-        in_specs=[pl.BlockSpec(memory_space=pltpu.SMEM)] * 2 + [vmem, vmem, vmem, anywhere, anywhere],
-        out_specs=vmem,
+        out_shape=[
+            jax.ShapeDtypeStruct((n_tile, rows, R), jnp.float32)
+            for rows in (CHUNK_ROWS, FA * EDGE_ROWS)
+        ],
+        in_specs=[pl.BlockSpec(memory_space=pltpu.SMEM)] * 2 + [vmem, vmem, vmem, hbm, hbm],
+        out_specs=[vmem] * 2,
         scratch_shapes=[
             pltpu.VMEM((4, entries // 4, R, R), jnp.bfloat16),
             pltpu.VMEM((FA * sizes[1], R), jnp.float32),
@@ -243,7 +258,7 @@
             pltpu.SemaphoreType.DMA((chunks,)),
             pltpu.SemaphoreType.DMA((FA,)),
         ],
-        compiler_params=pltpu.CompilerParams(vmem_limit_bytes=56 * MIB),
+        compiler_params=pltpu.CompilerParams(vmem_limit_bytes=LIMIT * MIB),
         cost_estimate=pl.CostEstimate(
             flops=2000 * entries * R * R, bytes_accessed=weights.size * 2, transcendentals=0
         ),
@@ -251,9 +266,32 @@
     )(is_sea, place, source, tile, slot, x, weights.reshape(4, entries // 4, R, R))
 
 
-def combine_kernel(sizes, sea_ref, recv_ref, out_ref):
+def join_kernel(comp_ref, sent_ref, handed_ref, out_ref, sem):
+    @pl.when(comp_ref[0] == 2)
+    def _():
+        copy = pltpu.make_async_copy(handed_ref, out_ref.at[:, pl.ds(MAIN_ROWS, FA * EDGE_ROWS)], sem)
+        copy.start()
+        copy.wait()
+
+
+def join(comp, sent, handed):
+    hbm = pl.BlockSpec(memory_space=pltpu.HBM)
+    return pl.pallas_call(
+        join_kernel,
+        out_shape=jax.ShapeDtypeStruct(sent.shape, jnp.float32),
+        in_specs=[pl.BlockSpec(memory_space=pltpu.SMEM), hbm, pl.BlockSpec(memory_space=pltpu.VMEM)],
+        out_specs=hbm,
+        input_output_aliases={1: 0},
+        scratch_shapes=[pltpu.SemaphoreType.DMA(())],
+        compiler_params=pltpu.CompilerParams(vmem_limit_bytes=LIMIT * MIB),
+        cost_estimate=pl.CostEstimate(flops=0, bytes_accessed=0, transcendentals=0),
+        name="join",
+    )(comp, sent, handed)
+
+
+def combine_kernel(sizes, comp_ref, recv_ref, first_ref, keep_ref, mine_ref, share_ref):
     atm_cols, sea_cols = sizes
-    n_tile, per_group = recv_ref.shape[0], out_ref.shape[2]
+    n_tile, per_group = recv_ref.shape[0], share_ref.shape[2]
     rows = 4 * per_group
     spots = lax.broadcasted_iota(jnp.int32, (rows, R), 0).astype(jnp.float32) + 1.0
     total = [jnp.zeros((rows, R), jnp.float32) for _ in range(FA)]
@@ -270,37 +308,61 @@
             total[f] = total[f] + (both[:, :R] + both[:, R:])
     for f in range(FA):
         for c in range(4):
-            out_ref[c, f] = total[f][c * per_group : (c + 1) * per_group]
+            share_ref[c, f] = total[f][c * per_group : (c + 1) * per_group]
+    comp = comp_ref[0]
+    mine_ref[...] = jnp.zeros_like(mine_ref)
     for f in range(FA):
-        start = f * FIELD_ROWS + CAP
-        edge = jnp.sum(recv_ref[:, start : start + EDGE_ROWS, :], axis=0)
-
-        @pl.when(sea_ref[0] == 0)
-        def _(f=f, edge=edge):
-            out_ref[3, f, 0:HALO, :] = edge[0:HALO]
-            out_ref[3, f, HALO + sea_cols : 2 * HALO + sea_cols, :] = edge[HALO : 2 * HALO]
-
-        @pl.when(sea_ref[0] != 0)
-        def _(f=f, edge=edge):
-            for c in range(3):
-                first = c * 2 * HALO
-                out_ref[c, f, 0:HALO, :] = edge[first : first + HALO]
-                out_ref[c, f, HALO + atm_cols : 2 * HALO + atm_cols, :] = edge[first + HALO : first + 2 * HALO]
-
-
-def combine(is_sea, recv, sizes):
+        starts = (f * FIELD_ROWS + CAP, MAIN_ROWS + f * EDGE_ROWS)
+        edge, extra = (jnp.sum(recv_ref[:, at : at + EDGE_ROWS, :], axis=0) for at in starts)
+
+        def place(ref, cols, rows, f=f):
+            ref[f, 0:HALO, :] = rows[:HALO]
+            ref[f, HALO + cols : 2 * HALO + cols, :] = rows[HALO:]
+
+        @pl.when(comp != 3)
+        def _(place=place, edge=edge):
+            place(share_ref.at[3], sea_cols, edge)
+
+        @pl.when(comp == 2)
+        def _(place=place, extra=extra):
+            place(mine_ref, atm_cols, extra)
+
+        @pl.when(comp == 3)
+        def _(place=place, edge=edge, extra=extra):
+            place(share_ref.at[0], atm_cols, edge)
+            place(share_ref.at[1], atm_cols, extra)
+
+    @pl.when(comp == 3)
+    def _():
+        first_ref[0] = share_ref[0]
+        first_ref[1] = share_ref[2]
+        keep_ref[...] = share_ref[1]
+
+    @pl.when(comp != 3)
+    def _():
+        ocean = share_ref[3]
+        first_ref[0] = jnp.where(comp == 1, 0.0, ocean)
+        first_ref[1] = jnp.zeros_like(ocean)
+        keep_ref[...] = jnp.where(comp == 1, ocean, 0.0)
+
+
+def combine(comp, recv, sizes):
     vmem = pl.BlockSpec(memory_space=pltpu.VMEM)
+    shape = (FA, sizes[1] + 2 * HALO, R)
     return pl.pallas_call(
         functools.partial(combine_kernel, sizes),
-        out_shape=jax.ShapeDtypeStruct((4, FA, sizes[1] + 2 * HALO, R), jnp.float32),
+        out_shape=[jax.ShapeDtypeStruct(s, jnp.float32) for s in ((2,) + shape, shape, shape)],
         in_specs=[pl.BlockSpec(memory_space=pltpu.SMEM), vmem],
-        out_specs=vmem,
+        out_specs=[vmem] * 3,
+        scratch_shapes=[pltpu.VMEM((4,) + shape, jnp.float32)],
         compiler_params=pltpu.CompilerParams(vmem_limit_bytes=16 * MIB),
         name="combine",
-    )(is_sea, recv)
-
-
-def edges_kernel(sea_ref, x_atm_ref, x_sea_ref, mask_ref, low_ref, high_ref, sems):
+    )(comp, recv)
+
+
+def edges_kernel(sea_ref, x_atm_ref, x_sea_ref, mask_hbm, low_ref, high_ref, mask_ref, sems):
+    mask_copy = pltpu.make_async_copy(mask_hbm, mask_ref, sems.at[2])
+    mask_copy.start()
     for sea, x_ref in ((False, x_atm_ref), (True, x_sea_ref)):
         count, blocks = x_ref.shape[0], x_ref.shape[1]
 
@@ -312,6 +374,7 @@
             ]
             for copy in copies:
                 copy.start()
+            mask_copy.wait()
             for ref, block in ((low_ref, 0), (high_ref, blocks - 1)):
                 if count < FA * LA:
                     ref[count : FA * LA] = jnp.zeros((FA * LA - count, HALO, R), jnp.float32)
@@ -323,16 +386,16 @@
 
 def edge_columns(is_sea, state, mask, sizes):
     atm_cols, sea_cols = sizes
-    anywhere = pl.BlockSpec(memory_space=pl.ANY)
+    hbm = pl.BlockSpec(memory_space=pltpu.HBM)
     vmem = pl.BlockSpec(memory_space=pltpu.VMEM)
     shape = jax.ShapeDtypeStruct((FA * LA + 2, HALO, R), jnp.float32)
     return pl.pallas_call(
         edges_kernel,
         out_shape=[shape, shape],
-        in_specs=[pl.BlockSpec(memory_space=pltpu.SMEM), anywhere, anywhere, vmem],
+        in_specs=[pl.BlockSpec(memory_space=pltpu.SMEM), hbm, hbm, hbm],
         out_specs=[vmem, vmem],
-        scratch_shapes=[pltpu.SemaphoreType.DMA((2,))],
-        compiler_params=pltpu.CompilerParams(vmem_limit_bytes=56 * MIB),
+        scratch_shapes=[pltpu.VMEM((sea_cols // HALO, HALO, R), jnp.int32), pltpu.SemaphoreType.DMA((3,))],
+        compiler_params=pltpu.CompilerParams(vmem_limit_bytes=LIMIT * MIB),
         name="edges",
     )(
         is_sea,
@@ -354,8 +417,8 @@
 
 
 def dynamics_part(
-    fields, levels, cols, surface, side, nu, x_ref, left_ref, right_ref, matrix_ref, mask_ref, op_ref, out_ref, column_ref,
-    x_vmem, out_vmem, y_vmem, lhs_ref, mid_ref, mask_vmem, in_sems, out_sems
+    fields, levels, cols, surface, side, nu, x_ref, left_ref, right_ref, matrix_ref, masked, mask_ref, out_ref, column_ref,
+    mask_vmem, x_vmem, out_vmem, op_ref, y_vmem, lhs_ref, mid_ref, in_sems, out_sems
 ):
     rows = levels * cols
 
@@ -368,13 +431,17 @@
         return pltpu.make_async_copy(out_vmem.at[span], out_ref.at[span], out_sems.at[f])
 
     read(0).start()
+    op_ref[...] = row_operator()
+    spare = FA * LA * HALO
+    mask_vmem[0:HALO, :] = jnp.zeros((HALO, R), jnp.float32)
+    mask_vmem[HALO : 2 * HALO, :] = left_ref[spare : spare + HALO, :]
+    mask_vmem[8 : 8 + cols, :] = mask_ref[:cols].astype(jnp.float32)
+    mask_vmem[8 + cols : 8 + HALO + cols, :] = right_ref[spare : spare + HALO, :]
+    tail = mask_vmem.shape[0] - 8 - HALO - cols
+    mask_vmem[8 + HALO + cols :, :] = jnp.zeros((tail, R), jnp.float32)
     mask = None
-    if mask_ref is not None:
-        spare = FA * LA * HALO
-        mask_vmem[0:HALO, :] = left_ref[spare : spare + HALO, :]
-        mask_vmem[HALO : HALO + cols, :] = mask_ref[...].astype(jnp.float32)
-        mask_vmem[HALO + cols : 2 * HALO + cols, :] = right_ref[spare : spare + HALO, :]
-        mask = lambda k: jnp.broadcast_to(mask_vmem[k + HALO : k + HALO + 1, :], (16, R))
+    if masked:
+        mask = lambda k: jnp.broadcast_to(mask_vmem[k + 8 : k + 9, :], (16, R))
 
     def field(f, carry):
         squared = jnp.dot(
@@ -436,26 +503,26 @@
 
 
 def dynamics_kernel(
-    sizes, sea_ref, x_ref, left_ref, right_ref, atm_ref, ocean_ref, mask_ref, op_ref, *rest
+    sizes, sea_ref, x_ref, left_ref, right_ref, atm_ref, ocean_ref, mask_ref, *rest
 ):
     atm_cols, sea_cols = sizes
 
     @pl.when(sea_ref[0] == 0)
     def _():
         dynamics_part(
-            FA, LA, atm_cols, LA - 1, SIDE[0], NU_ATMOS, x_ref, left_ref, right_ref, atm_ref, None, op_ref, *rest
+            FA, LA, atm_cols, LA - 1, SIDE[0], NU_ATMOS, x_ref, left_ref, right_ref, atm_ref, False, mask_ref, *rest
         )
 
     @pl.when(sea_ref[0] != 0)
     def _():
         dynamics_part(
-            FO, LO, sea_cols, 0, SIDE[1], NU_OCEAN, x_ref, left_ref, right_ref, ocean_ref, mask_ref, op_ref, *rest
+            FO, LO, sea_cols, 0, SIDE[1], NU_OCEAN, x_ref, left_ref, right_ref, ocean_ref, True, mask_ref, *rest
         )
 
 
 def dynamics(is_sea, x, left, right, atm_mixing, ocean_mixing, mask, sizes):
     vmem = pl.BlockSpec(memory_space=pltpu.VMEM)
-    anywhere = pl.BlockSpec(memory_space=pl.ANY)
+    hbm = pl.BlockSpec(memory_space=pltpu.HBM)
     rows = x.shape[0]
     widest = max(sizes)
     return pl.pallas_call(
@@ -463,25 +530,26 @@
         out_shape=[
             jax.ShapeDtypeStruct((rows, R), jnp.float32),
             jax.ShapeDtypeStruct((FA * LA, R), jnp.float32),
+            jax.ShapeDtypeStruct((widest + 16, R), jnp.float32),
         ],
-        in_specs=[pl.BlockSpec(memory_space=pltpu.SMEM), anywhere] + [vmem] * 6,
-        out_specs=[anywhere, vmem],
+        in_specs=[pl.BlockSpec(memory_space=pltpu.SMEM), hbm] + [vmem] * 5,
+        out_specs=[hbm, vmem, vmem],
         scratch_shapes=[
             pltpu.VMEM((rows, R), jnp.float32),
             pltpu.VMEM((rows, R), jnp.float32),
+            pltpu.VMEM((2 * R, 2 * R), jnp.bfloat16),
             pltpu.VMEM((2 * LA, widest * R), jnp.bfloat16),
             pltpu.VMEM((max(SIDE), 2, (widest + 6) * 16, 2 * R), jnp.bfloat16),
             pltpu.VMEM((max(SIDE), (widest + 4) * 16, R), jnp.float32),
-            pltpu.VMEM((widest + 2 * HALO, R), jnp.float32),
             pltpu.SemaphoreType.DMA((FO,)),
             pltpu.SemaphoreType.DMA((FO,)),
         ],
-        compiler_params=pltpu.CompilerParams(vmem_limit_bytes=56 * MIB),
+        compiler_params=pltpu.CompilerParams(vmem_limit_bytes=LIMIT * MIB),
         cost_estimate=pl.CostEstimate(
             flops=100 * rows * R * R, bytes_accessed=16 * rows * R, transcendentals=0
         ),
         name="dynamics",
-    )(is_sea, x, left, right, atm_mixing, ocean_mixing, mask, row_operator())
+    )(is_sea, x, left, right, atm_mixing, ocean_mixing, mask)
 
 
 def lane_edges(rows):
@@ -496,7 +564,7 @@
     return (before + after) + (down + up) - 4.0 * middle
 
 
-def filter_forcing(cols, nu, shares_ref, masked, mask_ref, work_ref, g_ref):
+def filter_forcing(cols, nu, forcing_of, masked, mask_ref, work_ref, g_ref):
     lo, hi, rows = 8, 8 + cols, cols + 16
     edges = lane_edges(rows)
     mask = mask_ref[0:rows, :]
@@ -505,9 +573,8 @@
         return lap(pltpu.roll(v, 1, 0), v, pltpu.roll(v, rows - 1, 0), edges)
 
     for f in range(FA):
-        forcing = (shares_ref[0, f] + shares_ref[1, f]) + (shares_ref[2, f] + shares_ref[3, f])
         work_ref[0:rows, :] = jnp.zeros((rows, R), jnp.float32)
-        work_ref[lo - HALO : hi + HALO, :] = COUPLE_RATE * forcing[: cols + 2 * HALO]
+        work_ref[lo - HALO : hi + HALO, :] = COUPLE_RATE * forcing_of(f)
         value = work_ref[0:rows, :] * mask
         for _ in range(2):
             value = value - nu * along(along(value))
@@ -517,40 +584,27 @@
 
 
 def update_part(
-    cols, levels, fields, pieces, masked, nu, column_ref, part_ref, shares_ref, mask_ref, left_ref, right_ref, out_ref,
-    work_ref, g_ref, mask_vmem, stage_ref, in_sems, out_sems, mask_sems
+    cols, levels, fields, pieces, masked, nu, comp_ref, column_ref, part_ref, first_ref, second_ref, mine_ref, mask_ref, out_ref,
+    work_ref, g_ref, stage_ref, out_sems
 ):
     per_piece = fields * levels // pieces
     rows = per_piece * cols
 
-    def read(p):
-        span = pl.ds(pl.multiple_of(p * rows, 8), rows)
-        return pltpu.make_async_copy(part_ref.at[span], stage_ref.at[span], in_sems.at[p])
-
     def write(p):
         span = pl.ds(pl.multiple_of(p * rows, 8), rows)
         return pltpu.make_async_copy(stage_ref.at[span], out_ref.at[span], out_sems.at[p])
 
-    span = pl.ds(FA * LA * HALO, 8)
-    ends = [
-        pltpu.make_async_copy(left_ref.at[span], mask_vmem.at[pl.ds(64, 8)], mask_sems.at[0]),
-        pltpu.make_async_copy(right_ref.at[span], mask_vmem.at[pl.ds(72, 8)], mask_sems.at[1]),
-    ]
-    for copy in ends:
-        copy.start()
-    for p in range(pieces):
-        read(p).start()
-    mask_vmem[0:8, :] = jnp.zeros((8, R), jnp.float32)
-    mask_vmem[8 : 8 + cols, :] = mask_ref[:cols].astype(jnp.float32)
-    mask_vmem[8 + cols : 16 + cols, :] = jnp.zeros((8, R), jnp.float32)
-    for copy in ends:
-        copy.wait()
-    mask_vmem[8 - HALO : 8, :] = mask_vmem[64 : 64 + HALO, :]
-    mask_vmem[8 + cols : 8 + HALO + cols, :] = mask_vmem[72 : 72 + HALO, :]
-    filter_forcing(cols, nu, shares_ref, masked, mask_vmem, work_ref, g_ref)
+    wide = cols + 2 * HALO
+
+    def forcing_of(f):
+        if fields == FO:
+            return first_ref[0, f, :wide] + second_ref[f, :wide]
+        own = first_ref[1, f, :wide] + mine_ref[f, :wide]
+        return jnp.where(comp_ref[0] == 2, own, 0.0) + second_ref[f, :wide]
+
+    filter_forcing(cols, nu, forcing_of, masked, mask_ref, work_ref, g_ref)
 
     def piece(p, carry):
-        read(p).wait()
         field = p * per_piece // levels
 
         @pl.when(field < FA)
@@ -562,10 +616,15 @@
                 factor = jnp.broadcast_to(column_ref[pl.ds(number, 1), :], (8, R))
                 for v in range(cols // 8):
                     span = pl.ds(pl.multiple_of(number * cols + v * 8, 8), 8)
-                    stage_ref[span, :] = stage_ref[span, :] + factor * pushed[v]
+                    stage_ref[span, :] = part_ref[span, :] + factor * pushed[v]
                 return carry
 
             lax.fori_loop(0, per_piece, group, 0, unroll=8)
+
+        @pl.when(field >= FA)
+        def _():
+            span = pl.ds(pl.multiple_of(p * rows, 8), rows)
+            stage_ref[span, :] = part_ref[span, :]
 
         write(p).start()
         return carry
@@ -575,43 +634,65 @@
         write(p).wait()
 
 
-def update_kernel(sizes, sea_ref, *rest):
+def fetch_kernel(part_ref, after_ref, out_ref, sems):
+    rows = part_ref.shape[0] // 8
+    copies = []
+    for p in range(8):
+        span = pl.ds(p * rows, rows)
+        copies.append(pltpu.make_async_copy(part_ref.at[span], out_ref.at[span], sems.at[p]))
+        copies[-1].start()
+    for copy in copies:
+        copy.wait()
+
+
+def fetch(part, after):
+    vmem = pl.BlockSpec(memory_space=pltpu.VMEM)
+    hbm = pl.BlockSpec(memory_space=pltpu.HBM)
+    return pl.pallas_call(
+        fetch_kernel,
+        out_shape=pltpu.VMEM(part.shape, jnp.float32),
+        in_specs=[hbm, hbm],
+        out_specs=vmem,
+        scratch_shapes=[pltpu.SemaphoreType.DMA((8,))],
+        compiler_params=pltpu.CompilerParams(vmem_limit_bytes=40 * MIB),
+        cost_estimate=pl.CostEstimate(flops=0, bytes_accessed=4 * part.size, transcendentals=0),
+        name="fetch",
+    )(part, after)
+
+
+def update_kernel(sizes, comp_ref, *rest):
     atm_cols, sea_cols = sizes
 
-    @pl.when(sea_ref[0] == 0)
+    @pl.when(comp_ref[0] != 3)
     def _():
-        update_part(atm_cols, LA, FA, 4 * FA, False, NU_ATMOS, *rest)
-
-    @pl.when(sea_ref[0] != 0)
+        update_part(atm_cols, LA, FA, 4 * FA, False, NU_ATMOS, comp_ref, *rest)
+
+    @pl.when(comp_ref[0] == 3)
     def _():
-        update_part(sea_cols, LO, FO, 2 * FO, True, NU_OCEAN, *rest)
-
-
-def update(is_sea, column, part, shares, mask, left, right, sizes):
+        update_part(sea_cols, LO, FO, 2 * FO, True, NU_OCEAN, comp_ref, *rest)
+
+
+def update(comp, column, part, first, second, mine, mask, sizes):
     vmem = pl.BlockSpec(memory_space=pltpu.VMEM)
-    smem = pl.BlockSpec(memory_space=pltpu.SMEM)
-    anywhere = pl.BlockSpec(memory_space=pl.ANY)
+    hbm = pl.BlockSpec(memory_space=pltpu.HBM)
     rows = part.shape[0]
     return pl.pallas_call(
         functools.partial(update_kernel, sizes),
         out_shape=jax.ShapeDtypeStruct((rows, R), jnp.float32),
-        in_specs=[smem, vmem, anywhere, vmem, vmem, anywhere, anywhere],
-        out_specs=anywhere,
+        in_specs=[pl.BlockSpec(memory_space=pltpu.SMEM)] + [vmem] * 6,
+        out_specs=hbm,
         scratch_shapes=[
             pltpu.VMEM((max(sizes) + 16, R), jnp.float32),
             pltpu.VMEM((FA, max(sizes), R), jnp.float32),
-            pltpu.VMEM((80, R), jnp.float32),
             pltpu.VMEM((rows, R), jnp.float32),
             pltpu.SemaphoreType.DMA((4 * FA,)),
-            pltpu.SemaphoreType.DMA((4 * FA,)),
-            pltpu.SemaphoreType.DMA((2,)),
         ],
-        compiler_params=pltpu.CompilerParams(vmem_limit_bytes=56 * MIB),
+        compiler_params=pltpu.CompilerParams(vmem_limit_bytes=40 * MIB),
         cost_estimate=pl.CostEstimate(
             flops=2 * rows * R, bytes_accessed=8 * rows * R, transcendentals=0
         ),
         name="update",
-    )(is_sea, column, part, shares, mask, left, right)
+    )(comp, column, part, first, second, mine, mask)
 
 
 def local(
@@ -636,7 +717,7 @@
     left = lax.ppermute(high_edge, "tile", forward)
     right = lax.ppermute(low_edge, "tile", backward)
 
-    sent = remap(
+    sent, third = remap(
         sea_flag,
         lax.axis_index("tile").reshape(1),
         source_slot.reshape(1, -1),
@@ -647,18 +728,24 @@
         n_tile,
         sizes,
     )
-    received = lax.all_to_all(
-        sent, "tile", split_axis=0, concat_axis=0, tiled=True
-    )
+    comp = lax.axis_index("comp")
+    handed = lax.ppermute(third, "comp", [(3, 2)])
+    comp_flag = comp.reshape(1)
+    sent = join(comp_flag, sent, handed)
+    received = lax.all_to_all(sent, "tile", split_axis=0, concat_axis=0, tiled=True)
 
     x = state.reshape(-1, R)
     flat_left = left.reshape(-1, R)
     flat_right = right.reshape(-1, R)
-    part, column = dynamics(sea_flag, x, flat_left, flat_right, atm_mixing, ocean_mixing, mask, sizes)
+    part, column, wide_mask = dynamics(sea_flag, x, flat_left, flat_right, atm_mixing, ocean_mixing, mask, sizes)
 
     received, part = lax.optimization_barrier((received, part))
-    shares = lax.all_to_all(combine(sea_flag, received, sizes), "comp", split_axis=0, concat_axis=0, tiled=True)
-    done = update(sea_flag, column, part, shares, mask, flat_left, flat_right, sizes)
+    first, keep, mine = combine(comp_flag, received, sizes)
+    other_core = lax.ppermute(first, "comp", [(0, 1), (1, 0), (2, 3), (3, 2)])
+    onward = keep + jnp.where(comp == 3, 0.0, other_core[0])
+    other_chip = lax.ppermute(onward, "comp", [(0, 2), (2, 0), (1, 3), (3, 1)])
+    part = fetch(part, onward)
+    done = update(comp_flag, column, part, other_core, other_chip, mine, wide_mask, sizes)
     return done.reshape(1, 1, -1)
 
 

time: 74.1 us -> 63.4 us (0.86)
  blocking collectives: 11.6 us -> 0 us
  Pallas kernels: 38.1 us -> 31.8 us
  starting transfers between devices: 13.9 us -> 19.8 us
  local copies, waits for them, and re-layouts: 0.96 us -> 2.59 us
    all_to_all x1 -> x0, blocking collectives: 11.6 us -> none  [local(): lax.all_to_all(combine(sea_flag, received, sizes), 'comp', split_axis=0,...]
    ppermute x0 -> x3, starting transfers between devices: none -> 5.92 us  [the longest x1 3.03 us: local(): other_chip = lax.ppermute(onward, 'comp', [(0, 2), (2, 0), (1, 3), (3, 1)])]
    all_to_all x1, waiting for transfers between devices: 5.03 us -> 1.07 us  [local(): lax.all_to_all(sent, 'tile', split_axis=0, concat_axis=0, tiled=True)]
    pallas_call x1, Pallas kernels: 7.48 us -> 3.7 us  [update(): pl.pallas_call(functools.partial(update_kernel, sizes), out_shape=jax.Sha...]
    pallas_call x1 -> x3, Pallas kernels: 0.59 us -> 3.96 us  [the longest x1 3.32 us: fetch(): pl.pallas_call(fetch_kernel, out_shape=pltpu.VMEM(part.shape, jnp.float32...]
    pallas_call x1, Pallas kernels: 9.2 us -> 6.32 us  [remap(): pl.pallas_call(functools.partial(remap_kernel, sizes, n_tile, chunks), ou...]
    ppermute x1, waiting for transfers between devices: 4.05 us -> 6.56 us  [local(): left = lax.ppermute(high_edge, 'tile', forward)]
    pallas_call x1, Pallas kernels: 17.5 us -> 15.4 us  [dynamics(): pl.pallas_call(functools.partial(dynamics_kernel, sizes), out_shape=[jax....]
  transfers between devices with their start and end apart: 3 -> 6, of which waited for: 2 -> 3; matrix products, arithmetic and copies ran while one was open for 0% -> 0% of each run, Pallas kernels for 36% -> 40%
where the time goes in v4:
time: 63.4 us; the launch traced here: 62.9 us
  Pallas kernels  31.8 us (50%)
  starting transfers between devices  19.8 us (31%)
  waiting for transfers between devices  8.67 us (14%)
  local copies, waits for them, and re-layouts  2.59 us (4%)
    pallas_call x1, Pallas kernels, dynamics(): pl.pallas_call(functools.partial(dynamics_kernel, sizes), out_shape=[jax....  15.4 us
    ppermute x1, starting transfers between devices, local(): right = lax.ppermute(low_edge, 'tile', backward)  7.45 us
    ppermute x1, waiting for transfers between devices, local(): left = lax.ppermute(high_edge, 'tile', forward)  6.56 us
    pallas_call x1, Pallas kernels, remap(): pl.pallas_call(functools.partial(remap_kernel, sizes, n_tile, chunks), ou...  6.32 us
    all_to_all x1, starting transfers between devices, local(): lax.all_to_all(sent, 'tile', split_axis=0, concat_axis=0, tiled=True)  4.23 us
    pallas_call x1, Pallas kernels, update(): pl.pallas_call(functools.partial(update_kernel, sizes), out_shape=jax.Sha...  3.7 us
    pallas_call x1, Pallas kernels, fetch(): pl.pallas_call(fetch_kernel, out_shape=pltpu.VMEM(part.shape, jnp.float32...  3.32 us
    ppermute x1, starting transfers between devices, local(): other_chip = lax.ppermute(onward, 'comp', [(0, 2), (2, 0), (1, 3), (3, 1)])  3.03 us
  transfers between devices with their start and end apart: 6, of which 3 were waited for; matrix products, arithmetic and copies ran while one was open for 0% of the time, Pallas kernels for 40%

profile of v4, /device:TPU:1, one launch (start us, length us, event | category | flops | bytes accessed | tf_op | source)
XLA Modules:
  0.0 62.9 jit_solution(2559774781173721502)
XLA Ops:
  0.0 0.0 copy-start
  0.0 0.7 %copy-done = s32[1,1,48,128]{3,2,1,0:T(8,128)S(1)} copy-done((s32[1,1,48,128]{3,2,1,0:T(8,128)S(1)}, s32[1,1,48,128]{3,2,1,0:T(8,128)}, u32[]{:S(2)}) %copy-start) | copy-done | bytes 24600
  0.7 0.0 copy-start.4
  0.7 0.0 copy-start.5
  0.7 0.0 copy-start.6
  0.7 2.4 %edges.1 = (f32[386,4,128]{2,1,0:T(4,128)S(1)}, f32[386,4,128]{2,1,0:T(4,128)}) custom-call(s32[1]{0:T(128)} %bitcast.1.sea_ref, f32[384,10,4,128]{3,2,1,0:T(4,128)} %bitcast.26, f32[320,12,4,128]{3,2,1,0:T(4,128)} %bitcast.27, s32[12,4,128]{2,1,0:T(4,128)S(1)} %bitcast.20), custom_call_target="tpu_custom_call" | custom-call | tf_op jit(solution)/shard_map/edges/pallas_call | solution.py:392
  3.2 2.2 %collective-permute-start = (f32[386,4,128]{2,1,0:T(4,128)}, f32[386,4,128]{2,1,0:T(4,128)S(1)}, u32[]{:S(2)}, u32[]{:S(2)}) collective-permute-start(f32[386,4,128]{2,1,0:T(4,128)} %get-tuple-element.22), channel_id=1, source_target_pairs={{0,1},{1,2},{2,3},{3,4},{4,5},{5,6},{6,7},{7,8},{8,9},{9,10},{10,1... | collective-permute-start | bytes 2371592 | tf_op jit(solution)/shard_map/ppermute | solution.py:717
  5.4 7.5 %collective-permute-start.1 = (f32[386,4,128]{2,1,0:T(4,128)S(1)}, f32[386,4,128]{2,1,0:T(4,128)}, u32[]{:S(2)}, u32[]{:S(2)}) collective-permute-start(f32[386,4,128]{2,1,0:T(4,128)S(1)} %get-tuple-element.23), channel_id=1, source_target_pairs={{1,0},{2,1},{3,2},{4,3},{5,4},{6,5},{7,6},{8,7},{9,8},{10,9},{11,1... | collective-permute-start | bytes 2371592 | tf_op jit(solution)/shard_map/ppermute | solution.py:718
  12.8 0.0 copy-done.4
  12.8 0.0 copy-done.5
  12.8 0.0 copy-done.6
  12.8 0.0 copy-start.1
  12.8 6.3 %remap.1 = (f32[32,104,128]{2,1,0:T(8,128)}, f32[32,24,128]{2,1,0:T(8,128)S(1)}) custom-call(s32[1]{0:T(128)} %bitcast.1.sea_ref, s32[1]{0:T(128)} %bitcast.10.place_ref, s32[1,256]{1,0:T(1,128)S(1)} %bitcast.23, s32[1,256]{1,0:T(1,128)S(1)} %bitcast.24, s32[1,256]{1,0:T(1,128)S(1)} %bitcast.25, f32[15360,128]{1,0:T(8,128)} %bitcast.28, ...), custom_call_target="tpu_custom_call" | custom-call | flops 8388608000 | bytes 8388608 | tf_op jit(solution)/shard_map/remap/pallas_call | solution.py:245
  19.2 0.7 %collective-permute-start.2 = (f32[32,24,128]{2,1,0:T(8,128)S(1)}, f32[32,24,128]{2,1,0:T(8,128)S(1)}, u32[]{:S(2)}, u32[]{:S(2)}) collective-permute-start(f32[32,24,128]{2,1,0:T(8,128)S(1)} %get-tuple-element.27), channel_id=1, source_target_pairs={{96,64},{97,65},{98,66},{99,67},{100,68},{101,69},{102,70},{103,71... | collective-permute-start | bytes 1179656 | tf_op jit(solution)/shard_map/ppermute | solution.py:732
  19.9 0.0 collective-permute-done.2.handed_ref
  19.9 4.2 %all-to-all-start = ((f32[32,104,128]{2,1,0:T(8,128)}), f32[32,104,128]{2,1,0:T(8,128)S(1)}, u32[]{:S(2)}, u32[]{:S(2)}) async-start(f32[32,104,128]{2,1,0:T(8,128)} %join.1), calls=%async_computation | async-start | bytes 3407872 | tf_op jit(solution)/shard_map/all_to_all | solution.py:735
  24.1 6.6 %collective-permute-done = f32[386,4,128]{2,1,0:T(4,128)S(1)} collective-permute-done((f32[386,4,128]{2,1,0:T(4,128)}, f32[386,4,128]{2,1,0:T(4,128)S(1)}, u32[]{:S(2)}, u32[]{:S(2)}) %collective-permute-start) | collective-permute-done | bytes 790560 | tf_op jit(solution)/shard_map/ppermute | solution.py:717
  30.7 0.0 collective-permute-done.1
  30.7 0.0 copy-done.1
  30.7 0.0 copy-start.2
  30.7 0.9 %copy-done.2 = f32[3,128,128]{2,1,0:T(8,128)S(1)} copy-done((f32[3,128,128]{2,1,0:T(8,128)S(1)}, f32[3,128,128]{2,1,0:T(8,128)}, u32[]{:S(2)}) %copy-start.2) | copy-done | bytes 196632
  31.6 0.0 copy-start.3
  31.6 0.9 %copy-done.3 = f32[4,80,80]{2,1,0:T(8,128)S(1)} copy-done((f32[4,80,80]{2,1,0:T(8,128)S(1)}, f32[4,80,80]{2,1,0:T(8,128)}, u32[]{:S(2)}) %copy-start.3) | copy-done | bytes 102424
  32.5 15.4 %dynamics.1 = (f32[15360,128]{1,0:T(8,128)}, f32[384,128]{1,0:T(8,128)S(1)}, f32[64,128]{1,0:T(8,128)S(1)}) custom-call(s32[1]{0:T(128)} %bitcast.1.sea_ref, f32[15360,128]{1,0:T(8,128)} %bitcast.29, f32[1544,128]{1,0:T(8,128)S(1)} %bitcast.22, f32[1544,128]{1,0:T(8,128)} %bitcast.8.right_ref, f32[3,128,128]{2,1,0:T(8,128)S(1)} %copy-done.2, ...), custom_call_target="tpu_custom_call" | custom-call | flops 25165824000 | bytes 31457280 | tf_op jit(solution)/shard_map/dynamics/pallas_call | solution.py:528
  47.9 1.1 %all-to-all-done.recv_ref = f32[32,104,128]{2,1,0:T(8,128)S(1)} async-done(((f32[32,104,128]{2,1,0:T(8,128)}), f32[32,104,128]{2,1,0:T(8,128)S(1)}, u32[]{:S(2)}, u32[]{:S(2)}) %all-to-all-start) | async-done | bytes 1703968 | tf_op jit(solution)/shard_map/all_to_all | solution.py:735
  49.0 0.6 combine.1
  49.6 2.2 %collective-permute-start.3 = (f32[2,3,56,128]{3,2,1,0:T(8,128)S(1)}, f32[2,3,56,128]{3,2,1,0:T(8,128)S(1)}, u32[]{:S(2)}, u32[]{:S(2)}) collective-permute-start(f32[2,3,56,128]{3,2,1,0:T(8,128)S(1)} %get-tuple-element.32), channel_id=1, source_target_pairs={{0,32},{32,0},{64,96},{96,64},{1,33},{33,1},{65,97},{97,65},{2,34}... | collective-permute-start | bytes 516104 | tf_op jit(solution)/shard_map/ppermute | solution.py:744
  51.8 1.0 %collective-permute-done.3.rest_2_ = f32[2,3,56,128]{3,2,1,0:T(8,128)S(1)} collective-permute-done((f32[2,3,56,128]{3,2,1,0:T(8,128)S(1)}, f32[2,3,56,128]{3,2,1,0:T(8,128)S(1)}, u32[]{:S(2)}, u32[]{:S(2)}) %collective-permute-start.3) | collective-permute-done | bytes 172064 | tf_op jit(solution)/shard_map/ppermute | solution.py:744
  52.9 3.0 %collective-permute-start.4 = (f32[3,56,128]{2,1,0:T(8,128)S(1)}, f32[3,56,128]{2,1,0:T(8,128)S(1)}, u32[]{:S(2)}, u32[]{:S(2)}) collective-permute-start(f32[3,56,128]{2,1,0:T(8,128)S(1)} %fusion.1.after_ref), channel_id=1, source_target_pairs={{0,64},{64,0},{32,96},{96,32},{1,65},{65,1},{33,97},{97,33},{2,66}... | collective-permute-start | bytes 258056 | tf_op jit(solution)/shard_map/ppermute | solution.py:746
  55.9 3.3 %fetch.1.rest_1_ = f32[15360,128]{1,0:T(8,128)S(1)} custom-call(f32[15360,128]{1,0:T(8,128)} %get-tuple-element.29.part_ref, f32[3,56,128]{2,1,0:T(8,128)S(1)} %fusion.1.after_ref), custom_call_target="tpu_custom_call" | custom-call | bytes 7864320 | tf_op jit(solution)/shard_map/fetch/pallas_call | solution.py:651
  59.2 0.0 collective-permute-done.4.rest_3_
  59.2 3.7 %update.1 = f32[15360,128]{1,0:T(8,128)} custom-call(s32[1]{0:T(128)} %bitcast.comp_ref, f32[384,128]{1,0:T(8,128)S(1)} %get-tuple-element.24.rest_0_, f32[15360,128]{1,0:T(8,128)S(1)} %fetch.1.rest_1_, f32[2,3,56,128]{3,2,1,0:T(8,128)S(1)} %collective-permute-done.3.rest_2_, f32[3,56,128]{2,1,0:T(8,128)S(1)} %collective-permute-done.4.rest_3_, ...), custom_call_target="tpu_custom_call" | custom-call | flops 3932160 | bytes 15728640 | tf_op jit(solution)/shard_map/update/pallas_call | solution.py:679
  (2 shorter events, 0.0 us)
Async XLA Ops:
  0.0 0.7 %copy-start = (s32[1,1,48,128]{3,2,1,0:T(8,128)S(1)}, s32[1,1,48,128]{3,2,1,0:T(8,128)}, u32[]{:S(2)}) copy-start(s32[1,1,48,128]{3,2,1,0:T(8,128)} %param.11) | copy-start | bytes 73732
  0.7 12.1 %copy-start.4 = (s32[1,1,256]{2,1,0:T(1,128)S(1)}, s32[1,1,256]{2,1,0:T(1,128)}, u32[]{:S(2)}) copy-start(s32[1,1,256]{2,1,0:T(1,128)} %param.12) | copy-start | bytes 3076
  0.7 12.1 %copy-start.5 = (s32[1,1,256,1]{2,3,1,0:T(1,128)S(1)}, s32[1,1,256,1]{2,3,1,0:T(1,128)}, u32[]{:S(2)}) copy-start(s32[1,1,256,1]{2,3,1,0:T(1,128)} %param.13) | copy-start | bytes 3076
  0.7 12.1 %copy-start.6 = (s32[1,1,256]{2,1,0:T(1,128)S(1)}, s32[1,1,256]{2,1,0:T(1,128)}, u32[]{:S(2)}) copy-start(s32[1,1,256]{2,1,0:T(1,128)} %param.14) | copy-start | bytes 3076
  3.2 27.5 %collective-permute-start = (f32[386,4,128]{2,1,0:T(4,128)}, f32[386,4,128]{2,1,0:T(4,128)S(1)}, u32[]{:S(2)}, u32[]{:S(2)}) collective-permute-start(f32[386,4,128]{2,1,0:T(4,128)} %get-tuple-element.22), channel_id=1, source_target_pairs={{0,1},{1,2},{2,3},{3,4},{4,5},{5,6},{6,7},{7,8},{8,9},{9,10},{10,1... | collective-permute-start | bytes 2371592 | tf_op jit(solution)/shard_map/ppermute | solution.py:717
  5.4 25.3 %collective-permute-start.1 = (f32[386,4,128]{2,1,0:T(4,128)S(1)}, f32[386,4,128]{2,1,0:T(4,128)}, u32[]{:S(2)}, u32[]{:S(2)}) collective-permute-start(f32[386,4,128]{2,1,0:T(4,128)S(1)} %get-tuple-element.23), channel_id=1, source_target_pairs={{1,0},{2,1},{3,2},{4,3},{5,4},{6,5},{7,6},{8,7},{9,8},{10,9},{11,1... | collective-permute-start | bytes 2371592 | tf_op jit(solution)/shard_map/ppermute | solution.py:718
  12.8 17.9 %copy-start.1 = (s32[1,1,48,128]{3,2,1,0:T(8,128)S(1)}, s32[1,1,48,128]{3,2,1,0:T(8,128)}, u32[]{:S(2)}) copy-start(s32[1,1,48,128]{3,2,1,0:T(8,128)} %param.11) | copy-start | bytes 73732
  19.2 0.7 %collective-permute-start.2 = (f32[32,24,128]{2,1,0:T(8,128)S(1)}, f32[32,24,128]{2,1,0:T(8,128)S(1)}, u32[]{:S(2)}, u32[]{:S(2)}) collective-permute-start(f32[32,24,128]{2,1,0:T(8,128)S(1)} %get-tuple-element.27), channel_id=1, source_target_pairs={{96,64},{97,65},{98,66},{99,67},{100,68},{101,69},{102,70},{103,71... | collective-permute-start | bytes 1179656 | tf_op jit(solution)/shard_map/ppermute | solution.py:732
  19.9 29.1 %all-to-all-start = ((f32[32,104,128]{2,1,0:T(8,128)}), f32[32,104,128]{2,1,0:T(8,128)S(1)}, u32[]{:S(2)}, u32[]{:S(2)}) async-start(f32[32,104,128]{2,1,0:T(8,128)} %join.1), calls=%async_computation | async-start | bytes 3407872 | tf_op jit(solution)/shard_map/all_to_all | solution.py:735
  30.7 0.9 %copy-start.2 = (f32[3,128,128]{2,1,0:T(8,128)S(1)}, f32[3,128,128]{2,1,0:T(8,128)}, u32[]{:S(2)}) copy-start(f32[3,128,128]{2,1,0:T(8,128)} %atm_ref.1) | copy-start | bytes 589828
  31.6 0.9 %copy-start.3 = (f32[4,80,80]{2,1,0:T(8,128)S(1)}, f32[4,80,80]{2,1,0:T(8,128)}, u32[]{:S(2)}) copy-start(f32[4,80,80]{2,1,0:T(8,128)} %ocean_ref.1) | copy-start | bytes 307204
  49.6 3.2 %collective-permute-start.3 = (f32[2,3,56,128]{3,2,1,0:T(8,128)S(1)}, f32[2,3,56,128]{3,2,1,0:T(8,128)S(1)}, u32[]{:S(2)}, u32[]{:S(2)}) collective-permute-start(f32[2,3,56,128]{3,2,1,0:T(8,128)S(1)} %get-tuple-element.32), channel_id=1, source_target_pairs={{0,32},{32,0},{64,96},{96,64},{1,33},{33,1},{65,97},{97,65},{2,34}... | collective-permute-start | bytes 516104 | tf_op jit(solution)/shard_map/ppermute | solution.py:744
  52.9 6.4 %collective-permute-start.4 = (f32[3,56,128]{2,1,0:T(8,128)S(1)}, f32[3,56,128]{2,1,0:T(8,128)S(1)}, u32[]{:S(2)}, u32[]{:S(2)}) collective-permute-start(f32[3,56,128]{2,1,0:T(8,128)S(1)} %fusion.1.after_ref), channel_id=1, source_target_pairs={{0,64},{64,0},{32,96},{96,32},{1,65},{65,1},{33,97},{97,33},{2,66}... | collective-permute-start | bytes 258056 | tf_op jit(solution)/shard_map/ppermute | solution.py:746

commit v5 on v4

--- a/solution.py
+++ b/solution.py
@@ -564,7 +564,7 @@
     return (before + after) + (down + up) - 4.0 * middle
 
 
-def filter_forcing(cols, nu, forcing_of, masked, mask_ref, work_ref, g_ref):
+def filter_forcing(f, cols, nu, forcing_of, masked, mask_ref, work_ref, g_ref):
     lo, hi, rows = 8, 8 + cols, cols + 16
     edges = lane_edges(rows)
     mask = mask_ref[0:rows, :]
@@ -572,15 +572,14 @@
     def along(v):
         return lap(pltpu.roll(v, 1, 0), v, pltpu.roll(v, rows - 1, 0), edges)
 
-    for f in range(FA):
-        work_ref[0:rows, :] = jnp.zeros((rows, R), jnp.float32)
-        work_ref[lo - HALO : hi + HALO, :] = COUPLE_RATE * forcing_of(f)
-        value = work_ref[0:rows, :] * mask
-        for _ in range(2):
-            value = value - nu * along(along(value))
-            if masked:
-                value = value * mask
-        g_ref[f, :cols] = value[lo:hi]
+    work_ref[0:rows, :] = jnp.zeros((rows, R), jnp.float32)
+    work_ref[lo - HALO : hi + HALO, :] = COUPLE_RATE * forcing_of(f)
+    value = work_ref[0:rows, :] * mask
+    for _ in range(2):
+        value = value - nu * along(along(value))
+        if masked:
+            value = value * mask
+    g_ref[f, :cols] = value[lo:hi]
 
 
 def update_part(
@@ -601,8 +600,6 @@
             return first_ref[0, f, :wide] + second_ref[f, :wide]
         own = first_ref[1, f, :wide] + mine_ref[f, :wide]
         return jnp.where(comp_ref[0] == 2, own, 0.0) + second_ref[f, :wide]
-
-    filter_forcing(cols, nu, forcing_of, masked, mask_ref, work_ref, g_ref)
 
     def piece(p, carry):
         field = p * per_piece // levels
@@ -629,7 +626,11 @@
         write(p).start()
         return carry
 
-    lax.fori_loop(0, pieces, piece, 0)
+    per_field = pieces // fields
+    for f in range(fields):
+        if f < FA:
+            filter_forcing(f, cols, nu, forcing_of, masked, mask_ref, work_ref, g_ref)
+        lax.fori_loop(f * per_field, (f + 1) * per_field, piece, 0)
     for p in range(pieces):
         write(p).wait()
 

time: 63.4 us -> 63.3 us (level)
  no operation moved by 1% of the time
where the time goes in v5:
time: 63.3 us; the launch traced here: 62.9 us
  Pallas kernels  31.7 us (50%)
  starting transfers between devices  19.8 us (31%)
  waiting for transfers between devices  8.67 us (14%)
  local copies, waits for them, and re-layouts  2.59 us (4%)
    pallas_call x1, Pallas kernels, dynamics(): pl.pallas_call(functools.partial(dynamics_kernel, sizes), out_shape=[jax....  15.4 us
    ppermute x1, starting transfers between devices, local(): right = lax.ppermute(low_edge, 'tile', backward)  7.45 us
    ppermute x1, waiting for transfers between devices, local(): left = lax.ppermute(high_edge, 'tile', forward)  6.56 us
    pallas_call x1, Pallas kernels, remap(): pl.pallas_call(functools.partial(remap_kernel, sizes, n_tile, chunks), ou...  6.32 us
    all_to_all x1, starting transfers between devices, local(): lax.all_to_all(sent, 'tile', split_axis=0, concat_axis=0, tiled=True)  4.23 us
    pallas_call x1, Pallas kernels, update(): pl.pallas_call(functools.partial(update_kernel, sizes), out_shape=jax.Sha...  3.65 us
    pallas_call x1, Pallas kernels, fetch(): pl.pallas_call(fetch_kernel, out_shape=pltpu.VMEM(part.shape, jnp.float32...  3.32 us
    ppermute x1, starting transfers between devices, local(): other_chip = lax.ppermute(onward, 'comp', [(0, 2), (2, 0), (1, 3), (3, 1)])  3.03 us
  transfers between devices with their start and end apart: 6, of which 3 were waited for; matrix products, arithmetic and copies ran while one was open for 0% of the time, Pallas kernels for 40%

profile of v5, /device:TPU:1, one launch (start us, length us, event | category | flops | bytes accessed | tf_op | source)
XLA Modules:
  0.0 62.9 jit_solution(4453964143842769391)
XLA Ops:
  0.0 0.0 copy-start
  0.0 0.7 %copy-done = s32[1,1,48,128]{3,2,1,0:T(8,128)S(1)} copy-done((s32[1,1,48,128]{3,2,1,0:T(8,128)S(1)}, s32[1,1,48,128]{3,2,1,0:T(8,128)}, u32[]{:S(2)}) %copy-start) | copy-done | bytes 24600
  0.7 0.0 copy-start.4
  0.7 0.0 copy-start.5
  0.7 0.0 copy-start.6
  0.7 2.4 %edges.1 = (f32[386,4,128]{2,1,0:T(4,128)S(1)}, f32[386,4,128]{2,1,0:T(4,128)}) custom-call(s32[1]{0:T(128)} %bitcast.1.sea_ref, f32[384,10,4,128]{3,2,1,0:T(4,128)} %bitcast.26, f32[320,12,4,128]{3,2,1,0:T(4,128)} %bitcast.27, s32[12,4,128]{2,1,0:T(4,128)S(1)} %bitcast.20), custom_call_target="tpu_custom_call" | custom-call | tf_op jit(solution)/shard_map/edges/pallas_call | solution.py:392
  3.2 2.2 %collective-permute-start = (f32[386,4,128]{2,1,0:T(4,128)}, f32[386,4,128]{2,1,0:T(4,128)S(1)}, u32[]{:S(2)}, u32[]{:S(2)}) collective-permute-start(f32[386,4,128]{2,1,0:T(4,128)} %get-tuple-element.22), channel_id=1, source_target_pairs={{0,1},{1,2},{2,3},{3,4},{4,5},{5,6},{6,7},{7,8},{8,9},{9,10},{10,1... | collective-permute-start | bytes 2371592 | tf_op jit(solution)/shard_map/ppermute | solution.py:718
  5.4 7.5 %collective-permute-start.1 = (f32[386,4,128]{2,1,0:T(4,128)S(1)}, f32[386,4,128]{2,1,0:T(4,128)}, u32[]{:S(2)}, u32[]{:S(2)}) collective-permute-start(f32[386,4,128]{2,1,0:T(4,128)S(1)} %get-tuple-element.23), channel_id=1, source_target_pairs={{1,0},{2,1},{3,2},{4,3},{5,4},{6,5},{7,6},{8,7},{9,8},{10,9},{11,1... | collective-permute-start | bytes 2371592 | tf_op jit(solution)/shard_map/ppermute | solution.py:719
  12.8 0.0 copy-done.4
  12.8 0.0 copy-done.5
  12.8 0.0 copy-done.6
  12.8 0.0 copy-start.1
  12.8 6.3 %remap.1 = (f32[32,104,128]{2,1,0:T(8,128)}, f32[32,24,128]{2,1,0:T(8,128)S(1)}) custom-call(s32[1]{0:T(128)} %bitcast.1.sea_ref, s32[1]{0:T(128)} %bitcast.10.place_ref, s32[1,256]{1,0:T(1,128)S(1)} %bitcast.23, s32[1,256]{1,0:T(1,128)S(1)} %bitcast.24, s32[1,256]{1,0:T(1,128)S(1)} %bitcast.25, f32[15360,128]{1,0:T(8,128)} %bitcast.28, ...), custom_call_target="tpu_custom_call" | custom-call | flops 8388608000 | bytes 8388608 | tf_op jit(solution)/shard_map/remap/pallas_call | solution.py:245
  19.2 0.7 %collective-permute-start.2 = (f32[32,24,128]{2,1,0:T(8,128)S(1)}, f32[32,24,128]{2,1,0:T(8,128)S(1)}, u32[]{:S(2)}, u32[]{:S(2)}) collective-permute-start(f32[32,24,128]{2,1,0:T(8,128)S(1)} %get-tuple-element.27), channel_id=1, source_target_pairs={{96,64},{97,65},{98,66},{99,67},{100,68},{101,69},{102,70},{103,71... | collective-permute-start | bytes 1179656 | tf_op jit(solution)/shard_map/ppermute | solution.py:733
  19.9 0.0 collective-permute-done.2.handed_ref
  19.9 4.2 %all-to-all-start = ((f32[32,104,128]{2,1,0:T(8,128)}), f32[32,104,128]{2,1,0:T(8,128)S(1)}, u32[]{:S(2)}, u32[]{:S(2)}) async-start(f32[32,104,128]{2,1,0:T(8,128)} %join.1), calls=%async_computation | async-start | bytes 3407872 | tf_op jit(solution)/shard_map/all_to_all | solution.py:736
  24.1 6.6 %collective-permute-done = f32[386,4,128]{2,1,0:T(4,128)S(1)} collective-permute-done((f32[386,4,128]{2,1,0:T(4,128)}, f32[386,4,128]{2,1,0:T(4,128)S(1)}, u32[]{:S(2)}, u32[]{:S(2)}) %collective-permute-start) | collective-permute-done | bytes 790560 | tf_op jit(solution)/shard_map/ppermute | solution.py:718
  30.7 0.0 collective-permute-done.1
  30.7 0.0 copy-done.1
  30.7 0.0 copy-start.2
  30.7 0.9 %copy-done.2 = f32[3,128,128]{2,1,0:T(8,128)S(1)} copy-done((f32[3,128,128]{2,1,0:T(8,128)S(1)}, f32[3,128,128]{2,1,0:T(8,128)}, u32[]{:S(2)}) %copy-start.2) | copy-done | bytes 196632
  31.6 0.0 copy-start.3
  31.6 0.9 %copy-done.3 = f32[4,80,80]{2,1,0:T(8,128)S(1)} copy-done((f32[4,80,80]{2,1,0:T(8,128)S(1)}, f32[4,80,80]{2,1,0:T(8,128)}, u32[]{:S(2)}) %copy-start.3) | copy-done | bytes 102424
  32.5 15.4 %dynamics.1 = (f32[15360,128]{1,0:T(8,128)}, f32[384,128]{1,0:T(8,128)S(1)}, f32[64,128]{1,0:T(8,128)S(1)}) custom-call(s32[1]{0:T(128)} %bitcast.1.sea_ref, f32[15360,128]{1,0:T(8,128)} %bitcast.29, f32[1544,128]{1,0:T(8,128)S(1)} %bitcast.22, f32[1544,128]{1,0:T(8,128)} %bitcast.8.right_ref, f32[3,128,128]{2,1,0:T(8,128)S(1)} %copy-done.2, ...), custom_call_target="tpu_custom_call" | custom-call | flops 25165824000 | bytes 31457280 | tf_op jit(solution)/shard_map/dynamics/pallas_call | solution.py:528
  47.9 1.1 %all-to-all-done.recv_ref = f32[32,104,128]{2,1,0:T(8,128)S(1)} async-done(((f32[32,104,128]{2,1,0:T(8,128)}), f32[32,104,128]{2,1,0:T(8,128)S(1)}, u32[]{:S(2)}, u32[]{:S(2)}) %all-to-all-start) | async-done | bytes 1703968 | tf_op jit(solution)/shard_map/all_to_all | solution.py:736
  49.0 0.6 combine.1
  49.6 2.2 %collective-permute-start.3 = (f32[2,3,56,128]{3,2,1,0:T(8,128)S(1)}, f32[2,3,56,128]{3,2,1,0:T(8,128)S(1)}, u32[]{:S(2)}, u32[]{:S(2)}) collective-permute-start(f32[2,3,56,128]{3,2,1,0:T(8,128)S(1)} %get-tuple-element.32), channel_id=1, source_target_pairs={{0,32},{32,0},{64,96},{96,64},{1,33},{33,1},{65,97},{97,65},{2,34}... | collective-permute-start | bytes 516104 | tf_op jit(solution)/shard_map/ppermute | solution.py:745
  51.8 1.0 %collective-permute-done.3.rest_2_ = f32[2,3,56,128]{3,2,1,0:T(8,128)S(1)} collective-permute-done((f32[2,3,56,128]{3,2,1,0:T(8,128)S(1)}, f32[2,3,56,128]{3,2,1,0:T(8,128)S(1)}, u32[]{:S(2)}, u32[]{:S(2)}) %collective-permute-start.3) | collective-permute-done | bytes 172064 | tf_op jit(solution)/shard_map/ppermute | solution.py:745
  52.9 3.0 %collective-permute-start.4 = (f32[3,56,128]{2,1,0:T(8,128)S(1)}, f32[3,56,128]{2,1,0:T(8,128)S(1)}, u32[]{:S(2)}, u32[]{:S(2)}) collective-permute-start(f32[3,56,128]{2,1,0:T(8,128)S(1)} %fusion.1.after_ref), channel_id=1, source_target_pairs={{0,64},{64,0},{32,96},{96,32},{1,65},{65,1},{33,97},{97,33},{2,66}... | collective-permute-start | bytes 258056 | tf_op jit(solution)/shard_map/ppermute | solution.py:747
  55.9 3.3 %fetch.1.rest_1_ = f32[15360,128]{1,0:T(8,128)S(1)} custom-call(f32[15360,128]{1,0:T(8,128)} %get-tuple-element.29.part_ref, f32[3,56,128]{2,1,0:T(8,128)S(1)} %fusion.1.after_ref), custom_call_target="tpu_custom_call" | custom-call | bytes 7864320 | tf_op jit(solution)/shard_map/fetch/pallas_call | solution.py:652
  59.2 0.0 collective-permute-done.4.rest_3_
  59.2 3.6 %update.1 = f32[15360,128]{1,0:T(8,128)} custom-call(s32[1]{0:T(128)} %bitcast.comp_ref, f32[384,128]{1,0:T(8,128)S(1)} %get-tuple-element.24.rest_0_, f32[15360,128]{1,0:T(8,128)S(1)} %fetch.1.rest_1_, f32[2,3,56,128]{3,2,1,0:T(8,128)S(1)} %collective-permute-done.3.rest_2_, f32[3,56,128]{2,1,0:T(8,128)S(1)} %collective-permute-done.4.rest_3_, ...), custom_call_target="tpu_custom_call" | custom-call | flops 3932160 | bytes 15728640 | tf_op jit(solution)/shard_map/update/pallas_call | solution.py:680
  (2 shorter events, 0.0 us)
Async XLA Ops:
  0.0 0.7 %copy-start = (s32[1,1,48,128]{3,2,1,0:T(8,128)S(1)}, s32[1,1,48,128]{3,2,1,0:T(8,128)}, u32[]{:S(2)}) copy-start(s32[1,1,48,128]{3,2,1,0:T(8,128)} %param.11) | copy-start | bytes 73732
  0.7 12.1 %copy-start.4 = (s32[1,1,256]{2,1,0:T(1,128)S(1)}, s32[1,1,256]{2,1,0:T(1,128)}, u32[]{:S(2)}) copy-start(s32[1,1,256]{2,1,0:T(1,128)} %param.12) | copy-start | bytes 3076
  0.7 12.1 %copy-start.5 = (s32[1,1,256,1]{2,3,1,0:T(1,128)S(1)}, s32[1,1,256,1]{2,3,1,0:T(1,128)}, u32[]{:S(2)}) copy-start(s32[1,1,256,1]{2,3,1,0:T(1,128)} %param.13) | copy-start | bytes 3076
  0.7 12.1 %copy-start.6 = (s32[1,1,256]{2,1,0:T(1,128)S(1)}, s32[1,1,256]{2,1,0:T(1,128)}, u32[]{:S(2)}) copy-start(s32[1,1,256]{2,1,0:T(1,128)} %param.14) | copy-start | bytes 3076
  3.2 27.5 %collective-permute-start = (f32[386,4,128]{2,1,0:T(4,128)}, f32[386,4,128]{2,1,0:T(4,128)S(1)}, u32[]{:S(2)}, u32[]{:S(2)}) collective-permute-start(f32[386,4,128]{2,1,0:T(4,128)} %get-tuple-element.22), channel_id=1, source_target_pairs={{0,1},{1,2},{2,3},{3,4},{4,5},{5,6},{6,7},{7,8},{8,9},{9,10},{10,1... | collective-permute-start | bytes 2371592 | tf_op jit(solution)/shard_map/ppermute | solution.py:718
  5.4 25.3 %collective-permute-start.1 = (f32[386,4,128]{2,1,0:T(4,128)S(1)}, f32[386,4,128]{2,1,0:T(4,128)}, u32[]{:S(2)}, u32[]{:S(2)}) collective-permute-start(f32[386,4,128]{2,1,0:T(4,128)S(1)} %get-tuple-element.23), channel_id=1, source_target_pairs={{1,0},{2,1},{3,2},{4,3},{5,4},{6,5},{7,6},{8,7},{9,8},{10,9},{11,1... | collective-permute-start | bytes 2371592 | tf_op jit(solution)/shard_map/ppermute | solution.py:719
  12.8 17.9 %copy-start.1 = (s32[1,1,48,128]{3,2,1,0:T(8,128)S(1)}, s32[1,1,48,128]{3,2,1,0:T(8,128)}, u32[]{:S(2)}) copy-start(s32[1,1,48,128]{3,2,1,0:T(8,128)} %param.11) | copy-start | bytes 73732
  19.2 0.7 %collective-permute-start.2 = (f32[32,24,128]{2,1,0:T(8,128)S(1)}, f32[32,24,128]{2,1,0:T(8,128)S(1)}, u32[]{:S(2)}, u32[]{:S(2)}) collective-permute-start(f32[32,24,128]{2,1,0:T(8,128)S(1)} %get-tuple-element.27), channel_id=1, source_target_pairs={{96,64},{97,65},{98,66},{99,67},{100,68},{101,69},{102,70},{103,71... | collective-permute-start | bytes 1179656 | tf_op jit(solution)/shard_map/ppermute | solution.py:733
  19.9 29.1 %all-to-all-start = ((f32[32,104,128]{2,1,0:T(8,128)}), f32[32,104,128]{2,1,0:T(8,128)S(1)}, u32[]{:S(2)}, u32[]{:S(2)}) async-start(f32[32,104,128]{2,1,0:T(8,128)} %join.1), calls=%async_computation | async-start | bytes 3407872 | tf_op jit(solution)/shard_map/all_to_all | solution.py:736
  30.7 0.9 %copy-start.2 = (f32[3,128,128]{2,1,0:T(8,128)S(1)}, f32[3,128,128]{2,1,0:T(8,128)}, u32[]{:S(2)}) copy-start(f32[3,128,128]{2,1,0:T(8,128)} %atm_ref.1) | copy-start | bytes 589828
  31.6 0.9 %copy-start.3 = (f32[4,80,80]{2,1,0:T(8,128)S(1)}, f32[4,80,80]{2,1,0:T(8,128)}, u32[]{:S(2)}) copy-start(f32[4,80,80]{2,1,0:T(8,128)} %ocean_ref.1) | copy-start | bytes 307204
  49.6 3.2 %collective-permute-start.3 = (f32[2,3,56,128]{3,2,1,0:T(8,128)S(1)}, f32[2,3,56,128]{3,2,1,0:T(8,128)S(1)}, u32[]{:S(2)}, u32[]{:S(2)}) collective-permute-start(f32[2,3,56,128]{3,2,1,0:T(8,128)S(1)} %get-tuple-element.32), channel_id=1, source_target_pairs={{0,32},{32,0},{64,96},{96,64},{1,33},{33,1},{65,97},{97,65},{2,34}... | collective-permute-start | bytes 516104 | tf_op jit(solution)/shard_map/ppermute | solution.py:745
  52.9 6.4 %collective-permute-start.4 = (f32[3,56,128]{2,1,0:T(8,128)S(1)}, f32[3,56,128]{2,1,0:T(8,128)S(1)}, u32[]{:S(2)}, u32[]{:S(2)}) collective-permute-start(f32[3,56,128]{2,1,0:T(8,128)S(1)} %fusion.1.after_ref), channel_id=1, source_target_pairs={{0,64},{64,0},{32,96},{96,32},{1,65},{65,1},{33,97},{97,33},{2,66}... | collective-permute-start | bytes 258056 | tf_op jit(solution)/shard_map/ppermute | solution.py:747
